TPU v7x, 256 devices: a whole 4x4x8 slice. The times are simulated.
256 devices in a mesh: dp: 64 (over y, x_lo, z), group: 4 (over x_hi, core).
Axes of the slice: x: 4 (x_hi: 2, x_lo: 2; x = x_hi * 2 + x_lo), y: 4, z: 8, core: 2. Of those that a mesh axis runs over, the one named last changes fastest.
Arguments:
- activations: bfloat16 [2, 24576, 5120], P(None, 'dp')
- tile_owner: int32 [55], replicated, may hold values from 0 to 63, as said below
- gradient: bfloat16 [10, 512, 4096], P(None, 'dp', 'group'), may hold values from -6 to 6
- block_owner: int32 [10], replicated, may hold values from 0 to 63, as said below
- eigen_basis: bfloat16 [128, 512, 512], P('dp'), may hold values from -0.25 to 0.25
- eigen_values: float32 [128, 512], P('dp'), may hold values from 0.05 to 5
Outputs:
- factor_tiles: float32 [128, 512, 512], P('dp', None, 'group')
- preconditioned: bfloat16 [10, 512, 4096], P(None, 'dp', 'group')
Inputs may be any that keep to these rules, and one draw needn't show every extreme that they name: `tile_owner`: no owner holds more than 2 tiles, and some owner holds exactly 2. `block_owner`: no owner holds more than 2 blocks, and some owner holds exactly 2.
All inputs are finite; a program needn't handle non-finite values.
Results may differ from a plain program's by a relative error of at most 0.0043.
Values may be sent and summed in bfloat16 or wider, within the bound.
No kernel may reach another device: no remote copies, remote signals or barrier semaphores. Data moves between devices by JAX's collectives and lax.ppermute only.
A program may use at most 128 MiB of HBM per device.

v0:
```python
import jax
import jax.numpy as jnp
import numpy as np
from jax import lax
from jax.sharding import PartitionSpec as P

TILE = 512
NT = 10


damping = 0.1


def slot_rank(owner_ids):
    entries = owner_ids.shape[0]
    position = jnp.arange(entries)
    same_owner = owner_ids[:, None] == owner_ids[None, :]
    earlier = position[None, :] < position[:, None]
    return jnp.sum(jnp.logical_and(same_owner, earlier), axis=1)


def precondition_blocks(gradient, block_owner, eigen_basis, eigen_values):
    dp_count = lax.axis_size("dp")
    slot_count = eigen_basis.shape[0]
    block_count, row_count, col_total = gradient.shape
    destination = slot_rank(block_owner) * dp_count + block_owner
    selector = (destination[None, :] == jnp.arange(slot_count * dp_count)[:, None]).astype(
        jnp.bfloat16
    )
    packed = jnp.einsum("pn,nrq->prq", selector, gradient, preferred_element_type=jnp.float32)
    packed = packed.astype(jnp.bfloat16).reshape(slot_count, dp_count, row_count, col_total)
    received = lax.all_to_all(packed, "dp", split_axis=1, concat_axis=1, tiled=True)
    col_count = received.shape[3]
    blocks = received.reshape(slot_count, dp_count * row_count, col_count)
    turned = jnp.einsum("gkr,gkc->grc", eigen_basis, blocks, preferred_element_type=jnp.float32)
    scaled = (turned / (eigen_values[:, :, None] + damping)).astype(jnp.bfloat16)
    rotated = jnp.einsum("gkr,grc->gkc", eigen_basis, scaled, preferred_element_type=jnp.float32)
    rotated = rotated.astype(jnp.bfloat16).reshape(slot_count, dp_count, row_count, col_count)
    returned = lax.all_to_all(rotated, "dp", split_axis=1, concat_axis=1, tiled=True)
    flattened = returned.reshape(slot_count * dp_count, row_count, col_total)
    result = jnp.einsum("pn,prq->nrq", selector, flattened, preferred_element_type=jnp.float32)
    return result.astype(jnp.bfloat16)


def shards(activations, tile_owner, gradient, block_owner, eigen_basis, eigen_values):
    dp_count = lax.axis_size("dp")
    group_count = lax.axis_size("group")
    micro_count = activations.shape[0]
    token_count = activations.shape[1]
    slab_width = TILE // group_count
    row_share = TILE // dp_count
    tile_count = NT * (NT + 1) // 2
    slot_count = max(2, (tile_count + dp_count - 1) // dp_count + 1)
    tiled = activations.reshape(micro_count, token_count, NT, TILE)
    slab = lax.dynamic_slice_in_dim(tiled, lax.axis_index("group") * slab_width, slab_width, 3)
    first_index, second_index = np.triu_indices(NT)
    pair_flat = first_index * NT + second_index
    product = jnp.einsum("mtir,mtjc->rijc", tiled, slab, preferred_element_type=jnp.float32)
    summed = lax.psum_scatter(
        product.reshape(lax.axis_size("dp") * row_share, NT * NT, slab_width),
        "dp",
        scatter_dimension=0,
        tiled=True,
    )
    shares = summed[:, pair_flat]
    shares = shares / (micro_count * token_count * dp_count)
    destination = slot_rank(tile_owner) * dp_count + tile_owner
    selector = (destination[None, :] == jnp.arange(slot_count * dp_count)[:, None]).astype(
        jnp.float32
    )
    packed = jnp.einsum("pu,rus->prs", selector, shares, precision=lax.Precision.HIGHEST)
    packed = packed.reshape(slot_count, dp_count, row_share, slab_width)
    arrived = lax.all_to_all(packed, "dp", split_axis=1, concat_axis=1, tiled=True)
    factor = arrived.reshape(slot_count, TILE, slab_width)
    result = precondition_blocks(gradient, block_owner, eigen_basis, eigen_values)
    return (factor, result)


def solution(mesh):
    placed = (
        P(None, "dp", None),
        P(),
        P(None, "dp", "group"),
        P(),
        P("dp", None, None),
        P("dp", None),
    )
    return jax.shard_map(
        shards,
        mesh=mesh,
        in_specs=placed,
        out_specs=(P("dp", None, "group"), P(None, "dp", "group")),
        check_vma=False,
    )
```

profile of v0, /device:TPU:32, one launch (start us, length us, event | category | flops | bytes accessed | tf_op | source)
XLA Modules:
  0.0 552.7 jit_solution(14472998925394739712)
XLA Ops:
  7.2 0.0 copy-start
  7.2 0.0 reduce-scatter.2.cloned.1.call-start
  7.2 10.7 %copy.39 = bf16[2,384,5120]{1,2,0:T(8,128)(2,1)} copy(bf16[2,384,5120]{2,1,0:T(8,128)(2,1)} %param.8) | data formatting | bytes 15728640 | tf_op args[0]
  18.0 18.1 %convolution_bitcast_fusion = f32[512,10,10,128]{0,3,1,2:T(8,128)} fusion(bf16[2,384,10,512,1]{1,3,2,0,4:T(8,128)(2,1)} %bitcast.49, bf16[2,384,10,512]{1,3,2,0:T(8,128)(2,1)} %bitcast.50, s32[]{:T(128)S(6)} %select_n.6), kind=kOutput, calls=%fused_computation.1 | convolution fusion | flops 10066329600 | bytes 36044804 | tf_op jit(solution)/shard_map/mtir,mtjc->rijc/dot_general | solution.py:58
  36.1 27.4 %copy.42 = f32[512,10,10,128]{3,0,2,1:T(8,128)} copy(f32[512,10,10,128]{0,3,1,2:T(8,128)} %convolution_bitcast_fusion) | data formatting | bytes 52428800 | tf_op jit(solution)/shard_map/mtir,mtjc->rijc/transpose | solution.py:58
  63.4 0.0 copy-start.4
  63.4 0.0 copy-start.1
  63.4 0.0 reduce-scatter.2.cloned.1.call-update
  63.5 0.6 copy-done.4
  64.1 0.2 convert_reduce_fusion.1
  64.3 0.1 copy-done.1
  64.4 0.8 convolution_convert_fusion
  65.2 2.5 copy.46
  67.7 0.0 copy-start.2
  67.7 12.8 %all-to-all-start.1 = ((bf16[2,64,8,1024]{3,2,0,1:T(8,128)(2,1)}), bf16[2,64,8,1024]{3,2,0,1:T(8,128)(2,1)S(1)}, u32[]{:S(2)}, u32[]{:S(2)}) async-start(bf16[2,64,8,1024]{3,2,0,1:T(8,128)(2,1)} %copy.46), calls=%async_computation.2 | async-start | bytes 4194304 | tf_op jit(solution)/shard_map/all_to_all | solution.py:32
  80.5 0.0 copy-done.2
  80.5 73.8 %all-to-all-done.1 = bf16[2,64,8,1024]{3,2,0,1:T(8,128)(2,1)S(1)} async-done(((bf16[2,64,8,1024]{3,2,0,1:T(8,128)(2,1)}), bf16[2,64,8,1024]{3,2,0,1:T(8,128)(2,1)S(1)}, u32[]{:S(2)}, u32[]{:S(2)}) %all-to-all-start.1) | async-done | bytes 2097184 | tf_op jit(solution)/shard_map/all_to_all | solution.py:32
  154.4 0.0 copy-done
  154.4 3.8 convert_bitcast_fusion
  158.2 3.2 copy.49
  161.4 0.0 copy-start.3
  161.4 0.0 copy-start.5
  161.4 7.0 %all-to-all-start.2 = ((bf16[2,64,8,1024]{3,2,0,1:T(8,128)(2,1)}), bf16[2,64,8,1024]{3,2,0,1:T(8,128)(2,1)S(1)}, u32[]{:S(2)}, u32[]{:S(2)}) async-start(bf16[2,64,8,1024]{3,2,0,1:T(8,128)(2,1)} %copy.49), calls=%async_computation.3 | async-start | bytes 4194304 | tf_op jit(solution)/shard_map/all_to_all | solution.py:39
  168.4 0.0 copy-done.3
  168.4 0.0 copy-done.5
  168.4 0.2 convert_reduce_fusion
  168.6 349.7 %reduce-scatter.2.cloned.1.call-done = f32[8,100,128]{2,0,1:T(8,128)} async-done(((f32[512,100,128]{2,0,1:T(8,128)}), f32[8,100,128]{2,0,1:T(8,128)}) %reduce-scatter.2.cloned.1.call-update) | async-done | bytes 409616 | tf_op jit(solution)/shard_map/reduce_scatter | solution.py:59
  518.3 1.6 gather_fusion
  520.0 0.5 fusion.11
  520.4 1.2 copy.44
  521.6 0.0 all-to-all-done.2
  521.7 8.3 %all-to-all-start = ((f32[2,64,8,128]{3,0,2,1:T(2,128)}), f32[2,64,8,128]{3,0,2,1:T(2,128)}, u32[]{:S(2)}, u32[]{:S(2)}) async-start(f32[2,64,8,128]{3,0,2,1:T(2,128)} %copy.44), calls=%async_computation.1 | async-start | bytes 1048576 | tf_op jit(solution)/shard_map/all_to_all | solution.py:73
  529.9 1.2 copy.50
  531.1 0.4 convolution_convert_fusion.1
  531.5 0.8 copy.52
  532.3 11.7 %all-to-all-done = f32[2,64,8,128]{3,0,2,1:T(2,128)} async-done(((f32[2,64,8,128]{3,0,2,1:T(2,128)}), f32[2,64,8,128]{3,0,2,1:T(2,128)}, u32[]{:S(2)}, u32[]{:S(2)}) %all-to-all-start) | async-done | bytes 524320 | tf_op jit(solution)/shard_map/all_to_all | solution.py:73
  544.0 1.9 copy.51
  (5 shorter events, 0.0 us)
Async XLA Ops:
  7.2 147.2 %copy-start = (bf16[2,512,512]{2,1,0:T(8,128)(2,1)S(1)}, bf16[2,512,512]{2,1,0:T(8,128)(2,1)}, u32[]{:S(2)}) copy-start(bf16[2,512,512]{2,1,0:T(8,128)(2,1)} %param.12) | copy-start | bytes 3145732
  7.2 511.2 %reduce-scatter.2.cloned.1.call-start = ((), (), s32[]{:S(2)}) async-start(), calls=%async_computation.4 | async-start | bytes 26624000 | tf_op jit(solution)/shard_map/reduce_scatter | solution.py:59
  63.4 0.7 copy-start.4
  63.4 0.9 copy-start.1
  67.7 12.8 %copy-start.2 = (f32[2,512]{1,0:T(2,128)S(1)}, f32[2,512]{1,0:T(2,128)}, u32[]{:S(2)}) copy-start(f32[2,512]{1,0:T(2,128)} %param.13) | copy-start | bytes 12292
  67.7 86.7 %all-to-all-start.1 = ((bf16[2,64,8,1024]{3,2,0,1:T(8,128)(2,1)}), bf16[2,64,8,1024]{3,2,0,1:T(8,128)(2,1)S(1)}, u32[]{:S(2)}, u32[]{:S(2)}) async-start(bf16[2,64,8,1024]{3,2,0,1:T(8,128)(2,1)} %copy.46), calls=%async_computation.2 | async-start | bytes 4194304 | tf_op jit(solution)/shard_map/all_to_all | solution.py:32
  161.4 7.0 %copy-start.3 = (s32[55]{0:T(128)S(1)}, s32[55]{0:T(128)}, u32[]{:S(2)}) copy-start(s32[55]{0:T(128)} %constant.30) | copy-start | bytes 664
  161.4 7.1 %copy-start.5 = (s32[55]{0:T(128)S(1)}, s32[55]{0:T(128)}, u32[]{:S(2)}) copy-start(s32[55]{0:T(128)} %param.9) | copy-start | bytes 664
  161.4 360.3 %all-to-all-start.2 = ((bf16[2,64,8,1024]{3,2,0,1:T(8,128)(2,1)}), bf16[2,64,8,1024]{3,2,0,1:T(8,128)(2,1)S(1)}, u32[]{:S(2)}, u32[]{:S(2)}) async-start(bf16[2,64,8,1024]{3,2,0,1:T(8,128)(2,1)} %copy.49), calls=%async_computation.3 | async-start | bytes 4194304 | tf_op jit(solution)/shard_map/all_to_all | solution.py:39
  521.7 22.3 %all-to-all-start = ((f32[2,64,8,128]{3,0,2,1:T(2,128)}), f32[2,64,8,128]{3,0,2,1:T(2,128)}, u32[]{:S(2)}, u32[]{:S(2)}) async-start(f32[2,64,8,128]{3,0,2,1:T(2,128)} %copy.44), calls=%async_computation.1 | async-start | bytes 1048576 | tf_op jit(solution)/shard_map/all_to_all | solution.py:73
Sparse Core Ops, SparseCore 0:
  63.6 454.6 reduce-scatter.1
where the time goes:
time: 555 us; the launch traced here: 553 us
  waiting for transfers between devices  435 us (78%)
  local copies, waits for them, and re-layouts  51.1 us (9%)
  starting transfers between devices  28.1 us (5%)
  matrix products  23.7 us (4%)
  between operations  14.1 us (3%)
    reduce_scatter x1, waiting for transfers between devices, shards(): lax.psum_scatter(product.reshape(lax.axis_size('dp') * row_share, NT * NT...  350 us
    all_to_all x1, waiting for transfers between devices, precondition_blocks(): lax.all_to_all(packed, 'dp', split_axis=1, concat_axis=1, tiled=True)  73.8 us
    transpose x1, local copies, waits for them, and re-layouts, shards(): jnp.einsum('mtir,mtjc->rijc', tiled, slab, preferred_element_type=jnp.flo...  27.4 us
    dot_general x1, matrix products, shards(): jnp.einsum('mtir,mtjc->rijc', tiled, slab, preferred_element_type=jnp.flo...  18.1 us
    unnamed x15, local copies, waits for them, and re-layouts  14.1 us
    all_to_all x1, starting transfers between devices, precondition_blocks(): lax.all_to_all(packed, 'dp', split_axis=1, concat_axis=1, tiled=True)  12.8 us
    all_to_all x1, waiting for transfers between devices, shards(): lax.all_to_all(packed, 'dp', split_axis=1, concat_axis=1, tiled=True)  11.7 us
  transfers between devices with their start and end apart: 4, of which 3 were waited for; matrix products, arithmetic and copies ran while one was open for 3% of the time, Pallas kernels for 0%

commit v1 on v0

v1 whole, which is shorter than its diff:
```python
import functools

import jax
import jax.numpy as jnp
import numpy as np
from jax import lax
from jax.experimental import pallas as pl
from jax.experimental.pallas import tpu as pltpu
from jax.sharding import Mesh, PartitionSpec as P

TILE = 512
NT = 10
UT = NT * (NT + 1) // 2
SLOTS = 2
SLAB = 128
FIRST_ROWS = 3
FIRST_TILES = sum(NT - i for i in range(FIRST_ROWS))
LAST_TILES = UT - FIRST_TILES
DP = ("y", "xl", "z")

damping = 0.1
bf16 = jnp.bfloat16
f32 = jnp.float32


def slot_rank(owner_ids):
    entries = owner_ids.shape[0]
    position = jnp.arange(entries)
    same_owner = owner_ids[:, None] == owner_ids[None, :]
    earlier = position[None, :] < position[:, None]
    return jnp.sum(jnp.logical_and(same_owner, earlier), axis=1)


def dot(a, b):
    return lax.dot_general(a, b, (((1,), (0,)), ((), ())), preferred_element_type=f32)


def first_kernel(place, act, own, near, far, slab, other, turned):
    low, mine, theirs = place[0], place[1], place[2]
    for j in range(NT):
        at = j * TILE
        slab[:, j * SLAB : (j + 1) * SLAB] = act[:, pl.ds(pl.multiple_of(at + mine * SLAB, SLAB), SLAB)]
        other[:, j * SLAB : (j + 1) * SLAB] = act[:, pl.ds(pl.multiple_of(at + theirs * SLAB, SLAB), SLAB)]
    start = 0
    for i in range(FIRST_ROWS):
        for q in range(4):
            row = pl.multiple_of(lax.rem(q + 2 * low, 4) * SLAB, SLAB)
            turned[pl.ds(row, SLAB), :] = act[:, i * TILE + q * SLAB : i * TILE + (q + 1) * SLAB].T
        for begin in range(i * SLAB, NT * SLAB, 256):
            end = min(begin + 256, NT * SLAB)
            to = slice(start, start + end - begin)
            kept = dot(turned[0:384, :], slab[:, begin:end])
            own[:, to] = kept[0:256]
            near[:, to] = kept[256:384].astype(bf16)
            far[:, to] = dot(turned[384:512, :], other[:, begin:end]).astype(bf16)
            start += end - begin


def last_kernel(place, act, out, slab, turned):
    mine = place[1]
    for j in range(FIRST_ROWS, NT):
        slab[:, j * SLAB : (j + 1) * SLAB] = act[:, pl.ds(pl.multiple_of(j * TILE + mine * SLAB, SLAB), SLAB)]
    start = 0
    for i in range(FIRST_ROWS, NT):
        turned[...] = act[:, i * TILE : (i + 1) * TILE].T
        for begin in range(i * SLAB, NT * SLAB, 256):
            end = min(begin + 256, NT * SLAB)
            out[:, start : start + end - begin] = dot(turned[...], slab[:, begin:end])
            start += end - begin


def first_products(act, place):
    tokens = act.shape[0]
    wide = FIRST_TILES * SLAB
    vmem = pl.BlockSpec(memory_space=pltpu.VMEM)
    return pl.pallas_call(
        first_kernel,
        out_shape=(
            jax.ShapeDtypeStruct((256, wide), f32),
            jax.ShapeDtypeStruct((128, wide), bf16),
            jax.ShapeDtypeStruct((128, wide), bf16),
        ),
        in_specs=[pl.BlockSpec(memory_space=pltpu.SMEM), vmem],
        out_specs=(vmem, vmem, vmem),
        scratch_shapes=[
            pltpu.VMEM((tokens, NT * SLAB), bf16),
            pltpu.VMEM((tokens, NT * SLAB), bf16),
            pltpu.VMEM((TILE, tokens), bf16),
        ],
        compiler_params=pltpu.CompilerParams(vmem_limit_bytes=40 * 2**20),
        cost_estimate=pl.CostEstimate(
            flops=2 * tokens * TILE * wide, bytes_accessed=act.size * 2 + 768 * wide * 2, transcendentals=0
        ),
    )(place, act)


def last_products(act, place):
    tokens = act.shape[0]
    wide = LAST_TILES * SLAB
    vmem = pl.BlockSpec(memory_space=pltpu.VMEM)
    return pl.pallas_call(
        last_kernel,
        out_shape=jax.ShapeDtypeStruct((TILE, wide), f32),
        in_specs=[pl.BlockSpec(memory_space=pltpu.SMEM), vmem],
        out_specs=vmem,
        scratch_shapes=[
            pltpu.VMEM((tokens, NT * SLAB), bf16),
            pltpu.VMEM((TILE, tokens), bf16),
        ],
        compiler_params=pltpu.CompilerParams(vmem_limit_bytes=40 * 2**20),
        cost_estimate=pl.CostEstimate(
            flops=2 * tokens * TILE * wide, bytes_accessed=act.size * 2 + TILE * wide * 4, transcendentals=0
        ),
    )(place, act)


def around_z(product):
    n = lax.axis_size("z")
    z = lax.axis_index("z")
    rows = product.shape[0] // n
    half = rows // 2
    up = [(i, (i + 1) % n) for i in range(n)]
    down = [(i, (i - 1) % n) for i in range(n)]

    def chunk(k):
        return lax.dynamic_slice_in_dim(product, lax.rem(z + (k + n), n) * rows, rows, 0)

    ahead = lax.ppermute(chunk(n // 2)[:half].astype(bf16), "z", up)
    back = lax.ppermute(chunk(n // 2)[half:].astype(bf16), "z", down)
    ahead = jnp.concatenate([ahead, jnp.zeros_like(ahead)], axis=0)
    back = jnp.concatenate([jnp.zeros_like(back), back], axis=0)
    for k in range(n // 2 - 1, 0, -1):
        ahead = lax.ppermute((chunk(k) + ahead.astype(f32)).astype(bf16), "z", up)
        back = lax.ppermute((chunk(-k) + back.astype(f32)).astype(bf16), "z", down)
    return chunk(0) + ahead.astype(f32) + back.astype(f32)


def scatter_sum(x, axis):
    n = lax.axis_size(axis)
    got = lax.all_to_all(x.astype(bf16), axis, split_axis=0, concat_axis=0, tiled=True)
    return jnp.sum(got.reshape(n, x.shape[0] // n, x.shape[1]).astype(f32), axis=0)


def factor_shares(activations):
    micro, tokens, width = activations.shape
    act = activations.reshape(micro * tokens, width)
    low = lax.axis_index("xl")
    high, core = lax.axis_index("xh"), lax.axis_index("c")
    place = jnp.stack([low, high * 2 + core, (1 - high) * 2 + core]).astype(jnp.int32)
    own, near, far = first_products(act, place)
    near = lax.ppermute(near, "xl", [(0, 1), (1, 0)])
    far = lax.ppermute(far, ("xl", "xh"), [(i, 3 - i) for i in range(4)])
    last = last_products(act, place)

    last = around_z(last)
    half = last.shape[0] // 2
    sent = lax.dynamic_slice_in_dim(last, (1 - low) * half, half, 0)
    kept = lax.dynamic_slice_in_dim(last, low * half, half, 0)
    last = kept + lax.ppermute(sent.astype(bf16), "xl", [(0, 1), (1, 0)]).astype(f32)
    last = scatter_sum(last, "y")

    first = own + jnp.concatenate([near, far], axis=0).astype(f32)
    first = scatter_sum(first, "y")
    first = scatter_sum(first, "z")
    return jnp.concatenate([first, last], axis=1)


def factor_part(activations, tile_owner):
    dp_count = lax.axis_size(DP)
    total = activations.shape[0] * activations.shape[1] * dp_count
    rows = TILE // dp_count
    rank = slot_rank(tile_owner)
    shares = factor_shares(activations) / total
    destination = rank * dp_count + tile_owner
    selector = (destination[None, :] == jnp.arange(SLOTS * dp_count)[:, None]).astype(bf16)
    packed = jnp.einsum(
        "pu,rus->prs", selector, shares.astype(bf16).reshape(rows, UT, SLAB), preferred_element_type=f32
    ).astype(bf16)
    packed = packed.reshape(SLOTS, dp_count, rows, SLAB)
    arrived = lax.all_to_all(packed, DP, split_axis=1, concat_axis=1, tiled=True)
    ny, nx, nz = (lax.axis_size(a) for a in DP)
    arrived = arrived.reshape(SLOTS, ny, nx, nz, rows, SLAB)
    me = lax.axis_index(DP)
    slot = jnp.arange(SLOTS)
    held = (tile_owner[None, :] == me) & (rank[None, :] == slot[:, None])
    is_first = jnp.any(held & (jnp.arange(UT) < FIRST_TILES)[None, :], axis=1)
    as_first = arrived.transpose(0, 2, 1, 3, 4, 5).reshape(SLOTS, TILE, SLAB)
    as_last = arrived.transpose(0, 3, 2, 1, 4, 5).reshape(SLOTS, TILE, SLAB)
    return jnp.where(is_first[:, None, None], as_first, as_last).astype(f32)


def precondition_blocks(gradient, block_owner, eigen_basis, eigen_values):
    dp_count = lax.axis_size(DP)
    slot_count = eigen_basis.shape[0]
    block_count, row_count, col_total = gradient.shape
    destination = slot_rank(block_owner) * dp_count + block_owner
    selector = (destination[None, :] == jnp.arange(slot_count * dp_count)[:, None]).astype(bf16)
    packed = jnp.einsum("pn,nrq->prq", selector, gradient, preferred_element_type=f32)
    packed = packed.astype(bf16).reshape(slot_count, dp_count, row_count, col_total)
    received = lax.all_to_all(packed, DP, split_axis=1, concat_axis=1, tiled=True)
    col_count = received.shape[3]
    blocks = received.reshape(slot_count, dp_count * row_count, col_count)
    turned = jnp.einsum("gkr,gkc->grc", eigen_basis, blocks, preferred_element_type=f32)
    scaled = (turned / (eigen_values[:, :, None] + damping)).astype(bf16)
    rotated = jnp.einsum("gkr,grc->gkc", eigen_basis, scaled, preferred_element_type=f32)
    rotated = rotated.astype(bf16).reshape(slot_count, dp_count, row_count, col_count)
    returned = lax.all_to_all(rotated, DP, split_axis=1, concat_axis=1, tiled=True)
    flattened = returned.reshape(slot_count * dp_count, row_count, col_total)
    result = jnp.einsum("pn,prq->nrq", selector, flattened, preferred_element_type=f32)
    return result.astype(bf16)


def shards(activations, tile_owner, gradient, block_owner, eigen_basis, eigen_values):
    factor = factor_part(activations, tile_owner)
    result = precondition_blocks(gradient, block_owner, eigen_basis, eigen_values)
    return (factor, result)


def solution(mesh):
    fine = Mesh(mesh.devices.reshape(4, 2, 8, 2, 2), ("y", "xl", "z", "xh", "c"))
    group = ("xh", "c")
    placed = (
        P(None, DP, None),
        P(),
        P(None, DP, group),
        P(),
        P(DP, None, None),
        P(DP, None),
    )
    return jax.shard_map(
        shards,
        mesh=fine,
        in_specs=placed,
        out_specs=(P(DP, None, group), P(None, DP, group)),
        check_vma=False,
    )
```

time: 555 us -> 265 us (0.48)
  waiting for transfers between devices: 435 us -> 157 us
  local copies, waits for them, and re-layouts: 51.1 us -> 18.5 us
  starting transfers between devices: 28.1 us -> 50.5 us
  other arithmetic: 0.4 us -> 20.5 us
  matrix products: 23.7 us -> 5.29 us
  between operations: 14.1 us -> 0.92 us
  Pallas kernels: 0 us -> 11.5 us
    reduce_scatter x1 -> x0, waiting for transfers between devices: 350 us -> none  [shards(): lax.psum_scatter(product.reshape(lax.axis_size('dp') * row_share, NT * NT...]
    ppermute x0 -> x11, waiting for transfers between devices: none -> 52.8 us  [the longest x3 17.4 us: around_z(): ahead = lax.ppermute((chunk(k) + ahead.astype(f32)).astype(bf16), 'z', up)]
    transpose x1 -> x2, local copies, waits for them, and re-layouts: 27.4 us -> 0.09 us  [the longest x1 0.05 us: factor_part(): as_last = arrived.transpose(0, 3, 2, 1, 4, 5).reshape(SLOTS, TILE, SLAB)]
    all_to_all x3 -> x6, waiting for transfers between devices: 85.5 us -> 104 us  [the longest x1 39.9 us: precondition_blocks(): lax.all_to_all(rotated, DP, split_axis=1, concat_axis=1, tiled=True)]
    dot_general x5 -> x4, matrix products: 23.7 us -> 5.29 us  [the longest x1 3.7 us: precondition_blocks(): jnp.einsum('gkr,grc->gkc', eigen_basis, scaled, preferred_element_type=f32)]
    ppermute x0 -> x11, starting transfers between devices: none -> 18.3 us  [the longest x3 7.53 us: around_z(): back = lax.ppermute((chunk(-k) + back.astype(f32)).astype(bf16), 'z', down)]
    convert_element_type x0 -> x8, other arithmetic: none -> 13.4 us  [the longest x2 4.22 us: around_z(): back = lax.ppermute((chunk(-k) + back.astype(f32)).astype(bf16), 'z', down)]
    pallas_call x0 -> x2, Pallas kernels: none -> 11.5 us  [the longest x1 6.91 us: last_products(): pl.pallas_call(last_kernel, out_shape=jax.ShapeDtypeStruct((TILE, wide),...]
  transfers between devices with their start and end apart: 4 -> 17, of which waited for: 3 -> 14; matrix products, arithmetic and copies ran while one was open for 3% -> 10% of each run, Pallas kernels for 0% -> 2%
where the time goes in v1:
time: 265 us; the launch traced here: 264 us
  waiting for transfers between devices  157 us (59%)
  starting transfers between devices  50.5 us (19%)
  other arithmetic  20.5 us (8%)
  local copies, waits for them, and re-layouts  18.5 us (7%)
  Pallas kernels  11.5 us (4%)
  matrix products  5.29 us (2%)
    all_to_all x1, waiting for transfers between devices, precondition_blocks(): lax.all_to_all(rotated, DP, split_axis=1, concat_axis=1, tiled=True)  39.9 us
    all_to_all x1, waiting for transfers between devices, precondition_blocks(): lax.all_to_all(packed, DP, split_axis=1, concat_axis=1, tiled=True)  39 us
    all_to_all x3, waiting for transfers between devices, scatter_sum(): lax.all_to_all(x.astype(bf16), axis, split_axis=0, concat_axis=0, tiled=T...  20.4 us
    ppermute x3, waiting for transfers between devices, around_z(): ahead = lax.ppermute((chunk(k) + ahead.astype(f32)).astype(bf16), 'z', up)  17.4 us
    all_to_all x3, starting transfers between devices, scatter_sum(): lax.all_to_all(x.astype(bf16), axis, split_axis=0, concat_axis=0, tiled=T...  13.8 us
    unnamed x23, local copies, waits for them, and re-layouts  10.6 us
    ppermute x1, waiting for transfers between devices, factor_shares(): near = lax.ppermute(near, 'xl', [(0, 1), (1, 0)])  10.2 us
    ppermute x3, starting transfers between devices, around_z(): back = lax.ppermute((chunk(-k) + back.astype(f32)).astype(bf16), 'z', down)  7.53 us
  transfers between devices with their start and end apart: 17, of which 14 were waited for; matrix products, arithmetic and copies ran while one was open for 10% of the time, Pallas kernels for 2%

profile of v1, /device:TPU:32, one launch (start us, length us, event | category | flops | bytes accessed | tf_op | source)
XLA Modules:
  0.0 264.2 jit_solution(3539327429165724830)
XLA Ops:
  0.7 6.9 %shard_map.78 = f32[512,3584]{1,0:T(8,128)S(1)} custom-call(s32[3]{0:T(128)S(1)} %pad_add_fusion.place, bf16[768,5120]{1,0:T(8,128)(2,1)} %bitcast.45), custom_call_target="tpu_custom_call" | custom-call | flops 2818572288 | bytes 15204352 | tf_op jit(solution)/shard_map/pallas_call | solution.py:101
  7.7 2.9 %copy-done.1 = f32[512,3584]{1,0:T(8,128)} copy-done((f32[512,3584]{1,0:T(8,128)}, f32[512,3584]{1,0:T(8,128)S(1)}, u32[]{:S(2)}) %copy-start.1) | copy-done | bytes 7340056
  10.7 2.0 collective-permute-start.2
  12.7 5.4 %collective-permute-done.2 = bf16[32,3584]{1,0:T(8,128)(2,1)S(1)} collective-permute-done((bf16[32,3584]{1,0:T(8,128)(2,1)S(1)}, bf16[32,3584]{1,0:T(8,128)(2,1)S(1)}, u32[]{:S(2)}, u32[]{:S(2)}) %collective-permute-start.2) | collective-permute-done | bytes 229408 | tf_op jit(solution)/shard_map/ppermute | solution.py:128
  18.1 1.3 add_convert_fusion.6
  19.4 2.0 collective-permute-start.3
  21.4 12.3 %collective-permute-done.3 = bf16[64,3584]{1,0:T(8,128)(2,1)S(1)} collective-permute-done((bf16[64,3584]{1,0:T(8,128)(2,1)S(1)}, bf16[64,3584]{1,0:T(8,128)(2,1)S(1)}, u32[]{:S(2)}, u32[]{:S(2)}) %collective-permute-start.3) | collective-permute-done | bytes 458784 | tf_op jit(solution)/shard_map/ppermute | solution.py:133
  33.7 1.3 add_convert_fusion.5
  35.1 3.0 %collective-permute-start.6 = (bf16[32,3584]{1,0:T(8,128)(2,1)S(1)}, bf16[32,3584]{1,0:T(8,128)(2,1)S(1)}, u32[]{:S(2)}, u32[]{:S(2)}) collective-permute-start(bf16[32,3584]{1,0:T(8,128)(2,1)S(1)} %get-tuple-element.19), channel_id=1, source_target_pairs={{0,28},{4,0},{8,4},{12,8},{16,12},{20,16},{24,20},{28,24},{1,29},{... | collective-permute-start | bytes 688136 | tf_op jit(solution)/shard_map/ppermute | solution.py:129
  38.1 3.8 %collective-permute-done.6 = bf16[32,3584]{1,0:T(8,128)(2,1)S(1)} collective-permute-done((bf16[32,3584]{1,0:T(8,128)(2,1)S(1)}, bf16[32,3584]{1,0:T(8,128)(2,1)S(1)}, u32[]{:S(2)}, u32[]{:S(2)}) %collective-permute-start.6) | collective-permute-done | bytes 229408 | tf_op jit(solution)/shard_map/ppermute | solution.py:129
  41.9 5.1 %collective-permute-done.4 = bf16[64,3584]{1,0:T(8,128)(2,1)S(1)} collective-permute-done((bf16[64,3584]{1,0:T(8,128)(2,1)S(1)}, bf16[64,3584]{1,0:T(8,128)(2,1)S(1)}, u32[]{:S(2)}, u32[]{:S(2)}) %collective-permute-start.4) | collective-permute-done | bytes 458784 | tf_op jit(solution)/shard_map/ppermute | solution.py:133
  47.1 1.6 add_convert_fusion.4
  48.7 3.0 %collective-permute-start.7 = (bf16[64,3584]{1,0:T(8,128)(2,1)S(1)}, bf16[64,3584]{1,0:T(8,128)(2,1)S(1)}, u32[]{:S(2)}, u32[]{:S(2)}) collective-permute-start(bf16[64,3584]{1,0:T(8,128)(2,1)S(1)} %get-tuple-element.17), channel_id=1, source_target_pairs={{0,28},{4,0},{8,4},{12,8},{16,12},{20,16},{24,20},{28,24},{1,29},{... | collective-permute-start | bytes 1376264 | tf_op jit(solution)/shard_map/ppermute | solution.py:134
  51.8 7.4 %collective-permute-done.7 = bf16[64,3584]{1,0:T(8,128)(2,1)S(1)} collective-permute-done((bf16[64,3584]{1,0:T(8,128)(2,1)S(1)}, bf16[64,3584]{1,0:T(8,128)(2,1)S(1)}, u32[]{:S(2)}, u32[]{:S(2)}) %collective-permute-start.7) | collective-permute-done | bytes 458784 | tf_op jit(solution)/shard_map/ppermute | solution.py:134
  59.2 2.1 add_convert_fusion.2
  61.2 2.5 collective-permute-start.8
  63.7 3.2 %copy-done.2 = bf16[2,384,5120]{2,1,0:T(8,128)(2,1)S(1)} copy-done((bf16[2,384,5120]{2,1,0:T(8,128)(2,1)S(1)}, bf16[2,384,5120]{2,1,0:T(8,128)(2,1)}, u32[]{:S(2)}) %copy-start.2) | copy-done | bytes 7864344
  66.9 4.6 %shard_map.77 = (f32[256,3456]{1,0:T(8,128)S(1)}, bf16[128,3456]{1,0:T(8,128)(2,1)S(1)}, bf16[128,3456]{1,0:T(8,128)(2,1)S(1)}) custom-call(s32[3]{0:T(128)S(1)} %pad_add_fusion.place, bf16[768,5120]{1,0:T(8,128)(2,1)S(1)} %bitcast.46), custom_call_target="tpu_custom_call" | custom-call | flops 2717908992 | bytes 13172736 | tf_op jit(solution)/shard_map/pallas_call | solution.py:76
  71.5 1.9 copy-done.3
  73.4 1.5 collective-permute-start
  74.9 2.1 collective-permute-start.1
  77.0 2.2 add_convert_fusion.1
  79.1 2.0 collective-permute-start.9
  81.2 10.2 %collective-permute-done = bf16[128,3456]{1,0:T(8,128)(2,1)} collective-permute-done((bf16[128,3456]{1,0:T(8,128)(2,1)S(1)}, bf16[128,3456]{1,0:T(8,128)(2,1)}, u32[]{:S(2)}, u32[]{:S(2)}) %collective-permute-start) | collective-permute-done | bytes 884768 | tf_op jit(solution)/shard_map/ppermute | solution.py:151
  91.4 2.4 collective-permute-done.1
  93.8 4.0 %add_convert_fusion = bf16[256,3456]{1,0:T(8,128)(2,1)} fusion(f32[256,3456]{1,0:T(8,128)} %copy-done.3, bf16[128,3456]{1,0:T(8,128)(2,1)} %collective-permute-done.1, bf16[128,3456]{1,0:T(8,128)(2,1)} %collective-permute-done), kind=kLoop, calls=%fused_computation.1 | loop fusion | flops 5308416 | bytes 7077888 | tf_op jit(solution)/shard_map/convert_element_type | solution.py:140
  97.9 4.5 %all-to-all-start = ((bf16[4,64,3456]{2,1,0:T(8,128)(2,1)}), bf16[4,64,3456]{2,1,0:T(8,128)(2,1)S(1)}, u32[]{:S(2)}, u32[]{:S(2)}) async-start(bf16[4,64,3456]{2,1,0:T(8,128)(2,1)} %bitcast.5), calls=%async_computation | async-start | bytes 3538944 | tf_op jit(solution)/shard_map/all_to_all | solution.py:140
  102.3 1.6 convert_add_fusion
  105.0 6.0 %collective-permute-done.10 = bf16[32,3584]{1,0:T(8,128)(2,1)S(1)} collective-permute-done((bf16[32,3584]{1,0:T(8,128)(2,1)S(1)}, bf16[32,3584]{1,0:T(8,128)(2,1)S(1)}, u32[]{:S(2)}, u32[]{:S(2)}) %collective-permute-start.10) | collective-permute-done | bytes 229408 | tf_op jit(solution)/shard_map/ppermute | solution.py:159
  111.0 1.8 fusion.10
  112.8 7.7 %all-to-all-done = bf16[4,64,3456]{2,1,0:T(8,128)(2,1)S(1)} async-done(((bf16[4,64,3456]{2,1,0:T(8,128)(2,1)}), bf16[4,64,3456]{2,1,0:T(8,128)(2,1)S(1)}, u32[]{:S(2)}, u32[]{:S(2)}) %all-to-all-start) | async-done | bytes 1769504 | tf_op jit(solution)/shard_map/all_to_all | solution.py:140
  120.4 3.4 %all-to-all-start.2 = ((bf16[4,8,3584]{2,1,0:T(8,128)(2,1)}), bf16[4,8,3584]{2,1,0:T(8,128)(2,1)S(1)}, u32[]{:S(2)}, u32[]{:S(2)}) async-start(bf16[4,8,3584]{2,1,0:T(8,128)(2,1)} %fusion.10), calls=%async_computation.2 | async-start | bytes 458752 | tf_op jit(solution)/shard_map/all_to_all | solution.py:140
  123.8 1.1 reduce_sum.49
  125.0 5.3 %all-to-all-done.2 = bf16[4,8,3584]{2,1,0:T(8,128)(2,1)S(1)} async-done(((bf16[4,8,3584]{2,1,0:T(8,128)(2,1)}), bf16[4,8,3584]{2,1,0:T(8,128)(2,1)S(1)}, u32[]{:S(2)}, u32[]{:S(2)}) %all-to-all-start.2) | async-done | bytes 229408 | tf_op jit(solution)/shard_map/all_to_all | solution.py:140
  130.3 6.0 %all-to-all-start.1 = ((bf16[8,8,3456]{2,1,0:T(8,128)(2,1)}), bf16[8,8,3456]{2,1,0:T(8,128)(2,1)S(1)}, u32[]{:S(2)}, u32[]{:S(2)}) async-start(bf16[8,8,3456]{2,1,0:T(8,128)(2,1)} %bitcast.6), calls=%async_computation.1 | async-start | bytes 884736 | tf_op jit(solution)/shard_map/all_to_all | solution.py:140
  137.3 2.5 copy.36
  139.8 7.4 %all-to-all-done.1 = bf16[8,8,3456]{2,1,0:T(8,128)(2,1)S(1)} async-done(((bf16[8,8,3456]{2,1,0:T(8,128)(2,1)}), bf16[8,8,3456]{2,1,0:T(8,128)(2,1)S(1)}, u32[]{:S(2)}, u32[]{:S(2)}) %all-to-all-start.1) | async-done | bytes 442400 | tf_op jit(solution)/shard_map/all_to_all | solution.py:140
  148.0 5.6 %all-to-all-start.4 = ((bf16[2,64,8,1024]{3,2,0,1:T(8,128)(2,1)}), bf16[2,64,8,1024]{3,2,0,1:T(8,128)(2,1)S(1)}, u32[]{:S(2)}, u32[]{:S(2)}) async-start(bf16[2,64,8,1024]{3,2,0,1:T(8,128)(2,1)} %copy.36), calls=%async_computation.4 | async-start | bytes 4194304 | tf_op jit(solution)/shard_map/all_to_all | solution.py:200
  153.9 1.0 convert_reduce_fusion.1
  154.8 1.1 convert_reduce_fusion
  157.3 39.0 %all-to-all-done.4 = bf16[2,64,8,1024]{3,2,0,1:T(8,128)(2,1)S(1)} async-done(((bf16[2,64,8,1024]{3,2,0,1:T(8,128)(2,1)}), bf16[2,64,8,1024]{3,2,0,1:T(8,128)(2,1)S(1)}, u32[]{:S(2)}, u32[]{:S(2)}) %all-to-all-start.4) | async-done | bytes 2097184 | tf_op jit(solution)/shard_map/all_to_all | solution.py:200
  196.3 6.4 %all-to-all-start.3 = ((bf16[2,64,8,128]{3,0,2,1:T(2,128)(2,1)}), bf16[2,64,8,128]{3,0,2,1:T(2,128)(2,1)S(1)}, u32[]{:S(2)}, u32[]{:S(2)}) async-start(bf16[2,64,8,128]{3,0,2,1:T(2,128)(2,1)} %copy.32), calls=%async_computation.3 | async-start | bytes 524288 | tf_op jit(solution)/shard_map/all_to_all | solution.py:180
  202.7 3.7 %convert_bitcast_fusion = bf16[2,64,8,1024]{3,2,1,0:T(8,128)(2,1)} fusion(bf16[2,512,512]{2,1,0:T(8,128)(2,1)S(1)} %copy-done, f32[2,512]{1,0:T(2,128)S(1)} %broadcast_add_fusion, bf16[2,64,8,1024]{3,2,0,1:T(8,128)(2,1)S(1)} %all-to-all-done.4), kind=kOutput, calls=%fused_computation.5 | convolution fusion | flops 2150629376 | bytes 5246976 | tf_op jit(solution)/shard_map/gkr,grc->gkc/dot_general | solution.py:205
  206.4 3.2 %copy.39 = bf16[2,64,8,1024]{3,2,0,1:T(8,128)(2,1)} copy(bf16[2,64,8,1024]{3,2,1,0:T(8,128)(2,1)} %convert_bitcast_fusion) | data formatting | bytes 4194304 | tf_op jit(solution)/shard_map/reshape | solution.py:206
  209.5 4.9 %all-to-all-done.3 = bf16[2,64,8,128]{3,0,2,1:T(2,128)(2,1)S(1)} async-done(((bf16[2,64,8,128]{3,0,2,1:T(2,128)(2,1)}), bf16[2,64,8,128]{3,0,2,1:T(2,128)(2,1)S(1)}, u32[]{:S(2)}, u32[]{:S(2)}) %all-to-all-start.3) | async-done | bytes 262176 | tf_op jit(solution)/shard_map/all_to_all | solution.py:180
  214.4 6.4 %all-to-all-start.5 = ((bf16[2,64,8,1024]{3,2,0,1:T(8,128)(2,1)}), bf16[2,64,8,1024]{3,2,0,1:T(8,128)(2,1)S(1)}, u32[]{:S(2)}, u32[]{:S(2)}) async-start(bf16[2,64,8,1024]{3,2,0,1:T(8,128)(2,1)} %copy.39), calls=%async_computation.5 | async-start | bytes 4194304 | tf_op jit(solution)/shard_map/all_to_all | solution.py:207
  221.9 39.9 %all-to-all-done.5 = bf16[2,64,8,1024]{3,2,0,1:T(8,128)(2,1)S(1)} async-done(((bf16[2,64,8,1024]{3,2,0,1:T(8,128)(2,1)}), bf16[2,64,8,1024]{3,2,0,1:T(8,128)(2,1)S(1)}, u32[]{:S(2)}, u32[]{:S(2)}) %all-to-all-start.5) | async-done | bytes 2097184 | tf_op jit(solution)/shard_map/all_to_all | solution.py:207
  261.9 1.2 copy.40
  (45 shorter events, 7.0 us)
Async XLA Ops:
  0.6 202.0 %copy-start = (bf16[2,512,512]{2,1,0:T(8,128)(2,1)S(1)}, bf16[2,512,512]{2,1,0:T(8,128)(2,1)}, u32[]{:S(2)}) copy-start(bf16[2,512,512]{2,1,0:T(8,128)(2,1)} %param.10) | copy-start | bytes 3145732
  7.7 3.0 %copy-start.1 = (f32[512,3584]{1,0:T(8,128)}, f32[512,3584]{1,0:T(8,128)S(1)}, u32[]{:S(2)}) copy-start(f32[512,3584]{1,0:T(8,128)S(1)} %shard_map.78) | copy-start | bytes 22020100
  10.7 7.4 %collective-permute-start.2 = (bf16[32,3584]{1,0:T(8,128)(2,1)S(1)}, bf16[32,3584]{1,0:T(8,128)(2,1)S(1)}, u32[]{:S(2)}, u32[]{:S(2)}) collective-permute-start(bf16[32,3584]{1,0:T(8,128)(2,1)S(1)} %get-tuple-element.18), channel_id=1, source_target_pairs={{0,4},{4,8},{8,12},{12,16},{16,20},{20,24},{24,28},{28,0},{1,5},{5... | collective-permute-start | bytes 688136 | tf_op jit(solution)/shard_map/ppermute | solution.py:128
  19.4 14.3 %collective-permute-start.3 = (bf16[64,3584]{1,0:T(8,128)(2,1)S(1)}, bf16[64,3584]{1,0:T(8,128)(2,1)S(1)}, u32[]{:S(2)}, u32[]{:S(2)}) collective-permute-start(bf16[64,3584]{1,0:T(8,128)(2,1)S(1)} %add_convert_fusion.6), channel_id=1, source_target_pairs={{0,4},{4,8},{8,12},{12,16},{16,20},{20,24},{24,28},{28,0},{1,5},{5... | collective-permute-start | bytes 1376264 | tf_op jit(solution)/shard_map/ppermute | solution.py:133
  35.0 12.1 %collective-permute-start.4 = (bf16[64,3584]{1,0:T(8,128)(2,1)S(1)}, bf16[64,3584]{1,0:T(8,128)(2,1)S(1)}, u32[]{:S(2)}, u32[]{:S(2)}) collective-permute-start(bf16[64,3584]{1,0:T(8,128)(2,1)S(1)} %add_convert_fusion.5), channel_id=1, source_target_pairs={{0,4},{4,8},{8,12},{12,16},{16,20},{20,24},{24,28},{28,0},{1,5},{5... | collective-permute-start | bytes 1376264 | tf_op jit(solution)/shard_map/ppermute | solution.py:133
  35.1 6.9 %collective-permute-start.6 = (bf16[32,3584]{1,0:T(8,128)(2,1)S(1)}, bf16[32,3584]{1,0:T(8,128)(2,1)S(1)}, u32[]{:S(2)}, u32[]{:S(2)}) collective-permute-start(bf16[32,3584]{1,0:T(8,128)(2,1)S(1)} %get-tuple-element.19), channel_id=1, source_target_pairs={{0,28},{4,0},{8,4},{12,8},{16,12},{20,16},{24,20},{28,24},{1,29},{... | collective-permute-start | bytes 688136 | tf_op jit(solution)/shard_map/ppermute | solution.py:129
  48.7 10.4 %collective-permute-start.7 = (bf16[64,3584]{1,0:T(8,128)(2,1)S(1)}, bf16[64,3584]{1,0:T(8,128)(2,1)S(1)}, u32[]{:S(2)}, u32[]{:S(2)}) collective-permute-start(bf16[64,3584]{1,0:T(8,128)(2,1)S(1)} %get-tuple-element.17), channel_id=1, source_target_pairs={{0,28},{4,0},{8,4},{12,8},{16,12},{20,16},{24,20},{28,24},{1,29},{... | collective-permute-start | bytes 1376264 | tf_op jit(solution)/shard_map/ppermute | solution.py:134
  61.2 15.8 %collective-permute-start.8 = (bf16[64,3584]{1,0:T(8,128)(2,1)}, bf16[64,3584]{1,0:T(8,128)(2,1)}, u32[]{:S(2)}, u32[]{:S(2)}) collective-permute-start(bf16[64,3584]{1,0:T(8,128)(2,1)} %add_convert_fusion.2), channel_id=1, source_target_pairs={{0,28},{4,0},{8,4},{12,8},{16,12},{20,16},{24,20},{28,24},{1,29},{... | collective-permute-start | bytes 1376264 | tf_op jit(solution)/shard_map/ppermute | solution.py:134
  63.7 3.2 %copy-start.2 = (bf16[2,384,5120]{2,1,0:T(8,128)(2,1)S(1)}, bf16[2,384,5120]{2,1,0:T(8,128)(2,1)}, u32[]{:S(2)}) copy-start(bf16[2,384,5120]{2,1,0:T(8,128)(2,1)} %param.6) | copy-start | bytes 23592964
  71.5 1.9 copy-start.3
  73.4 18.0 %collective-permute-start = (bf16[128,3456]{1,0:T(8,128)(2,1)S(1)}, bf16[128,3456]{1,0:T(8,128)(2,1)}, u32[]{:S(2)}, u32[]{:S(2)}) collective-permute-start(bf16[128,3456]{1,0:T(8,128)(2,1)S(1)} %get-tuple-element.6), channel_id=1, source_target_pairs={{0,32},{32,0},{1,33},{33,1},{2,34},{34,2},{3,35},{35,3},{4,36},{36... | collective-permute-start | bytes 2654216 | tf_op jit(solution)/shard_map/ppermute | solution.py:151
  74.9 18.9 %collective-permute-start.1 = (bf16[128,3456]{1,0:T(8,128)(2,1)S(1)}, bf16[128,3456]{1,0:T(8,128)(2,1)}, u32[]{:S(2)}, u32[]{:S(2)}) collective-permute-start(bf16[128,3456]{1,0:T(8,128)(2,1)S(1)} %get-tuple-element.7), channel_id=1, source_target_pairs={{0,34},{2,32},{32,2},{34,0},{1,35},{3,33},{33,3},{35,1},{4,38},{6,... | collective-permute-start | bytes 2654216 | tf_op jit(solution)/shard_map/ppermute | solution.py:152
  77.0 25.4 %collective-permute-start.5 = (bf16[64,3584]{1,0:T(8,128)(2,1)S(1)}, bf16[64,3584]{1,0:T(8,128)(2,1)}, u32[]{:S(2)}, u32[]{:S(2)}) collective-permute-start(bf16[64,3584]{1,0:T(8,128)(2,1)S(1)} %get-tuple-element.16), channel_id=1, source_target_pairs={{0,4},{4,8},{8,12},{12,16},{16,20},{20,24},{24,28},{28,0},{1,5},{5... | collective-permute-start | bytes 1376264 | tf_op jit(solution)/shard_map/ppermute | solution.py:133
  79.1 23.2 %collective-permute-start.9 = (bf16[64,3584]{1,0:T(8,128)(2,1)}, bf16[64,3584]{1,0:T(8,128)(2,1)}, u32[]{:S(2)}, u32[]{:S(2)}) collective-permute-start(bf16[64,3584]{1,0:T(8,128)(2,1)} %add_convert_fusion.1), channel_id=1, source_target_pairs={{0,28},{4,0},{8,4},{12,8},{16,12},{20,16},{24,20},{28,24},{1,29},{... | collective-permute-start | bytes 1376264 | tf_op jit(solution)/shard_map/ppermute | solution.py:134
  97.9 22.6 %all-to-all-start = ((bf16[4,64,3456]{2,1,0:T(8,128)(2,1)}), bf16[4,64,3456]{2,1,0:T(8,128)(2,1)S(1)}, u32[]{:S(2)}, u32[]{:S(2)}) async-start(bf16[4,64,3456]{2,1,0:T(8,128)(2,1)} %bitcast.5), calls=%async_computation | async-start | bytes 3538944 | tf_op jit(solution)/shard_map/all_to_all | solution.py:140
  103.9 0.9 copy-start.4
  104.9 6.1 %collective-permute-start.10 = (bf16[32,3584]{1,0:T(8,128)(2,1)S(1)}, bf16[32,3584]{1,0:T(8,128)(2,1)S(1)}, u32[]{:S(2)}, u32[]{:S(2)}) collective-permute-start(bf16[32,3584]{1,0:T(8,128)(2,1)S(1)} %dynamic-slice_convert_fusion.1), channel_id=1, source_target_pairs={{0,32},{32,0},{1,33},{33,1},{2,34},{34,2},{3,35},{35,3},{4,36},{36... | collective-permute-start | bytes 688136 | tf_op jit(solution)/shard_map/ppermute | solution.py:159
  105.0 31.3 %copy-start.10 = (s32[10]{0:T(128)S(1)}, s32[10]{0:T(128)}, u32[]{:S(2)}) copy-start(s32[10]{0:T(128)} %param.9) | copy-start | bytes 124
  105.0 31.5 %copy-start.7 = (bf16[10,8,1024]{2,1,0:T(8,128)(2,1)S(1)}, bf16[10,8,1024]{2,1,0:T(8,128)(2,1)}, u32[]{:S(2)}) copy-start(bf16[10,8,1024]{2,1,0:T(8,128)(2,1)} %param.8) | copy-start | bytes 491524
  120.4 9.9 %all-to-all-start.2 = ((bf16[4,8,3584]{2,1,0:T(8,128)(2,1)}), bf16[4,8,3584]{2,1,0:T(8,128)(2,1)S(1)}, u32[]{:S(2)}, u32[]{:S(2)}) async-start(bf16[4,8,3584]{2,1,0:T(8,128)(2,1)} %fusion.10), calls=%async_computation.2 | async-start | bytes 458752 | tf_op jit(solution)/shard_map/all_to_all | solution.py:140
  130.3 9.5 %copy-start.6 = (bf16[4,8,3584]{2,1,0:T(8,128)(2,1)}, bf16[4,8,3584]{2,1,0:T(8,128)(2,1)S(1)}, u32[]{:S(2)}) copy-start(bf16[4,8,3584]{2,1,0:T(8,128)(2,1)S(1)} %all-to-all-done.2) | copy-start | bytes 688132
  130.3 16.9 %all-to-all-start.1 = ((bf16[8,8,3456]{2,1,0:T(8,128)(2,1)}), bf16[8,8,3456]{2,1,0:T(8,128)(2,1)S(1)}, u32[]{:S(2)}, u32[]{:S(2)}) async-start(bf16[8,8,3456]{2,1,0:T(8,128)(2,1)} %bitcast.6), calls=%async_computation.1 | async-start | bytes 884736 | tf_op jit(solution)/shard_map/all_to_all | solution.py:140
  139.8 13.8 %copy-start.9 = (s32[55]{0:T(128)S(1)}, s32[55]{0:T(128)}, u32[]{:S(2)}) copy-start(s32[55]{0:T(128)} %param.7) | copy-start | bytes 664
  139.8 14.0 %copy-start.8 = (f32[2,512]{1,0:T(2,128)S(1)}, f32[2,512]{1,0:T(2,128)}, u32[]{:S(2)}) copy-start(f32[2,512]{1,0:T(2,128)} %param.11) | copy-start | bytes 12292
  147.2 0.8 copy-start.5
  148.0 48.3 %all-to-all-start.4 = ((bf16[2,64,8,1024]{3,2,0,1:T(8,128)(2,1)}), bf16[2,64,8,1024]{3,2,0,1:T(8,128)(2,1)S(1)}, u32[]{:S(2)}, u32[]{:S(2)}) async-start(bf16[2,64,8,1024]{3,2,0,1:T(8,128)(2,1)} %copy.36), calls=%async_computation.4 | async-start | bytes 4194304 | tf_op jit(solution)/shard_map/all_to_all | solution.py:200
  196.3 18.1 %all-to-all-start.3 = ((bf16[2,64,8,128]{3,0,2,1:T(2,128)(2,1)}), bf16[2,64,8,128]{3,0,2,1:T(2,128)(2,1)S(1)}, u32[]{:S(2)}, u32[]{:S(2)}) async-start(bf16[2,64,8,128]{3,0,2,1:T(2,128)(2,1)} %copy.32), calls=%async_computation.3 | async-start | bytes 524288 | tf_op jit(solution)/shard_map/all_to_all | solution.py:180
  214.4 47.5 %all-to-all-start.5 = ((bf16[2,64,8,1024]{3,2,0,1:T(8,128)(2,1)}), bf16[2,64,8,1024]{3,2,0,1:T(8,128)(2,1)S(1)}, u32[]{:S(2)}, u32[]{:S(2)}) async-start(bf16[2,64,8,1024]{3,2,0,1:T(8,128)(2,1)} %copy.39), calls=%async_computation.5 | async-start | bytes 4194304 | tf_op jit(solution)/shard_map/all_to_all | solution.py:207

commit v2 on v1

v2 whole, which is shorter than its diff:
```python
import functools

import jax
import jax.numpy as jnp
import numpy as np
from jax import lax
from jax.experimental import pallas as pl
from jax.experimental.pallas import tpu as pltpu
from jax.sharding import Mesh, PartitionSpec as P

TILE = 512
NT = 10
UT = NT * (NT + 1) // 2
SLOTS = 2
SLAB = 128
FIRST_ROWS = 3
FIRST_TILES = sum(NT - i for i in range(FIRST_ROWS))
LAST_TILES = UT - FIRST_TILES
DP = ("y", "xl", "z")

damping = 0.1
bf16 = jnp.bfloat16
f32 = jnp.float32


def slot_rank(owner_ids):
    entries = owner_ids.shape[0]
    position = jnp.arange(entries)
    same_owner = owner_ids[:, None] == owner_ids[None, :]
    earlier = position[None, :] < position[:, None]
    return jnp.sum(jnp.logical_and(same_owner, earlier), axis=1)


def dot(a, b):
    return lax.dot_general(a, b, (((1,), (0,)), ((), ())), preferred_element_type=f32)


def fill(slab, act, which, begin):
    for j in range(begin, NT):
        at = pl.multiple_of(j * TILE + which * SLAB, SLAB)
        slab[:, j * SLAB : (j + 1) * SLAB] = act[:, pl.ds(at, SLAB)]


def spans(i):
    return [(at, min(at + 256, NT * SLAB)) for at in range(i * SLAB, NT * SLAB, 256)]


def sent_kernel(place, act, near, far, out, slab, other, turned):
    low, mine, theirs = place[0], place[1], place[2]
    fill(slab, act, mine, 0)
    fill(other, act, theirs, 0)
    start = 0
    for i in range(FIRST_ROWS):
        at = pl.multiple_of(i * TILE + (1 - low) * 256, 256)
        turned[0:256, :] = act[:, pl.ds(at, 256)].T
        for begin, end in spans(i):
            to = slice(start, start + end - begin)
            near[:, to] = dot(turned[0:128, :], slab[:, begin:end]).astype(bf16)
            far[:, to] = dot(turned[128:256, :], other[:, begin:end]).astype(bf16)
            start += end - begin
    start = 0
    for i in range(FIRST_ROWS, NT):
        turned[...] = act[:, i * TILE : (i + 1) * TILE].T
        for begin, end in spans(i):
            out[:, start : start + end - begin] = dot(turned[...], slab[:, begin:end])
            start += end - begin


def kept_kernel(place, act, own, slab, turned):
    low, mine = place[0], place[1]
    fill(slab, act, mine, 0)
    start = 0
    for i in range(FIRST_ROWS):
        turned[...] = act[:, pl.ds(pl.multiple_of(i * TILE + low * 256, 256), 256)].T
        for begin, end in spans(i):
            own[:, start : start + end - begin] = dot(turned[...], slab[:, begin:end])
            start += end - begin


VMEM = pl.BlockSpec(memory_space=pltpu.VMEM)
SMEM = pl.BlockSpec(memory_space=pltpu.SMEM)


def call(kernel, outs, scratch, flops, *operands, scalars=1):
    moved = sum(x.size * x.dtype.itemsize for x in operands)
    moved += sum(x.size * x.dtype.itemsize for x in outs)
    return pl.pallas_call(
        kernel,
        out_shape=tuple(outs),
        in_specs=[SMEM] * scalars + [VMEM] * (len(operands) - scalars),
        out_specs=(VMEM,) * len(outs),
        scratch_shapes=[pltpu.VMEM(shape, dtype) for shape, dtype in scratch],
        compiler_params=pltpu.CompilerParams(vmem_limit_bytes=40 * 2**20),
        cost_estimate=pl.CostEstimate(flops=flops, bytes_accessed=moved, transcendentals=0),
    )(*operands)


def array(shape, dtype):
    return jax.ShapeDtypeStruct(shape, dtype)


def sent_products(act, place):
    tokens = act.shape[0]
    wide, rest = FIRST_TILES * SLAB, LAST_TILES * SLAB
    return call(
        sent_kernel,
        [array((128, wide), bf16), array((128, wide), bf16), array((TILE, rest), f32)],
        [((tokens, NT * SLAB), bf16), ((tokens, NT * SLAB), bf16), ((TILE, tokens), bf16)],
        2 * tokens * (256 * wide + TILE * rest),
        place,
        act,
    )


def kept_products(act, place):
    tokens = act.shape[0]
    wide = FIRST_TILES * SLAB
    [own] = call(
        kept_kernel,
        [array((256, wide), f32)],
        [((tokens, NT * SLAB), bf16), ((256, tokens), bf16)],
        2 * tokens * 256 * wide,
        place,
        act,
    )
    return own


def around_z(product):
    n = lax.axis_size("z")
    z = lax.axis_index("z")
    rows = product.shape[0] // n
    half = rows // 2
    up = [(i, (i + 1) % n) for i in range(n)]
    down = [(i, (i - 1) % n) for i in range(n)]

    def chunk(k):
        return lax.dynamic_slice_in_dim(product, lax.rem(z + (k + n), n) * rows, rows, 0)

    ahead = lax.ppermute(chunk(n // 2)[:half].astype(bf16), "z", up)
    back = lax.ppermute(chunk(n // 2)[half:].astype(bf16), "z", down)
    ahead = jnp.concatenate([ahead, jnp.zeros_like(ahead)], axis=0)
    back = jnp.concatenate([jnp.zeros_like(back), back], axis=0)
    for k in range(n // 2 - 1, 0, -1):
        ahead = lax.ppermute((chunk(k) + ahead.astype(f32)).astype(bf16), "z", up)
        back = lax.ppermute((chunk(-k) + back.astype(f32)).astype(bf16), "z", down)
    return chunk(0) + ahead.astype(f32) + back.astype(f32)


def scatter_sum(x, axis):
    n = lax.axis_size(axis)
    got = lax.all_to_all(x.astype(bf16), axis, split_axis=0, concat_axis=0, tiled=True)
    return jnp.sum(got.reshape(n, x.shape[0] // n, x.shape[1]).astype(f32), axis=0)


def block_units():
    places = [d for d in range(64) if (d // 8 + d % 8) % 8 < NT // 2]
    unit = [0] * 64
    for at, d in enumerate(places):
        unit[d] = at
    return unit, places


UNIT, PLACES = block_units()
COLS = 256


def scatter_kernel(place, basis, values, grad, out):
    half = pl.ds(pl.multiple_of(place[3] * 256, 256), 256)
    out[:, 0:256] = basis[0, :, half]
    out[:, 256:512] = basis[1, :, half]
    full = grad[...].astype(f32)

    def piece(d):
        block, quarter = divmod(UNIT[d], 4)
        return full[block * 8 : block * 8 + 8, quarter * COLS : (quarter + 1) * COLS]

    for d in range(0, 64, 2):
        pair = jnp.concatenate([piece(d), piece(d + 1)], axis=0)
        out[d * 8 : d * 8 + 16, 512:768] = pair.astype(bf16)
    parts, left = [], values[...]
    for _ in range(3):
        part = left.astype(bf16).astype(f32)
        parts.append(part)
        left = left - part
    rows = jnp.concatenate([*parts, jnp.zeros((122, TILE), f32)], axis=0)
    out[:, 768:896] = rows.T.astype(bf16)


def forward_kernel(owner, slot, got, out):
    found = []
    for b in range(NT):
        at = pl.multiple_of(owner[b] // 2 * 16, 16)
        pair = got[pl.ds(at, 16), :].astype(f32)
        mine = jnp.where(owner[b] % 2 == 0, pair[0:8], pair[8:16])
        rows = jnp.where(slot[b] == 0, mine[:, 0:256], mine[:, 256:512])
        found.append(jnp.concatenate([rows, mine[:, 768:896]], axis=1))
    for d in range(0, 64, 2):
        pair = jnp.concatenate([found[UNIT[d] // 4], found[UNIT[d + 1] // 4]], axis=0)
        out[d * 8 : d * 8 + 16, :] = pair.astype(bf16)


def rotate_kernel(place, mine, theirs, got, out, basis):
    core, slot = place[0], place[1]
    basis[:, pl.ds(pl.multiple_of(core * 256, 256), 256)] = mine[:, 0:256]
    basis[:, pl.ds(pl.multiple_of((1 - core) * 256, 256), 256)] = theirs[...]
    parts = mine[:, 256:384].astype(f32)
    lane = lax.broadcasted_iota(jnp.int32, parts.shape, 1)
    ours = (lane < 6) & (lane % 2 == slot)
    values = jnp.sum(jnp.where(ours, parts, 0.0), axis=1, keepdims=True)
    turned = dot(basis[...].T, got[:, 512:768])
    scaled = (turned / (values + damping)).astype(bf16)
    out[...] = dot(basis[...], scaled).astype(bf16)


def pack_kernel(total, owner, slot, first, last, rotated, out, sums, slots):
    wide = FIRST_TILES * SLAB
    for at, got in ((0, first), (wide, last)):
        full = got[...].astype(f32)
        acc = full[0:8]
        for k in range(8, full.shape[0], 8):
            acc = acc + full[k : k + 8]
        sums[:, at : at + full.shape[1]] = acc / total
    slots[...] = jnp.zeros_like(slots)
    for u in range(UT):
        row = pl.multiple_of(owner[u] * 8, 8)
        lane = pl.multiple_of(slot[u] * SLAB, SLAB)
        slots[pl.ds(row, 8), pl.ds(lane, SLAB)] = sums[:, u * SLAB : (u + 1) * SLAB]
    out[:, 0:256] = slots[...].astype(bf16)
    out[:, 256:512] = rotated[...]


def unpack_kernel(is_first, got, factor, result):
    shares = got[:, 0:256].astype(f32)
    for s in range(SLOTS):
        lanes = slice(s * SLAB, (s + 1) * SLAB)

        @pl.when(is_first[s] == 1)
        def _():
            for y in range(4):
                for x in range(2):
                    to, at = s * TILE + x * 256 + y * 64, (y * 2 + x) * 64
                    factor[to : to + 64, :] = shares[at : at + 64, lanes]

        @pl.when(is_first[s] == 0)
        def _():
            for y in range(4):
                for x in range(2):
                    for z in range(8):
                        to, at = s * TILE + z * 64 + x * 32 + y * 8, (y * 2 + x) * 64 + z * 8
                        factor[to : to + 8, :] = shares[at : at + 8, lanes]

    turned = got[:, 256:512].astype(f32)
    for b in range(0, NT, 2):
        for q in range(4):
            pair = [turned[PLACES[u] * 8 : PLACES[u] * 8 + 8] for u in (b * 4 + q, b * 4 + 4 + q)]
            result[b * 8 : b * 8 + 16, q * COLS : (q + 1) * COLS] = jnp.concatenate(pair, axis=0).astype(bf16)


def exchange(x, axis):
    return lax.all_to_all(x, axis, split_axis=0, concat_axis=0, tiled=True)


def shards(activations, tile_owner, gradient, block_owner, eigen_basis, eigen_values):
    micro, tokens, width = activations.shape
    blocks, rows, cols = gradient.shape
    dp_count = lax.axis_size(DP)
    act = activations.reshape(micro * tokens, width)
    me = lax.axis_index(DP)
    low = lax.axis_index("xl")
    high, core = lax.axis_index("xh"), lax.axis_index("c")
    place = jnp.stack([low, high * 2 + core, (1 - high) * 2 + core, core]).astype(jnp.int32)
    tile_rank = slot_rank(tile_owner).astype(jnp.int32)
    block_rank = slot_rank(block_owner).astype(jnp.int32)

    [out] = call(
        scatter_kernel, [array((TILE, 896), bf16)], [], 0,
        place, eigen_basis, eigen_values, gradient.reshape(blocks * rows, cols),
    )
    got = exchange(out, DP)

    near, far, last = sent_products(act, place)
    near = lax.ppermute(near, "xl", [(0, 1), (1, 0)])
    far = lax.ppermute(far, ("xl", "xh"), [(i, 3 - i) for i in range(4)])
    own = kept_products(act, place)

    [out] = call(forward_kernel, [array((TILE, 384), bf16)], [], 0, block_owner, block_rank, got, scalars=2)
    mine = exchange(out, DP)
    theirs = lax.ppermute(mine[:, :256], "c", [(0, 1), (1, 0)])
    my_block = jnp.asarray(np.array(UNIT) // 4, jnp.int32)[me]
    [rotated] = call(
        rotate_kernel, [array((TILE, COLS), bf16)], [((TILE, TILE), bf16)], 4 * TILE * TILE * COLS,
        jnp.stack([core, block_rank[my_block]]).astype(jnp.int32), mine, theirs, got,
    )

    last = around_z(last)
    half = last.shape[0] // 2
    sent = lax.dynamic_slice_in_dim(last, (1 - low) * half, half, 0)
    kept = lax.dynamic_slice_in_dim(last, low * half, half, 0)
    last = kept + lax.ppermute(sent.astype(bf16), "xl", [(0, 1), (1, 0)]).astype(f32)
    last = exchange(last.astype(bf16), "y")

    first = own + jnp.concatenate([near, far], axis=0).astype(f32)
    first = exchange(first.astype(bf16), "y")
    first = jnp.sum(first.reshape(4, 64, -1).astype(f32), axis=0)
    first = exchange(first.astype(bf16), "z")

    [out] = call(
        functools.partial(pack_kernel, micro * tokens * dp_count),
        [array((TILE, 512), bf16)], [((8, UT * SLAB), f32), ((TILE, 256), f32)], 0,
        tile_owner, tile_rank, first, last, rotated, scalars=2,
    )
    final = exchange(out, DP)
    slot = jnp.arange(SLOTS)
    held = (tile_owner[None, :] == me) & (tile_rank[None, :] == slot[:, None])
    is_first = jnp.any(held & (jnp.arange(UT) < FIRST_TILES)[None, :], axis=1)
    factor, result = call(
        unpack_kernel, [array((SLOTS * TILE, SLAB), f32), array((blocks * rows, cols), bf16)], [], 0,
        is_first.astype(jnp.int32), final,
    )
    return factor.reshape(SLOTS, TILE, SLAB), result.reshape(blocks, rows, cols)


def solution(mesh):
    fine = Mesh(mesh.devices.reshape(4, 2, 8, 2, 2), ("y", "xl", "z", "xh", "c"))
    group = ("xh", "c")
    placed = (
        P(None, DP, None),
        P(),
        P(None, DP, group),
        P(),
        P(DP, None, None),
        P(DP, None),
    )
    return jax.shard_map(
        shards,
        mesh=fine,
        in_specs=placed,
        out_specs=(P(DP, None, group), P(None, DP, group)),
        check_vma=False,
    )
```

time: 265 us -> 208 us (0.78)
  waiting for transfers between devices: 157 us -> 101 us
  local copies, waits for them, and re-layouts: 18.5 us -> 8.18 us
  Pallas kernels: 11.5 us -> 19.1 us
  starting transfers between devices: 50.5 us -> 57.5 us
  matrix products: 5.29 us -> 0 us
    all_to_all x6, waiting for transfers between devices: 104 us -> 52.9 us  [exchange(): return lax.all_to_all(x, axis, split_axis=0, concat_axis=0, tiled=True)]
    pallas_call x2 -> x7, Pallas kernels: 11.5 us -> 19.1 us  [call(): pl.pallas_call(kernel, out_shape=tuple(outs), in_specs=[SMEM] * scalars +...]
    reshape x3 -> x0, local copies, waits for them, and re-layouts: 6.63 us -> none  [the longest x1 3.17 us: precondition_blocks(): rotated.astype(bf16).reshape(slot_count, dp_count, row_count, col_count)]
    all_to_all x6, starting transfers between devices: 32.2 us -> 38 us  [exchange(): return lax.all_to_all(x, axis, split_axis=0, concat_axis=0, tiled=True)]
    ppermute x3 -> x4, waiting for transfers between devices: 18.6 us -> 13.2 us  [the longest x1 13.2 us: shards(): near = lax.ppermute(near, 'xl', [(0, 1), (1, 0)])]
    dot_general x4 -> x0, matrix products: 5.29 us -> none  [the longest x1 3.7 us: precondition_blocks(): jnp.einsum('gkr,grc->gkc', eigen_basis, scaled, preferred_element_type=f32)]
    unnamed x23 -> x16, local copies, waits for them, and re-layouts: 10.6 us -> 6.19 us
  transfers between devices with their start and end apart: 17 -> 18, of which waited for: 14 -> 11; matrix products, arithmetic and copies ran while one was open for 10% -> 6% of each run, Pallas kernels for 2% -> 3%
where the time goes in v2:
time: 208 us; the launch traced here: 207 us
  waiting for transfers between devices  101 us (49%)
  starting transfers between devices  57.5 us (28%)
  Pallas kernels  19.1 us (9%)
  other arithmetic  18.7 us (9%)
  local copies, waits for them, and re-layouts  8.18 us (4%)
  between operations  2.81 us (1%)
    all_to_all x6, waiting for transfers between devices, exchange(): return lax.all_to_all(x, axis, split_axis=0, concat_axis=0, tiled=True)  52.9 us
    all_to_all x6, starting transfers between devices, exchange(): return lax.all_to_all(x, axis, split_axis=0, concat_axis=0, tiled=True)  38 us
    pallas_call x7, Pallas kernels, call(): pl.pallas_call(kernel, out_shape=tuple(outs), in_specs=[SMEM] * scalars +...  19.1 us
    ppermute x3, waiting for transfers between devices, around_z(): ahead = lax.ppermute((chunk(k) + ahead.astype(f32)).astype(bf16), 'z', up)  17.4 us
    ppermute x1, waiting for transfers between devices, shards(): near = lax.ppermute(near, 'xl', [(0, 1), (1, 0)])  13.2 us
    ppermute x3, waiting for transfers between devices, around_z(): back = lax.ppermute((chunk(-k) + back.astype(f32)).astype(bf16), 'z', down)  7.73 us
    unnamed x16, local copies, waits for them, and re-layouts  6.19 us
    ppermute x3, starting transfers between devices, around_z(): back = lax.ppermute((chunk(-k) + back.astype(f32)).astype(bf16), 'z', down)  6 us
  transfers between devices with their start and end apart: 18, of which 11 were waited for; matrix products, arithmetic and copies ran while one was open for 6% of the time, Pallas kernels for 3%

profile of v2, /device:TPU:32, one launch (start us, length us, event | category | flops | bytes accessed | tf_op | source)
XLA Modules:
  0.0 207.1 jit_solution(23182142644457671)
XLA Ops:
  0.7 9.3 %shard_map.87 = (bf16[128,3456]{1,0:T(8,128)(2,1)S(1)}, bf16[128,3456]{1,0:T(8,128)(2,1)S(1)}, f32[512,3584]{1,0:T(8,128)S(1)}) custom-call(s32[4]{0:T(128)S(1)} %pad_add_fusion.place, bf16[768,5120]{1,0:T(8,128)(2,1)} %bitcast.23), custom_call_target="tpu_custom_call" | custom-call | flops 4177526784 | bytes 16973840 | tf_op jit(solution)/shard_map/pallas_call | solution.py:87
  10.0 2.9 %copy-done.1 = f32[512,3584]{1,0:T(8,128)} copy-done((f32[512,3584]{1,0:T(8,128)}, f32[512,3584]{1,0:T(8,128)S(1)}, u32[]{:S(2)}) %copy-start.1) | copy-done | bytes 7340056
  13.0 0.7 fusion.3
  13.7 1.9 collective-permute-start.2
  15.6 5.5 %collective-permute-done.2 = bf16[32,3584]{1,0:T(8,128)(2,1)S(1)} collective-permute-done((bf16[32,3584]{1,0:T(8,128)(2,1)S(1)}, bf16[32,3584]{1,0:T(8,128)(2,1)S(1)}, u32[]{:S(2)}, u32[]{:S(2)}) %collective-permute-start.2) | collective-permute-done | bytes 229408 | tf_op jit(solution)/shard_map/ppermute | solution.py:140
  21.1 1.2 add_convert_fusion.6
  22.3 2.0 collective-permute-start.3
  24.3 12.4 %collective-permute-done.3 = bf16[64,3584]{1,0:T(8,128)(2,1)} collective-permute-done((bf16[64,3584]{1,0:T(8,128)(2,1)S(1)}, bf16[64,3584]{1,0:T(8,128)(2,1)}, u32[]{:S(2)}, u32[]{:S(2)}) %collective-permute-start.3) | collective-permute-done | bytes 458784 | tf_op jit(solution)/shard_map/ppermute | solution.py:145
  36.7 1.4 add_convert_fusion.5
  38.2 3.0 %collective-permute-start.6 = (bf16[32,3584]{1,0:T(8,128)(2,1)}, bf16[32,3584]{1,0:T(8,128)(2,1)}, u32[]{:S(2)}, u32[]{:S(2)}) collective-permute-start(bf16[32,3584]{1,0:T(8,128)(2,1)} %get-tuple-element.15), channel_id=1, source_target_pairs={{0,28},{4,0},{8,4},{12,8},{16,12},{20,16},{24,20},{28,24},{1,29},{... | collective-permute-start | bytes 688136 | tf_op jit(solution)/shard_map/ppermute | solution.py:141
  41.3 4.1 %collective-permute-done.6 = bf16[32,3584]{1,0:T(8,128)(2,1)} collective-permute-done((bf16[32,3584]{1,0:T(8,128)(2,1)}, bf16[32,3584]{1,0:T(8,128)(2,1)}, u32[]{:S(2)}, u32[]{:S(2)}) %collective-permute-start.6) | collective-permute-done | bytes 229408 | tf_op jit(solution)/shard_map/ppermute | solution.py:141
  45.3 5.0 %collective-permute-done.4 = bf16[64,3584]{1,0:T(8,128)(2,1)} collective-permute-done((bf16[64,3584]{1,0:T(8,128)(2,1)S(1)}, bf16[64,3584]{1,0:T(8,128)(2,1)}, u32[]{:S(2)}, u32[]{:S(2)}) %collective-permute-start.4) | collective-permute-done | bytes 458784 | tf_op jit(solution)/shard_map/ppermute | solution.py:145
  50.4 2.5 %add_convert_fusion.4 = (bf16[64,3584]{1,0:T(8,128)(2,1)S(1)}, bf16[64,3584]{1,0:T(8,128)(2,1)}) fusion(bf16[64,3584]{1,0:T(8,128)(2,1)} %collective-permute-done.4, f32[512,3584]{1,0:T(8,128)} %copy-done.1, s32[]{:T(128)S(6)} %select_n.38, bf16[32,3584]{1,0:T(8,128)(2,1)} %collective-permute-done.6, s32[]{:T(128)S(6)} %select_n.44), kind=kLoop, calls=%fused_computation.5 | loop fusion | flops 1376256 | bytes 3440648 | tf_op jit(solution)/shard_map/convert_element_type | solution.py:145
  52.9 2.9 %collective-permute-start.7 = (bf16[64,3584]{1,0:T(8,128)(2,1)}, bf16[64,3584]{1,0:T(8,128)(2,1)}, u32[]{:S(2)}, u32[]{:S(2)}) collective-permute-start(bf16[64,3584]{1,0:T(8,128)(2,1)} %get-tuple-element.13), channel_id=1, source_target_pairs={{0,28},{4,0},{8,4},{12,8},{16,12},{20,16},{24,20},{28,24},{1,29},{... | collective-permute-start | bytes 1376264 | tf_op jit(solution)/shard_map/ppermute | solution.py:146
  55.8 7.7 %collective-permute-done.7 = bf16[64,3584]{1,0:T(8,128)(2,1)} collective-permute-done((bf16[64,3584]{1,0:T(8,128)(2,1)}, bf16[64,3584]{1,0:T(8,128)(2,1)}, u32[]{:S(2)}, u32[]{:S(2)}) %collective-permute-start.7) | collective-permute-done | bytes 458784 | tf_op jit(solution)/shard_map/ppermute | solution.py:146
  63.6 2.2 %add_convert_fusion.2 = bf16[64,3584]{1,0:T(8,128)(2,1)} fusion(bf16[64,3584]{1,0:T(8,128)(2,1)} %collective-permute-done.7, f32[512,3584]{1,0:T(8,128)} %copy-done.1, s32[]{:T(128)S(6)} %select_n.43), kind=kLoop, calls=%fused_computation.3 | loop fusion | flops 688128 | bytes 1835012 | tf_op jit(solution)/shard_map/convert_element_type | solution.py:146
  65.7 2.5 %collective-permute-start.8 = (bf16[64,3584]{1,0:T(8,128)(2,1)}, bf16[64,3584]{1,0:T(8,128)(2,1)}, u32[]{:S(2)}, u32[]{:S(2)}) collective-permute-start(bf16[64,3584]{1,0:T(8,128)(2,1)} %add_convert_fusion.2), channel_id=1, source_target_pairs={{0,28},{4,0},{8,4},{12,8},{16,12},{20,16},{24,20},{28,24},{1,29},{... | collective-permute-start | bytes 1376264 | tf_op jit(solution)/shard_map/ppermute | solution.py:146
  68.2 1.6 shard_map.88
  69.8 10.2 %all-to-all-start.3 = ((bf16[64,8,896]{2,1,0:T(8,128)(2,1)}), bf16[64,8,896]{2,1,0:T(8,128)(2,1)S(1)}, u32[]{:S(2)}, u32[]{:S(2)}) async-start(bf16[64,8,896]{2,1,0:T(8,128)(2,1)} %bitcast.12), calls=%async_computation.3 | async-start | bytes 1835008 | tf_op jit(solution)/shard_map/all_to_all | solution.py:261
  80.1 1.7 collective-permute-start
  81.8 1.9 collective-permute-start.1
  83.7 3.2 %copy-done = bf16[2,384,5120]{2,1,0:T(8,128)(2,1)S(1)} copy-done((bf16[2,384,5120]{2,1,0:T(8,128)(2,1)S(1)}, bf16[2,384,5120]{2,1,0:T(8,128)(2,1)}, u32[]{:S(2)}) %copy-start) | copy-done | bytes 7864344
  86.9 2.5 %shard_map.86 = f32[256,3456]{1,0:T(8,128)S(1)} custom-call(s32[4]{0:T(128)S(1)} %pad_add_fusion.place, bf16[768,5120]{1,0:T(8,128)(2,1)S(1)} %bitcast.24), custom_call_target="tpu_custom_call" | custom-call | flops 1358954496 | bytes 11403280 | tf_op jit(solution)/shard_map/pallas_call | solution.py:87
  89.4 1.5 collective-permute-start.5
  90.9 2.2 %add_convert_fusion.1 = bf16[64,3584]{1,0:T(8,128)(2,1)} fusion(bf16[64,3584]{1,0:T(8,128)(2,1)} %collective-permute-done.8, f32[512,3584]{1,0:T(8,128)} %copy-done.1, s32[]{:T(128)S(6)} %select_n.42), kind=kLoop, calls=%fused_computation.2 | loop fusion | flops 688128 | bytes 1835012 | tf_op jit(solution)/shard_map/convert_element_type | solution.py:146
  93.6 13.2 %collective-permute-done = bf16[128,3456]{1,0:T(8,128)(2,1)} collective-permute-done((bf16[128,3456]{1,0:T(8,128)(2,1)S(1)}, bf16[128,3456]{1,0:T(8,128)(2,1)}, u32[]{:S(2)}, u32[]{:S(2)}) %collective-permute-start) | collective-permute-done | bytes 884768 | tf_op jit(solution)/shard_map/ppermute | solution.py:283
  106.9 3.0 %add_convert_fusion = bf16[256,3456]{1,0:T(8,128)(2,1)} fusion(f32[256,3456]{1,0:T(8,128)S(1)} %shard_map.86, bf16[128,3456]{1,0:T(8,128)(2,1)} %collective-permute-done.1, bf16[128,3456]{1,0:T(8,128)(2,1)} %collective-permute-done), kind=kLoop, calls=%fused_computation | loop fusion | flops 5308416 | bytes 7077888 | tf_op jit(solution)/shard_map/convert_element_type | solution.py:304
  109.9 4.5 %all-to-all-start = ((bf16[4,64,3456]{2,1,0:T(8,128)(2,1)}), bf16[4,64,3456]{2,1,0:T(8,128)(2,1)}, u32[]{:S(2)}, u32[]{:S(2)}) async-start(bf16[4,64,3456]{2,1,0:T(8,128)(2,1)} %bitcast.5), calls=%async_computation | async-start | bytes 3538944 | tf_op jit(solution)/shard_map/all_to_all | solution.py:261
  114.4 1.6 convert_add_fusion
  116.1 1.2 collective-permute-start.10
  117.5 1.4 shard_map.89
  118.9 15.5 %all-to-all-done = bf16[4,64,3456]{2,1,0:T(8,128)(2,1)} async-done(((bf16[4,64,3456]{2,1,0:T(8,128)(2,1)}), bf16[4,64,3456]{2,1,0:T(8,128)(2,1)}, u32[]{:S(2)}, u32[]{:S(2)}) %all-to-all-start) | async-done | bytes 1769504 | tf_op jit(solution)/shard_map/all_to_all | solution.py:261
  134.4 9.6 %all-to-all-start.4 = ((bf16[64,8,384]{2,1,0:T(8,128)(2,1)}), bf16[64,8,384]{2,1,0:T(8,128)(2,1)S(1)}, u32[]{:S(2)}, u32[]{:S(2)}) async-start(bf16[64,8,384]{2,1,0:T(8,128)(2,1)} %bitcast.14), calls=%async_computation.4 | async-start | bytes 786432 | tf_op jit(solution)/shard_map/all_to_all | solution.py:261
  144.0 0.7 fusion
  144.7 12.3 %all-to-all-done.4 = bf16[64,8,384]{2,1,0:T(8,128)(2,1)S(1)} async-done(((bf16[64,8,384]{2,1,0:T(8,128)(2,1)}), bf16[64,8,384]{2,1,0:T(8,128)(2,1)S(1)}, u32[]{:S(2)}, u32[]{:S(2)}) %all-to-all-start.4) | async-done | bytes 393248 | tf_op jit(solution)/shard_map/all_to_all | solution.py:261
  157.0 3.4 %all-to-all-start.2 = ((bf16[4,8,3584]{2,1,0:T(8,128)(2,1)}), bf16[4,8,3584]{2,1,0:T(8,128)(2,1)S(1)}, u32[]{:S(2)}, u32[]{:S(2)}) async-start(bf16[4,8,3584]{2,1,0:T(8,128)(2,1)} %fusion), calls=%async_computation.2 | async-start | bytes 458752 | tf_op jit(solution)/shard_map/all_to_all | solution.py:261
  160.4 2.6 %reduce_sum.31 = bf16[64,3456]{1,0:T(8,128)(2,1)} reduce(bf16[4,64,3456]{2,1,0:T(8,128)(2,1)} %all-to-all-done, bf16[]{:T(256)} %constant.66.clone.1), dimensions={0}, to_apply=%region_2.0 | reduce | flops 663552 | bytes 2211842 | tf_op jit(solution)/shard_map/reduce_sum | solution.py:305
  163.0 3.8 %all-to-all-done.2 = bf16[4,8,3584]{2,1,0:T(8,128)(2,1)S(1)} async-done(((bf16[4,8,3584]{2,1,0:T(8,128)(2,1)}), bf16[4,8,3584]{2,1,0:T(8,128)(2,1)S(1)}, u32[]{:S(2)}, u32[]{:S(2)}) %all-to-all-start.2) | async-done | bytes 229408 | tf_op jit(solution)/shard_map/all_to_all | solution.py:261
  166.9 4.2 %all-to-all-start.1 = ((bf16[8,8,3456]{2,1,0:T(8,128)(2,1)}), bf16[8,8,3456]{2,1,0:T(8,128)(2,1)S(1)}, u32[]{:S(2)}, u32[]{:S(2)}) async-start(bf16[8,8,3456]{2,1,0:T(8,128)(2,1)} %bitcast.6), calls=%async_computation.1 | async-start | bytes 884736 | tf_op jit(solution)/shard_map/all_to_all | solution.py:261
  171.2 0.6 dynamic_slice.47
  173.7 0.6 dynamic_slice.48
  174.3 0.7 pad_add_fusion.1.place
  175.2 1.3 shard_map.90.rotated
  176.6 4.9 %all-to-all-done.1 = bf16[8,8,3456]{2,1,0:T(8,128)(2,1)S(1)} async-done(((bf16[8,8,3456]{2,1,0:T(8,128)(2,1)}), bf16[8,8,3456]{2,1,0:T(8,128)(2,1)S(1)}, u32[]{:S(2)}, u32[]{:S(2)}) %all-to-all-start.1) | async-done | bytes 442400 | tf_op jit(solution)/shard_map/all_to_all | solution.py:261
  181.4 1.6 shard_map.91
  183.0 6.1 %all-to-all-start.5 = ((bf16[64,8,512]{2,1,0:T(8,128)(2,1)}), bf16[64,8,512]{2,1,0:T(8,128)(2,1)S(1)}, u32[]{:S(2)}, u32[]{:S(2)}) async-start(bf16[64,8,512]{2,1,0:T(8,128)(2,1)} %bitcast.16), calls=%async_computation.5 | async-start | bytes 1048576 | tf_op jit(solution)/shard_map/all_to_all | solution.py:261
  189.2 16.4 %all-to-all-done.5 = bf16[64,8,512]{2,1,0:T(8,128)(2,1)S(1)} async-done(((bf16[64,8,512]{2,1,0:T(8,128)(2,1)}), bf16[64,8,512]{2,1,0:T(8,128)(2,1)S(1)}, u32[]{:S(2)}, u32[]{:S(2)}) %all-to-all-start.5) | async-done | bytes 524320 | tf_op jit(solution)/shard_map/all_to_all | solution.py:261
  205.7 1.5 shard_map.92
  (34 shorter events, 1.5 us)
Async XLA Ops:
  10.0 2.9 %copy-start.1 = (f32[512,3584]{1,0:T(8,128)}, f32[512,3584]{1,0:T(8,128)S(1)}, u32[]{:S(2)}) copy-start(f32[512,3584]{1,0:T(8,128)S(1)} %get-tuple-element.9) | copy-start | bytes 22020100
  13.7 7.4 %collective-permute-start.2 = (bf16[32,3584]{1,0:T(8,128)(2,1)S(1)}, bf16[32,3584]{1,0:T(8,128)(2,1)S(1)}, u32[]{:S(2)}, u32[]{:S(2)}) collective-permute-start(bf16[32,3584]{1,0:T(8,128)(2,1)S(1)} %get-tuple-element.14), channel_id=1, source_target_pairs={{0,4},{4,8},{8,12},{12,16},{16,20},{20,24},{24,28},{28,0},{1,5},{5... | collective-permute-start | bytes 688136 | tf_op jit(solution)/shard_map/ppermute | solution.py:140
  22.3 14.4 %collective-permute-start.3 = (bf16[64,3584]{1,0:T(8,128)(2,1)S(1)}, bf16[64,3584]{1,0:T(8,128)(2,1)}, u32[]{:S(2)}, u32[]{:S(2)}) collective-permute-start(bf16[64,3584]{1,0:T(8,128)(2,1)S(1)} %add_convert_fusion.6), channel_id=1, source_target_pairs={{0,4},{4,8},{8,12},{12,16},{16,20},{20,24},{24,28},{28,0},{1,5},{5... | collective-permute-start | bytes 1376264 | tf_op jit(solution)/shard_map/ppermute | solution.py:145
  24.3 43.9 %copy-start.2 = (bf16[2,512,512]{2,1,0:T(8,128)(2,1)S(1)}, bf16[2,512,512]{2,1,0:T(8,128)(2,1)}, u32[]{:S(2)}) copy-start(bf16[2,512,512]{2,1,0:T(8,128)(2,1)} %basis.1) | copy-start | bytes 3145732
  24.3 43.9 %copy-start.3 = (bf16[10,8,1024]{2,1,0:T(8,128)(2,1)S(1)}, bf16[10,8,1024]{2,1,0:T(8,128)(2,1)}, u32[]{:S(2)}) copy-start(bf16[10,8,1024]{2,1,0:T(8,128)(2,1)} %param.9) | copy-start | bytes 491524
  24.3 43.9 %copy-start.4 = (f32[2,512]{1,0:T(2,128)S(1)}, f32[2,512]{1,0:T(2,128)}, u32[]{:S(2)}) copy-start(f32[2,512]{1,0:T(2,128)} %values.1) | copy-start | bytes 12292
  38.1 12.2 %collective-permute-start.4 = (bf16[64,3584]{1,0:T(8,128)(2,1)S(1)}, bf16[64,3584]{1,0:T(8,128)(2,1)}, u32[]{:S(2)}, u32[]{:S(2)}) collective-permute-start(bf16[64,3584]{1,0:T(8,128)(2,1)S(1)} %add_convert_fusion.5), channel_id=1, source_target_pairs={{0,4},{4,8},{8,12},{12,16},{16,20},{20,24},{24,28},{28,0},{1,5},{5... | collective-permute-start | bytes 1376264 | tf_op jit(solution)/shard_map/ppermute | solution.py:145
  38.2 7.1 %collective-permute-start.6 = (bf16[32,3584]{1,0:T(8,128)(2,1)}, bf16[32,3584]{1,0:T(8,128)(2,1)}, u32[]{:S(2)}, u32[]{:S(2)}) collective-permute-start(bf16[32,3584]{1,0:T(8,128)(2,1)} %get-tuple-element.15), channel_id=1, source_target_pairs={{0,28},{4,0},{8,4},{12,8},{16,12},{20,16},{24,20},{28,24},{1,29},{... | collective-permute-start | bytes 688136 | tf_op jit(solution)/shard_map/ppermute | solution.py:141
  52.9 10.7 %collective-permute-start.7 = (bf16[64,3584]{1,0:T(8,128)(2,1)}, bf16[64,3584]{1,0:T(8,128)(2,1)}, u32[]{:S(2)}, u32[]{:S(2)}) collective-permute-start(bf16[64,3584]{1,0:T(8,128)(2,1)} %get-tuple-element.13), channel_id=1, source_target_pairs={{0,28},{4,0},{8,4},{12,8},{16,12},{20,16},{24,20},{28,24},{1,29},{... | collective-permute-start | bytes 1376264 | tf_op jit(solution)/shard_map/ppermute | solution.py:146
  65.7 25.2 %collective-permute-start.8 = (bf16[64,3584]{1,0:T(8,128)(2,1)}, bf16[64,3584]{1,0:T(8,128)(2,1)}, u32[]{:S(2)}, u32[]{:S(2)}) collective-permute-start(bf16[64,3584]{1,0:T(8,128)(2,1)} %add_convert_fusion.2), channel_id=1, source_target_pairs={{0,28},{4,0},{8,4},{12,8},{16,12},{20,16},{24,20},{28,24},{1,29},{... | collective-permute-start | bytes 1376264 | tf_op jit(solution)/shard_map/ppermute | solution.py:146
  69.8 40.1 %all-to-all-start.3 = ((bf16[64,8,896]{2,1,0:T(8,128)(2,1)}), bf16[64,8,896]{2,1,0:T(8,128)(2,1)S(1)}, u32[]{:S(2)}, u32[]{:S(2)}) async-start(bf16[64,8,896]{2,1,0:T(8,128)(2,1)} %bitcast.12), calls=%async_computation.3 | async-start | bytes 1835008 | tf_op jit(solution)/shard_map/all_to_all | solution.py:261
  80.1 26.8 %collective-permute-start = (bf16[128,3456]{1,0:T(8,128)(2,1)S(1)}, bf16[128,3456]{1,0:T(8,128)(2,1)}, u32[]{:S(2)}, u32[]{:S(2)}) collective-permute-start(bf16[128,3456]{1,0:T(8,128)(2,1)S(1)} %get-tuple-element.7), channel_id=1, source_target_pairs={{0,32},{32,0},{1,33},{33,1},{2,34},{34,2},{3,35},{35,3},{4,36},{36... | collective-permute-start | bytes 2654216 | tf_op jit(solution)/shard_map/ppermute | solution.py:283
  81.8 25.1 %collective-permute-start.1 = (bf16[128,3456]{1,0:T(8,128)(2,1)S(1)}, bf16[128,3456]{1,0:T(8,128)(2,1)}, u32[]{:S(2)}, u32[]{:S(2)}) collective-permute-start(bf16[128,3456]{1,0:T(8,128)(2,1)S(1)} %get-tuple-element.8), channel_id=1, source_target_pairs={{0,34},{2,32},{32,2},{34,0},{1,35},{3,33},{33,3},{35,1},{4,38},{6,... | collective-permute-start | bytes 2654216 | tf_op jit(solution)/shard_map/ppermute | solution.py:284
  83.7 3.2 %copy-start = (bf16[2,384,5120]{2,1,0:T(8,128)(2,1)S(1)}, bf16[2,384,5120]{2,1,0:T(8,128)(2,1)}, u32[]{:S(2)}) copy-start(bf16[2,384,5120]{2,1,0:T(8,128)(2,1)} %param.7) | copy-start | bytes 23592964
  89.4 25.0 %collective-permute-start.5 = (bf16[64,3584]{1,0:T(8,128)(2,1)S(1)}, bf16[64,3584]{1,0:T(8,128)(2,1)}, u32[]{:S(2)}, u32[]{:S(2)}) collective-permute-start(bf16[64,3584]{1,0:T(8,128)(2,1)S(1)} %get-tuple-element.12), channel_id=1, source_target_pairs={{0,4},{4,8},{8,12},{12,16},{16,20},{20,24},{24,28},{28,0},{1,5},{5... | collective-permute-start | bytes 1376264 | tf_op jit(solution)/shard_map/ppermute | solution.py:145
  93.1 21.3 %collective-permute-start.9 = (bf16[64,3584]{1,0:T(8,128)(2,1)}, bf16[64,3584]{1,0:T(8,128)(2,1)}, u32[]{:S(2)}, u32[]{:S(2)}) collective-permute-start(bf16[64,3584]{1,0:T(8,128)(2,1)} %add_convert_fusion.1), channel_id=1, source_target_pairs={{0,28},{4,0},{8,4},{12,8},{16,12},{20,16},{24,20},{28,24},{1,29},{... | collective-permute-start | bytes 1376264 | tf_op jit(solution)/shard_map/ppermute | solution.py:146
  109.9 7.4 %copy-start.6 = (s32[10]{0:T(128)S(1)}, s32[10]{0:T(128)}, u32[]{:S(2)}) copy-start(s32[10]{0:T(128)} %owner.2) | copy-start | bytes 124
  109.9 24.5 %all-to-all-start = ((bf16[4,64,3456]{2,1,0:T(8,128)(2,1)}), bf16[4,64,3456]{2,1,0:T(8,128)(2,1)}, u32[]{:S(2)}, u32[]{:S(2)}) async-start(bf16[4,64,3456]{2,1,0:T(8,128)(2,1)} %bitcast.5), calls=%async_computation | async-start | bytes 3538944 | tf_op jit(solution)/shard_map/all_to_all | solution.py:261
  116.1 27.9 %collective-permute-start.10 = (bf16[32,3584]{1,0:T(8,128)(2,1)S(1)}, bf16[32,3584]{1,0:T(8,128)(2,1)S(1)}, u32[]{:S(2)}, u32[]{:S(2)}) collective-permute-start(bf16[32,3584]{1,0:T(8,128)(2,1)S(1)} %dynamic-slice_convert_fusion.1), channel_id=1, source_target_pairs={{0,32},{32,0},{1,33},{33,1},{2,34},{34,2},{3,35},{35,3},{4,36},{36... | collective-permute-start | bytes 688136 | tf_op jit(solution)/shard_map/ppermute | solution.py:300
  117.5 53.7 %copy-start.7 = (s32[64]{0:T(128)S(1)}, s32[64]{0:T(128)}, u32[]{:S(2)}) copy-start(s32[64]{0:T(128)} %constant.77.clone) | copy-start | bytes 772
  117.5 57.5 %copy-start.5 = (s32[55]{0:T(128)S(1)}, s32[55]{0:T(128)}, u32[]{:S(2)}) copy-start(s32[55]{0:T(128)} %owner.3) | copy-start | bytes 664
  134.4 22.6 %all-to-all-start.4 = ((bf16[64,8,384]{2,1,0:T(8,128)(2,1)}), bf16[64,8,384]{2,1,0:T(8,128)(2,1)S(1)}, u32[]{:S(2)}, u32[]{:S(2)}) async-start(bf16[64,8,384]{2,1,0:T(8,128)(2,1)} %bitcast.14), calls=%async_computation.4 | async-start | bytes 786432 | tf_op jit(solution)/shard_map/all_to_all | solution.py:261
  157.0 9.9 %all-to-all-start.2 = ((bf16[4,8,3584]{2,1,0:T(8,128)(2,1)}), bf16[4,8,3584]{2,1,0:T(8,128)(2,1)S(1)}, u32[]{:S(2)}, u32[]{:S(2)}) async-start(bf16[4,8,3584]{2,1,0:T(8,128)(2,1)} %fusion), calls=%async_computation.2 | async-start | bytes 458752 | tf_op jit(solution)/shard_map/all_to_all | solution.py:261
  166.9 14.6 %all-to-all-start.1 = ((bf16[8,8,3456]{2,1,0:T(8,128)(2,1)}), bf16[8,8,3456]{2,1,0:T(8,128)(2,1)S(1)}, u32[]{:S(2)}, u32[]{:S(2)}) async-start(bf16[8,8,3456]{2,1,0:T(8,128)(2,1)} %bitcast.6), calls=%async_computation.1 | async-start | bytes 884736 | tf_op jit(solution)/shard_map/all_to_all | solution.py:261
  171.1 4.1 %collective-permute-start.11 = (bf16[512,256]{1,0:T(8,128)(2,1)S(1)}, bf16[512,256]{1,0:T(8,128)(2,1)S(1)}, u32[]{:S(2)}, u32[]{:S(2)}) collective-permute-start(bf16[512,256]{1,0:T(8,128)(2,1)S(1)} %slice.16), channel_id=1, source_target_pairs={{0,1},{1,0},{2,3},{3,2},{4,5},{5,4},{6,7},{7,6},{8,9},{9,8},{10,11... | collective-permute-start | bytes 786440 | tf_op jit(solution)/shard_map/ppermute | solution.py:289
  183.0 22.7 %all-to-all-start.5 = ((bf16[64,8,512]{2,1,0:T(8,128)(2,1)}), bf16[64,8,512]{2,1,0:T(8,128)(2,1)S(1)}, u32[]{:S(2)}, u32[]{:S(2)}) async-start(bf16[64,8,512]{2,1,0:T(8,128)(2,1)} %bitcast.16), calls=%async_computation.5 | async-start | bytes 1048576 | tf_op jit(solution)/shard_map/all_to_all | solution.py:261

commit v3 on v2

v3 whole, which is shorter than its diff:
```python
import functools

import jax
import jax.numpy as jnp
import numpy as np
from jax import lax
from jax.experimental import pallas as pl
from jax.experimental.pallas import tpu as pltpu
from jax.sharding import Mesh, PartitionSpec as P

TILE = 512
NT = 10
UT = NT * (NT + 1) // 2
SLOTS = 2
SLAB = 128
COLS = 256
DP = ("y", "xl", "z")
X_FIRST = (0, 1, 2, 5, 6)
Y_FIRST = tuple(i for i in range(NT) if i not in X_FIRST)
PAIRS = [(i, j) for i in range(NT) for j in range(i, NT)]
ORDER = [u for rows in (X_FIRST, Y_FIRST) for u, (i, _) in enumerate(PAIRS) if i in rows]
X_TILES = sum(NT - i for i in X_FIRST)
Y_TILES = UT - X_TILES

damping = 0.1
bf16 = jnp.bfloat16
f32 = jnp.float32


def slot_rank(owner_ids):
    entries = owner_ids.shape[0]
    position = jnp.arange(entries)
    same_owner = owner_ids[:, None] == owner_ids[None, :]
    earlier = position[None, :] < position[:, None]
    return jnp.sum(jnp.logical_and(same_owner, earlier), axis=1)


def dot(a, b):
    return lax.dot_general(a, b, (((1,), (0,)), ((), ())), preferred_element_type=f32)


def fill(slab, act, which, begin):
    for j in range(begin, NT):
        at = pl.multiple_of(j * TILE + which * SLAB, SLAB)
        slab[:, j * SLAB : (j + 1) * SLAB] = act[:, pl.ds(at, SLAB)]


def spans(i):
    return [(at, min(at + 256, NT * SLAB)) for at in range(i * SLAB, NT * SLAB, 256)]


def turn(act, i, y, turned, half=None):
    part = turned.shape[0] // 4
    for k in range(4):
        at = pl.multiple_of(i * TILE + lax.rem(y + k, 4) * SLAB, SLAB)
        chunk = act[:, pl.ds(at, SLAB)].T
        if half is not None:
            chunk = jnp.where(half == 0, chunk[:part], chunk[part:])
        turned[k * part : (k + 1) * part, :] = chunk


def sent_kernel(place, act, near, far, slab, other, turned):
    low, mine, theirs, y = place[0], place[1], place[2], place[3]
    fill(slab, act, mine, 0)
    fill(other, act, theirs, 0)
    start = 0
    for i in X_FIRST:
        turn(act, i, y, turned, 1 - low)
        for begin, end in spans(i):
            to = slice(start, start + end - begin)
            near[:, to] = dot(turned[0:128, :], slab[:, begin:end]).astype(bf16)
            far[:, to] = dot(turned[128:256, :], other[:, begin:end]).astype(bf16)
            start += end - begin


def kept_kernel(place, act, own0, own1, own2, own3, slab, turned):
    low, mine, y = place[0], place[1], place[3]
    fill(slab, act, mine, 0)
    start = 0
    for i in X_FIRST:
        turn(act, i, y, turned, low)
        for begin, end in spans(i):
            product = dot(turned[...], slab[:, begin:end])
            for k, own in enumerate((own0, own1, own2, own3)):
                own[:, start : start + end - begin] = product[k * 64 : k * 64 + 64]
            start += end - begin


def along_kernel(place, act, own0, own1, up, down, own3, slab, turned):
    mine, y = place[1], place[3]
    fill(slab, act, mine, min(Y_FIRST))
    start = 0
    for i in Y_FIRST:
        turn(act, i, y, turned)
        for begin, end in spans(i):
            to = slice(start, start + end - begin)
            product = dot(turned[...], slab[:, begin:end])
            own0[:, to] = product[0:128]
            own1[:, to] = product[128:256]
            up[:, to] = product[256:320].astype(bf16)
            down[:, to] = product[320:384].astype(bf16)
            own3[:, to] = product[384:512]
            start += end - begin


VMEM = pl.BlockSpec(memory_space=pltpu.VMEM)
SMEM = pl.BlockSpec(memory_space=pltpu.SMEM)


def call(kernel, outs, scratch, flops, *operands, scalars=1):
    moved = sum(x.size * x.dtype.itemsize for x in operands)
    moved += sum(x.size * x.dtype.itemsize for x in outs)
    return pl.pallas_call(
        kernel,
        out_shape=tuple(outs),
        in_specs=[SMEM] * scalars + [VMEM] * (len(operands) - scalars),
        out_specs=(VMEM,) * len(outs),
        scratch_shapes=[pltpu.VMEM(shape, dtype) for shape, dtype in scratch],
        compiler_params=pltpu.CompilerParams(vmem_limit_bytes=40 * 2**20),
        cost_estimate=pl.CostEstimate(flops=flops, bytes_accessed=moved, transcendentals=0),
    )(*operands)


def array(shape, dtype):
    return jax.ShapeDtypeStruct(shape, dtype)


def products(act, place):
    tokens = act.shape[0]
    wide, rest = X_TILES * SLAB, Y_TILES * SLAB
    slab = ((tokens, NT * SLAB), bf16)
    half = ((256, tokens), bf16)
    full = ((TILE, tokens), bf16)
    sent = call(
        sent_kernel, [array((128, wide), bf16)] * 2, [slab, slab, half], 2 * tokens * 256 * wide, place, act
    )
    along = call(
        along_kernel,
        [array((128, rest), f32)] * 2 + [array((64, rest), bf16)] * 2 + [array((128, rest), f32)],
        [slab, full],
        2 * tokens * TILE * rest,
        place,
        act,
    )
    kept = call(kept_kernel, [array((64, wide), f32)] * 4, [slab, half], 2 * tokens * 256 * wide, place, act)
    return sent, along, kept


def ring(axis, step):
    n = lax.axis_size(axis)
    return [(i, (i + step) % n) for i in range(n)]


def around_y(zero, one, up, down, three):
    up = lax.ppermute(up, "y", ring("y", 1))
    down = lax.ppermute(down, "y", ring("y", -1))
    none = jnp.zeros_like(up)
    up = one() + jnp.concatenate([up, none], axis=0).astype(f32)
    down = three() + jnp.concatenate([none, down], axis=0).astype(f32)
    up = lax.ppermute(up.astype(bf16), "y", ring("y", 1))
    down = lax.ppermute(down.astype(bf16), "y", ring("y", -1))
    return zero() + up.astype(f32) + down.astype(f32)


def block_units():
    places = [d for d in range(64) if (d // 8 + d % 8) % 8 < NT // 2]
    unit = [0] * 64
    for at, d in enumerate(places):
        unit[d] = at
    return unit, places


UNIT, PLACES = block_units()


def scatter_kernel(place, basis, values, grad, out):
    quarter = pl.ds(pl.multiple_of(place[1] * SLAB, SLAB), SLAB)
    out[:, 0:128] = basis[0, :, quarter]
    out[:, 128:256] = basis[1, :, quarter]
    full = grad[...].astype(f32)

    def piece(d):
        block, part = divmod(UNIT[d], 4)
        return full[block * 8 : block * 8 + 8, part * COLS : (part + 1) * COLS]

    for d in range(0, 64, 2):
        pair = jnp.concatenate([piece(d), piece(d + 1)], axis=0)
        out[d * 8 : d * 8 + 16, 256:512] = pair.astype(bf16)
    parts, left = [], values[...]
    for _ in range(3):
        part = left.astype(bf16).astype(f32)
        parts.append(part)
        left = left - part
    rows = jnp.concatenate([*parts, jnp.zeros((122, TILE), f32)], axis=0)
    out[:, 512:640] = rows.T.astype(bf16)


def forward_kernel(owner, slot, got, out):
    found = []
    for b in range(NT):
        at = pl.multiple_of(owner[b] // 2 * 16, 16)
        pair = got[pl.ds(at, 16), :].astype(f32)
        mine = jnp.where(owner[b] % 2 == 0, pair[0:8], pair[8:16])
        rows = jnp.where(slot[b] == 0, mine[:, 0:128], mine[:, 128:256])
        found.append(jnp.concatenate([rows, mine[:, 512:640]], axis=1))
    for d in range(0, 64, 2):
        pair = jnp.concatenate([found[UNIT[d] // 4], found[UNIT[d + 1] // 4]], axis=0)
        out[d * 8 : d * 8 + 16, :] = pair.astype(bf16)


def rotate_kernel(place, mine, one, two, three, got, out, basis):
    group, slot = place[0], place[1]
    for k, quarter in enumerate((mine, one, two, three)):
        at = pl.multiple_of(lax.bitwise_xor(group, k) * SLAB, SLAB)
        basis[:, pl.ds(at, SLAB)] = quarter[:, 0:128]
    parts = mine[:, 128:256].astype(f32)
    lane = lax.broadcasted_iota(jnp.int32, parts.shape, 1)
    ours = (lane < 6) & (lane % 2 == slot)
    values = jnp.sum(jnp.where(ours, parts, 0.0), axis=1, keepdims=True)
    turned = dot(basis[...].T, got[:, 256:512])
    scaled = (turned / (values + damping)).astype(bf16)
    out[...] = dot(basis[...], scaled).astype(bf16)


def pack_kernel(total, owner, slot, got, out, sums, slots):
    full = got[...].astype(f32)
    acc = full[0:8]
    for k in range(8, 64, 8):
        acc = acc + full[k : k + 8]
    sums[...] = acc / total
    slots[...] = jnp.zeros_like(slots)
    for at, u in enumerate(ORDER):
        row = pl.multiple_of(owner[u] * 8, 8)
        lane = pl.multiple_of(slot[u] * SLAB, SLAB)
        slots[pl.ds(row, 8), pl.ds(lane, SLAB)] = sums[:, at * SLAB : (at + 1) * SLAB]
    out[...] = slots[...].astype(bf16)


def unpack_kernel(got, returned, factor, result):
    for s in range(SLOTS):
        factor[s * TILE : (s + 1) * TILE, :] = got[:, s * SLAB : (s + 1) * SLAB].astype(f32)
    turned = returned[...].astype(f32)
    for b in range(0, NT, 2):
        for q in range(4):
            pair = [turned[PLACES[u] * 8 : PLACES[u] * 8 + 8] for u in (b * 4 + q, b * 4 + 4 + q)]
            result[b * 8 : b * 8 + 16, q * COLS : (q + 1) * COLS] = jnp.concatenate(pair, axis=0).astype(bf16)


def exchange(x, axis):
    return lax.all_to_all(x, axis, split_axis=0, concat_axis=0, tiled=True)


def shards(activations, tile_owner, gradient, block_owner, eigen_basis, eigen_values):
    micro, tokens, width = activations.shape
    blocks, rows, cols = gradient.shape
    dp_count = lax.axis_size(DP)
    act = activations.reshape(micro * tokens, width)
    me = lax.axis_index(DP)
    y, low = lax.axis_index("y"), lax.axis_index("xl")
    high, core = lax.axis_index("xh"), lax.axis_index("c")
    group = high * 2 + core
    place = jnp.stack([low, group, (1 - high) * 2 + core, y]).astype(jnp.int32)
    tile_rank = slot_rank(tile_owner).astype(jnp.int32)
    block_rank = slot_rank(block_owner).astype(jnp.int32)

    (near, far), (zero, one, up, down, three), own = products(act, place)
    near = lax.ppermute(near, "xl", [(0, 1), (1, 0)])
    far = lax.ppermute(far, ("xl", "xh"), [(i, 3 - i) for i in range(4)])

    [out] = call(
        scatter_kernel, [array((TILE, 640), bf16)], [], 0,
        place, eigen_basis, eigen_values, gradient.reshape(blocks * rows, cols),
    )
    got = exchange(out, DP)
    [out] = call(forward_kernel, [array((TILE, 256), bf16)], [], 0, block_owner, block_rank, got, scalars=2)
    mine = exchange(out, DP)
    quarter = mine[:, :SLAB]
    others = [lax.ppermute(quarter, ("xh", "c"), [(i, i ^ k) for i in range(4)]) for k in (1, 2, 3)]
    my_block = jnp.asarray(np.array(UNIT) // 4, jnp.int32)[me]
    [rotated] = call(
        rotate_kernel, [array((TILE, COLS), bf16)], [((TILE, TILE), bf16)], 4 * TILE * TILE * COLS,
        jnp.stack([group, block_rank[my_block]]).astype(jnp.int32), mine, *others, got,
    )
    returned = exchange(rotated, DP)

    along = around_y(lambda: zero, lambda: one, up, down, lambda: three)
    half = along.shape[0] // 2
    sent = lax.dynamic_slice_in_dim(along, (1 - low) * half, half, 0)
    kept = lax.dynamic_slice_in_dim(along, low * half, half, 0)
    along = kept + lax.ppermute(sent.astype(bf16), "xl", [(0, 1), (1, 0)]).astype(f32)

    opposite = (own[2] + far[:64].astype(f32)).astype(bf16)
    across = around_y(
        lambda: own[0] + near[:64].astype(f32),
        lambda: own[1] + near[64:].astype(f32),
        opposite[:32],
        opposite[32:],
        lambda: own[3] + far[64:].astype(f32),
    )
    sums = exchange(jnp.concatenate([across.astype(bf16), along.astype(bf16)], axis=1), "z")

    [out] = call(
        functools.partial(pack_kernel, micro * tokens * dp_count),
        [array((TILE, 256), bf16)], [((8, UT * SLAB), f32), ((TILE, 256), f32)], 0,
        tile_owner, tile_rank, sums, scalars=2,
    )
    final = exchange(out, DP)
    factor, result = call(
        unpack_kernel, [array((SLOTS * TILE, SLAB), f32), array((blocks * rows, cols), bf16)], [], 0,
        final, returned, scalars=0,
    )
    return factor.reshape(SLOTS, TILE, SLAB), result.reshape(blocks, rows, cols)


def solution(mesh):
    fine = Mesh(mesh.devices.reshape(4, 2, 8, 2, 2), ("y", "xl", "z", "xh", "c"))
    group = ("xh", "c")
    placed = (
        P(None, DP, None),
        P(),
        P(None, DP, group),
        P(),
        P(DP, None, None),
        P(DP, None),
    )
    return jax.shard_map(
        shards,
        mesh=fine,
        in_specs=placed,
        out_specs=(P(DP, None, group), P(None, DP, group)),
        check_vma=False,
    )
```

time: 208 us -> 169 us (0.81)
  waiting for transfers between devices: 101 us -> 53.7 us
  blocking collectives: 0 us -> 16.5 us
  other arithmetic: 18.7 us -> 12.5 us
    ppermute x9 -> x11, waiting for transfers between devices: 34.7 us -> 11.6 us  [the longest x2 10.8 us: around_y(): down = lax.ppermute(down, 'y', ring('y', -1))]
    all_to_all x6 -> x4, waiting for transfers between devices: 52.9 us -> 31 us  [exchange(): return lax.all_to_all(x, axis, split_axis=0, concat_axis=0, tiled=True)]
    all_to_all x0 -> x1, blocking collectives: none -> 16.5 us  [exchange(): return lax.all_to_all(x, axis, split_axis=0, concat_axis=0, tiled=True)]
    all_to_all x6 -> x4, starting transfers between devices: 38 us -> 32.4 us  [exchange(): return lax.all_to_all(x, axis, split_axis=0, concat_axis=0, tiled=True)]
    ppermute x1, waiting for transfers between devices: 13.2 us -> 8.24 us  [shards(): near = lax.ppermute(near, 'xl', [(0, 1), (1, 0)])]
    ppermute x9 -> x11, starting transfers between devices: 14.6 us -> 18.3 us  [the longest x2 7.28 us: around_y(): down = lax.ppermute(down.astype(bf16), 'y', ring('y', -1))]
    convert_element_type x7, other arithmetic: 12.5 us -> 8.85 us  [the longest x2 2.98 us: around_y(): up = lax.ppermute(up.astype(bf16), 'y', ring('y', 1))]
    reduce_sum x1 -> x0, other arithmetic: 2.62 us -> none  [shards(): first = jnp.sum(first.reshape(4, 64, -1).astype(f32), axis=0)]
  transfers between devices with their start and end apart: 18 -> 18, of which waited for: 11 -> 9; matrix products, arithmetic and copies ran while one was open for 6% -> 8% of each run, Pallas kernels for 3% -> 9%
where the time goes in v3:
time: 169 us; the launch traced here: 168 us
  starting transfers between devices  55.6 us (33%)
  waiting for transfers between devices  53.7 us (32%)
  Pallas kernels  19.1 us (11%)
  blocking collectives  16.5 us (10%)
  other arithmetic  12.5 us (7%)
  local copies, waits for them, and re-layouts  7.74 us (5%)
  between operations  2.76 us (2%)
    all_to_all x4, starting transfers between devices, exchange(): return lax.all_to_all(x, axis, split_axis=0, concat_axis=0, tiled=True)  32.4 us
    all_to_all x4, waiting for transfers between devices, exchange(): return lax.all_to_all(x, axis, split_axis=0, concat_axis=0, tiled=True)  31 us
    pallas_call x8, Pallas kernels, call(): pl.pallas_call(kernel, out_shape=tuple(outs), in_specs=[SMEM] * scalars +...  19.1 us
    all_to_all x1, blocking collectives, exchange(): return lax.all_to_all(x, axis, split_axis=0, concat_axis=0, tiled=True)  16.5 us
    ppermute x2, waiting for transfers between devices, around_y(): down = lax.ppermute(down, 'y', ring('y', -1))  10.8 us
    ppermute x1, waiting for transfers between devices, shards(): near = lax.ppermute(near, 'xl', [(0, 1), (1, 0)])  8.24 us
    ppermute x2, starting transfers between devices, around_y(): down = lax.ppermute(down.astype(bf16), 'y', ring('y', -1))  7.28 us
    unnamed x16, local copies, waits for them, and re-layouts  6.49 us
  transfers between devices with their start and end apart: 18, of which 9 were waited for; matrix products, arithmetic and copies ran while one was open for 8% of the time, Pallas kernels for 9%

profile of v3, /device:TPU:32, one launch (start us, length us, event | category | flops | bytes accessed | tf_op | source)
XLA Modules:
  0.0 167.8 jit_solution(5821572618388458787)
XLA Ops:
  0.7 3.2 %copy-done = bf16[2,384,5120]{2,1,0:T(8,128)(2,1)S(1)} copy-done((bf16[2,384,5120]{2,1,0:T(8,128)(2,1)S(1)}, bf16[2,384,5120]{2,1,0:T(8,128)(2,1)}, u32[]{:S(2)}) %copy-start) | copy-done | bytes 7864344
  4.0 3.4 %shard_map.88 = (f32[128,2432]{1,0:T(8,128)S(1)}, f32[128,2432]{1,0:T(8,128)S(1)}, bf16[64,2432]{1,0:T(8,128)(2,1)S(1)}, bf16[64,2432]{1,0:T(8,128)(2,1)S(1)}, f32[128,2432]{1,0:T(8,128)S(1)}) custom-call(s32[4]{0:T(128)S(1)} %pad_add_fusion.place, bf16[768,5120]{1,0:T(8,128)(2,1)S(1)} %bitcast.20), custom_call_target="tpu_custom_call" | custom-call | flops 1912602624 | bytes 12222480 | tf_op jit(solution)/shard_map/pallas_call | solution.py:113
  7.3 3.1 %collective-permute-start.8 = (bf16[64,2432]{1,0:T(8,128)(2,1)S(1)}, bf16[64,2432]{1,0:T(8,128)(2,1)S(1)}, u32[]{:S(2)}, u32[]{:S(2)}) collective-permute-start(bf16[64,2432]{1,0:T(8,128)(2,1)S(1)} %get-tuple-element.25), channel_id=1, source_target_pairs={{0,192},{64,0},{128,64},{192,128},{1,193},{65,1},{129,65},{193,129... | collective-permute-start | bytes 933896 | tf_op jit(solution)/shard_map/ppermute | solution.py:156
  10.4 6.6 %collective-permute-done.8 = bf16[64,2432]{1,0:T(8,128)(2,1)S(1)} collective-permute-done((bf16[64,2432]{1,0:T(8,128)(2,1)S(1)}, bf16[64,2432]{1,0:T(8,128)(2,1)S(1)}, u32[]{:S(2)}, u32[]{:S(2)}) %collective-permute-start.8) | collective-permute-done | bytes 311328 | tf_op jit(solution)/shard_map/ppermute | solution.py:156
  17.0 0.9 add_convert_fusion
  18.0 3.7 %collective-permute-start.9 = (bf16[128,2432]{1,0:T(8,128)(2,1)}, bf16[128,2432]{1,0:T(8,128)(2,1)}, u32[]{:S(2)}, u32[]{:S(2)}) collective-permute-start(bf16[128,2432]{1,0:T(8,128)(2,1)} %add_convert_fusion), channel_id=1, source_target_pairs={{0,192},{64,0},{128,64},{192,128},{1,193},{65,1},{129,65},{193,129... | collective-permute-start | bytes 1867784 | tf_op jit(solution)/shard_map/ppermute | solution.py:161
  21.7 0.9 add_convert_fusion.1
  22.6 5.8 %shard_map.87 = (bf16[128,4608]{1,0:T(8,128)(2,1)}, bf16[128,4608]{1,0:T(8,128)(2,1)}) custom-call(s32[4]{0:T(128)S(1)} %pad_add_fusion.place, bf16[768,5120]{1,0:T(8,128)(2,1)S(1)} %bitcast.21), custom_call_target="tpu_custom_call" | custom-call | flops 1811939328 | bytes 10223632 | tf_op jit(solution)/shard_map/pallas_call | solution.py:113
  28.4 2.8 %collective-permute-start.1 = (bf16[128,4608]{1,0:T(8,128)(2,1)}, bf16[128,4608]{1,0:T(8,128)(2,1)}, u32[]{:S(2)}, u32[]{:S(2)}) collective-permute-start(bf16[128,4608]{1,0:T(8,128)(2,1)} %get-tuple-element.19), channel_id=1, source_target_pairs={{0,34},{2,32},{32,2},{34,0},{1,35},{3,33},{33,3},{35,1},{4,38},{6,... | collective-permute-start | bytes 3538952 | tf_op jit(solution)/shard_map/ppermute | solution.py:268
  31.2 1.6 shard_map.90
  32.7 11.8 %all-to-all-start.2 = ((bf16[64,8,640]{2,1,0:T(8,128)(2,1)}), bf16[64,8,640]{2,1,0:T(8,128)(2,1)S(1)}, u32[]{:S(2)}, u32[]{:S(2)}) async-start(bf16[64,8,640]{2,1,0:T(8,128)(2,1)} %bitcast.11), calls=%async_computation.2 | async-start | bytes 1310720 | tf_op jit(solution)/shard_map/all_to_all | solution.py:250
  44.5 1.7 %collective-permute-start = (bf16[128,4608]{1,0:T(8,128)(2,1)}, bf16[128,4608]{1,0:T(8,128)(2,1)}, u32[]{:S(2)}, u32[]{:S(2)}) collective-permute-start(bf16[128,4608]{1,0:T(8,128)(2,1)} %get-tuple-element.16), channel_id=1, source_target_pairs={{0,32},{32,0},{1,33},{33,1},{2,34},{34,2},{3,35},{35,3},{4,36},{36... | collective-permute-start | bytes 3538952 | tf_op jit(solution)/shard_map/ppermute | solution.py:267
  46.3 0.2 convert_reduce_fusion.1.slot
  46.4 3.2 %copy-done.1 = bf16[2,384,5120]{2,1,0:T(8,128)(2,1)S(1)} copy-done((bf16[2,384,5120]{2,1,0:T(8,128)(2,1)S(1)}, bf16[2,384,5120]{2,1,0:T(8,128)(2,1)}, u32[]{:S(2)}) %copy-start.1) | copy-done | bytes 7864344
  49.7 3.3 %shard_map.86 = (f32[64,4608]{1,0:T(8,128)S(1)}, f32[64,4608]{1,0:T(8,128)S(1)}, f32[64,4608]{1,0:T(8,128)S(1)}, f32[64,4608]{1,0:T(8,128)S(1)}) custom-call(s32[4]{0:T(128)S(1)} %pad_add_fusion.place, bf16[768,5120]{1,0:T(8,128)(2,1)S(1)} %bitcast.22), custom_call_target="tpu_custom_call" | custom-call | flops 1811939328 | bytes 12582928 | tf_op jit(solution)/shard_map/pallas_call | solution.py:113
  53.0 1.5 convert_add_fusion
  54.5 2.1 %collective-permute-done.1 = bf16[128,4608]{1,0:T(8,128)(2,1)} collective-permute-done((bf16[128,4608]{1,0:T(8,128)(2,1)}, bf16[128,4608]{1,0:T(8,128)(2,1)}, u32[]{:S(2)}, u32[]{:S(2)}) %collective-permute-start.1) | collective-permute-done | bytes 1179680 | tf_op jit(solution)/shard_map/ppermute | solution.py:268
  56.5 1.2 add_convert_fusion.5
  57.7 3.0 %collective-permute-start.4 = (bf16[32,4608]{1,0:T(8,128)(2,1)S(1)}, bf16[32,4608]{1,0:T(8,128)(2,1)S(1)}, u32[]{:S(2)}, u32[]{:S(2)}) collective-permute-start(bf16[32,4608]{1,0:T(8,128)(2,1)S(1)} %get-tuple-element.29), channel_id=1, source_target_pairs={{0,192},{64,0},{128,64},{192,128},{1,193},{65,1},{129,65},{193,129... | collective-permute-start | bytes 884744 | tf_op jit(solution)/shard_map/ppermute | solution.py:156
  60.8 0.4 collective-permute-start.10
  61.1 4.2 %collective-permute-done.4 = bf16[32,4608]{1,0:T(8,128)(2,1)S(1)} collective-permute-done((bf16[32,4608]{1,0:T(8,128)(2,1)S(1)}, bf16[32,4608]{1,0:T(8,128)(2,1)S(1)}, u32[]{:S(2)}, u32[]{:S(2)}) %collective-permute-start.4) | collective-permute-done | bytes 294944 | tf_op jit(solution)/shard_map/ppermute | solution.py:156
  65.3 2.0 %add_convert_fusion.3 = bf16[64,4608]{1,0:T(8,128)(2,1)} fusion(f32[64,4608]{1,0:T(8,128)S(1)} %get-tuple-element.20, bf16[128,4608]{1,0:T(8,128)(2,1)} %collective-permute-done.1, bf16[32,4608]{1,0:T(8,128)(2,1)S(1)} %collective-permute-done.4), kind=kLoop, calls=%fused_computation.4 | loop fusion | flops 1474560 | bytes 2654208 | tf_op jit(solution)/shard_map/convert_element_type | solution.py:161
  67.3 3.6 %collective-permute-start.5 = (bf16[64,4608]{1,0:T(8,128)(2,1)}, bf16[64,4608]{1,0:T(8,128)(2,1)}, u32[]{:S(2)}, u32[]{:S(2)}) collective-permute-start(bf16[64,4608]{1,0:T(8,128)(2,1)} %add_convert_fusion.3), channel_id=1, source_target_pairs={{0,192},{64,0},{128,64},{192,128},{1,193},{65,1},{129,65},{193,129... | collective-permute-start | bytes 1769480 | tf_op jit(solution)/shard_map/ppermute | solution.py:161
  70.9 8.2 %collective-permute-done = bf16[128,4608]{1,0:T(8,128)(2,1)} collective-permute-done((bf16[128,4608]{1,0:T(8,128)(2,1)}, bf16[128,4608]{1,0:T(8,128)(2,1)}, u32[]{:S(2)}, u32[]{:S(2)}) %collective-permute-start) | collective-permute-done | bytes 1179680 | tf_op jit(solution)/shard_map/ppermute | solution.py:267
  79.2 2.1 %add_convert_fusion.4 = bf16[64,4608]{1,0:T(8,128)(2,1)} fusion(f32[64,4608]{1,0:T(8,128)S(1)} %get-tuple-element.17, bf16[128,4608]{1,0:T(8,128)(2,1)} %collective-permute-done, bf16[32,4608]{1,0:T(8,128)(2,1)S(1)} %collective-permute-done.2), kind=kLoop, calls=%fused_computation.5 | loop fusion | flops 1474560 | bytes 2654208 | tf_op jit(solution)/shard_map/convert_element_type | solution.py:160
  81.2 1.5 collective-permute-start.3
  82.7 0.9 collective-permute-done.10
  83.7 1.3 shard_map.91
  85.0 10.4 %all-to-all-start.3 = ((bf16[64,8,256]{2,1,0:T(8,128)(2,1)}), bf16[64,8,256]{2,1,0:T(8,128)(2,1)S(1)}, u32[]{:S(2)}, u32[]{:S(2)}) async-start(bf16[64,8,256]{2,1,0:T(8,128)(2,1)} %bitcast.13), calls=%async_computation.3 | async-start | bytes 524288 | tf_op jit(solution)/shard_map/all_to_all | solution.py:250
  95.4 1.7 %add_convert_fusion.2 = bf16[64,4608]{1,0:T(8,128)(2,1)S(1)} fusion(bf16[64,4608]{1,0:T(8,128)(2,1)} %collective-permute-done.5, bf16[64,4608]{1,0:T(8,128)(2,1)} %collective-permute-done.3, f32[64,4608]{1,0:T(8,128)S(1)} %get-tuple-element.15, bf16[128,4608]{1,0:T(8,128)(2,1)} %collective-permute-done), kind=kLoop, calls=%fused_computation.3 | loop fusion | flops 2064384 | bytes 3538944 | tf_op jit(solution)/shard_map/convert_element_type | solution.py:300
  97.1 1.0 maximum_bitcast_fusion
  98.1 9.0 %all-to-all-done.3 = bf16[64,8,256]{2,1,0:T(8,128)(2,1)S(1)} async-done(((bf16[64,8,256]{2,1,0:T(8,128)(2,1)}), bf16[64,8,256]{2,1,0:T(8,128)(2,1)S(1)}, u32[]{:S(2)}, u32[]{:S(2)}) %all-to-all-start.3) | async-done | bytes 262176 | tf_op jit(solution)/shard_map/all_to_all | solution.py:250
  107.1 4.5 %all-to-all-start = ((bf16[8,8,7040]{2,1,0:T(8,128)(2,1)}), bf16[8,8,7040]{2,1,0:T(8,128)(2,1)S(1)}, u32[]{:S(2)}, u32[]{:S(2)}) async-start(bf16[8,8,7040]{2,1,0:T(8,128)(2,1)} %maximum_bitcast_fusion), calls=%async_computation | async-start | bytes 1802240 | tf_op jit(solution)/shard_map/all_to_all | solution.py:250
  111.7 0.1 collective-permute-start.13
  111.8 1.4 collective-permute-start.12
  113.2 1.9 %collective-permute-start.11 = (bf16[512,128]{1,0:T(8,128)(2,1)S(1)}, bf16[512,128]{1,0:T(8,128)(2,1)S(1)}, u32[]{:S(2)}, u32[]{:S(2)}) collective-permute-start(bf16[512,128]{1,0:T(8,128)(2,1)S(1)} %slice.34), channel_id=1, source_target_pairs={{0,1},{1,0},{2,3},{3,2},{4,5},{5,4},{6,7},{7,6},{8,9},{9,8},{10,11... | collective-permute-start | bytes 393224 | tf_op jit(solution)/shard_map/ppermute | solution.py:278
  115.1 0.6 dynamic_slice.14
  117.6 0.6 dynamic_slice.15
  118.2 0.7 pad_add_fusion.1.place
  119.0 0.7 collective-permute-done.12.two
  119.7 2.1 %shard_map.92 = bf16[512,256]{1,0:T(8,128)(2,1)} custom-call(s32[2]{0:T(128)S(1)} %pad_add_fusion.1.place, bf16[512,256]{1,0:T(8,128)(2,1)S(1)} %bitcast.27, bf16[512,128]{1,0:T(8,128)(2,1)S(1)} %collective-permute-done.11.one, bf16[512,128]{1,0:T(8,128)(2,1)S(1)} %collective-permute-done.12.two, bf16[512,128]{1,0:T(8,128)(2,1)S(1)} %collective-permute-done.13.three, ...), custom_call_target="tpu_custom_call" | custom-call | flops 268435456 | bytes 1572872 | tf_op jit(solution)/shard_map/pallas_call | solution.py:113
  121.8 11.2 %all-to-all-done = bf16[8,8,7040]{2,1,0:T(8,128)(2,1)S(1)} async-done(((bf16[8,8,7040]{2,1,0:T(8,128)(2,1)}), bf16[8,8,7040]{2,1,0:T(8,128)(2,1)S(1)}, u32[]{:S(2)}, u32[]{:S(2)}) %all-to-all-start) | async-done | bytes 901152 | tf_op jit(solution)/shard_map/all_to_all | solution.py:250
  133.0 5.7 %all-to-all-start.4 = ((bf16[64,8,256]{2,1,0:T(8,128)(2,1)}), bf16[64,8,256]{2,1,0:T(8,128)(2,1)S(1)}, u32[]{:S(2)}, u32[]{:S(2)}) async-start(bf16[64,8,256]{2,1,0:T(8,128)(2,1)} %bitcast.15), calls=%async_computation.4 | async-start | bytes 524288 | tf_op jit(solution)/shard_map/all_to_all | solution.py:250
  138.7 0.2 convert_reduce_fusion.slot
  138.9 0.8 shard_map.89
  139.7 10.8 %all-to-all-done.4 = bf16[64,8,256]{2,1,0:T(8,128)(2,1)S(1)} async-done(((bf16[64,8,256]{2,1,0:T(8,128)(2,1)}), bf16[64,8,256]{2,1,0:T(8,128)(2,1)S(1)}, u32[]{:S(2)}, u32[]{:S(2)}) %all-to-all-start.4) | async-done | bytes 262176 | tf_op jit(solution)/shard_map/all_to_all | solution.py:250
  150.4 16.5 %all_to_all.55 = bf16[64,8,256]{2,1,0:T(8,128)(2,1)S(1)} all-to-all(bf16[64,8,256]{2,1,0:T(8,128)(2,1)S(1)} %bitcast.30), channel_id=1, replica_groups=mesh['y'=4,'xl'=2,'z'=8,'xh'=2,'c'=2] {'y','xl','z'}, dimensions={0} | all-to-all | bytes 524288 | tf_op jit(solution)/shard_map/all_to_all | solution.py:250
  167.0 0.9 shard_map.93
  (31 shorter events, 0.3 us)
Async XLA Ops:
  0.7 3.2 %copy-start = (bf16[2,384,5120]{2,1,0:T(8,128)(2,1)S(1)}, bf16[2,384,5120]{2,1,0:T(8,128)(2,1)}, u32[]{:S(2)}) copy-start(bf16[2,384,5120]{2,1,0:T(8,128)(2,1)} %param.7) | copy-start | bytes 23592964
  7.3 9.7 %collective-permute-start.8 = (bf16[64,2432]{1,0:T(8,128)(2,1)S(1)}, bf16[64,2432]{1,0:T(8,128)(2,1)S(1)}, u32[]{:S(2)}, u32[]{:S(2)}) collective-permute-start(bf16[64,2432]{1,0:T(8,128)(2,1)S(1)} %get-tuple-element.25), channel_id=1, source_target_pairs={{0,192},{64,0},{128,64},{192,128},{1,193},{65,1},{129,65},{193,129... | collective-permute-start | bytes 933896 | tf_op jit(solution)/shard_map/ppermute | solution.py:156
  10.4 11.3 %collective-permute-start.6 = (bf16[64,2432]{1,0:T(8,128)(2,1)S(1)}, bf16[64,2432]{1,0:T(8,128)(2,1)S(1)}, u32[]{:S(2)}, u32[]{:S(2)}) collective-permute-start(bf16[64,2432]{1,0:T(8,128)(2,1)S(1)} %get-tuple-element.23), channel_id=1, source_target_pairs={{0,64},{64,128},{128,192},{192,0},{1,65},{65,129},{129,193},{193,1... | collective-permute-start | bytes 933896 | tf_op jit(solution)/shard_map/ppermute | solution.py:155
  18.0 35.0 %collective-permute-start.9 = (bf16[128,2432]{1,0:T(8,128)(2,1)}, bf16[128,2432]{1,0:T(8,128)(2,1)}, u32[]{:S(2)}, u32[]{:S(2)}) collective-permute-start(bf16[128,2432]{1,0:T(8,128)(2,1)} %add_convert_fusion), channel_id=1, source_target_pairs={{0,192},{64,0},{128,64},{192,128},{1,193},{65,1},{129,65},{193,129... | collective-permute-start | bytes 1867784 | tf_op jit(solution)/shard_map/ppermute | solution.py:161
  22.6 8.6 %copy-start.2 = (bf16[2,512,512]{2,1,0:T(8,128)(2,1)S(1)}, bf16[2,512,512]{2,1,0:T(8,128)(2,1)}, u32[]{:S(2)}) copy-start(bf16[2,512,512]{2,1,0:T(8,128)(2,1)} %basis.1) | copy-start | bytes 3145732
  22.6 8.6 %copy-start.3 = (bf16[10,8,1024]{2,1,0:T(8,128)(2,1)S(1)}, bf16[10,8,1024]{2,1,0:T(8,128)(2,1)}, u32[]{:S(2)}) copy-start(bf16[10,8,1024]{2,1,0:T(8,128)(2,1)} %param.9) | copy-start | bytes 491524
  22.6 8.6 %copy-start.4 = (f32[2,512]{1,0:T(2,128)S(1)}, f32[2,512]{1,0:T(2,128)}, u32[]{:S(2)}) copy-start(f32[2,512]{1,0:T(2,128)} %values.1) | copy-start | bytes 12292
  22.6 30.4 %collective-permute-start.7 = (bf16[128,2432]{1,0:T(8,128)(2,1)}, bf16[128,2432]{1,0:T(8,128)(2,1)}, u32[]{:S(2)}, u32[]{:S(2)}) collective-permute-start(bf16[128,2432]{1,0:T(8,128)(2,1)} %add_convert_fusion.1), channel_id=1, source_target_pairs={{0,64},{64,128},{128,192},{192,0},{1,65},{65,129},{129,193},{193,1... | collective-permute-start | bytes 1867784 | tf_op jit(solution)/shard_map/ppermute | solution.py:160
  28.4 28.1 %collective-permute-start.1 = (bf16[128,4608]{1,0:T(8,128)(2,1)}, bf16[128,4608]{1,0:T(8,128)(2,1)}, u32[]{:S(2)}, u32[]{:S(2)}) collective-permute-start(bf16[128,4608]{1,0:T(8,128)(2,1)} %get-tuple-element.19), channel_id=1, source_target_pairs={{0,34},{2,32},{32,2},{34,0},{1,35},{3,33},{33,3},{35,1},{4,38},{6,... | collective-permute-start | bytes 3538952 | tf_op jit(solution)/shard_map/ppermute | solution.py:268
  31.2 15.1 %copy-start.5 = (s32[10]{0:T(128)S(1)}, s32[10]{0:T(128)}, u32[]{:S(2)}) copy-start(s32[10]{0:T(128)} %owner.3) | copy-start | bytes 124
  32.7 50.9 %all-to-all-start.2 = ((bf16[64,8,640]{2,1,0:T(8,128)(2,1)}), bf16[64,8,640]{2,1,0:T(8,128)(2,1)S(1)}, u32[]{:S(2)}, u32[]{:S(2)}) async-start(bf16[64,8,640]{2,1,0:T(8,128)(2,1)} %bitcast.11), calls=%async_computation.2 | async-start | bytes 1310720 | tf_op jit(solution)/shard_map/all_to_all | solution.py:250
  44.5 34.7 %collective-permute-start = (bf16[128,4608]{1,0:T(8,128)(2,1)}, bf16[128,4608]{1,0:T(8,128)(2,1)}, u32[]{:S(2)}, u32[]{:S(2)}) collective-permute-start(bf16[128,4608]{1,0:T(8,128)(2,1)} %get-tuple-element.16), channel_id=1, source_target_pairs={{0,32},{32,0},{1,33},{33,1},{2,34},{34,2},{3,35},{35,3},{4,36},{36... | collective-permute-start | bytes 3538952 | tf_op jit(solution)/shard_map/ppermute | solution.py:267
  46.4 3.2 %copy-start.1 = (bf16[2,384,5120]{2,1,0:T(8,128)(2,1)S(1)}, bf16[2,384,5120]{2,1,0:T(8,128)(2,1)}, u32[]{:S(2)}) copy-start(bf16[2,384,5120]{2,1,0:T(8,128)(2,1)} %param.7) | copy-start | bytes 23592964
  57.7 7.6 %collective-permute-start.4 = (bf16[32,4608]{1,0:T(8,128)(2,1)S(1)}, bf16[32,4608]{1,0:T(8,128)(2,1)S(1)}, u32[]{:S(2)}, u32[]{:S(2)}) collective-permute-start(bf16[32,4608]{1,0:T(8,128)(2,1)S(1)} %get-tuple-element.29), channel_id=1, source_target_pairs={{0,192},{64,0},{128,64},{192,128},{1,193},{65,1},{129,65},{193,129... | collective-permute-start | bytes 884744 | tf_op jit(solution)/shard_map/ppermute | solution.py:156
  60.8 22.8 %collective-permute-start.10 = (bf16[64,2432]{1,0:T(8,128)(2,1)S(1)}, bf16[64,2432]{1,0:T(8,128)(2,1)S(1)}, u32[]{:S(2)}, u32[]{:S(2)}) collective-permute-start(bf16[64,2432]{1,0:T(8,128)(2,1)S(1)} %dynamic-slice_convert_fusion), channel_id=1, source_target_pairs={{0,32},{32,0},{1,33},{33,1},{2,34},{34,2},{3,35},{35,3},{4,36},{36... | collective-permute-start | bytes 933896 | tf_op jit(solution)/shard_map/ppermute | solution.py:290
  61.1 18.0 %collective-permute-start.2 = (bf16[32,4608]{1,0:T(8,128)(2,1)S(1)}, bf16[32,4608]{1,0:T(8,128)(2,1)S(1)}, u32[]{:S(2)}, u32[]{:S(2)}) collective-permute-start(bf16[32,4608]{1,0:T(8,128)(2,1)S(1)} %get-tuple-element.28), channel_id=1, source_target_pairs={{0,64},{64,128},{128,192},{192,0},{1,65},{65,129},{129,193},{193,1... | collective-permute-start | bytes 884744 | tf_op jit(solution)/shard_map/ppermute | solution.py:155
  67.3 28.1 %collective-permute-start.5 = (bf16[64,4608]{1,0:T(8,128)(2,1)}, bf16[64,4608]{1,0:T(8,128)(2,1)}, u32[]{:S(2)}, u32[]{:S(2)}) collective-permute-start(bf16[64,4608]{1,0:T(8,128)(2,1)} %add_convert_fusion.3), channel_id=1, source_target_pairs={{0,192},{64,0},{128,64},{192,128},{1,193},{65,1},{129,65},{193,129... | collective-permute-start | bytes 1769480 | tf_op jit(solution)/shard_map/ppermute | solution.py:161
  81.2 14.2 %collective-permute-start.3 = (bf16[64,4608]{1,0:T(8,128)(2,1)}, bf16[64,4608]{1,0:T(8,128)(2,1)}, u32[]{:S(2)}, u32[]{:S(2)}) collective-permute-start(bf16[64,4608]{1,0:T(8,128)(2,1)} %add_convert_fusion.4), channel_id=1, source_target_pairs={{0,64},{64,128},{128,192},{192,0},{1,65},{65,129},{129,193},{193,1... | collective-permute-start | bytes 1769480 | tf_op jit(solution)/shard_map/ppermute | solution.py:160
  85.0 22.1 %all-to-all-start.3 = ((bf16[64,8,256]{2,1,0:T(8,128)(2,1)}), bf16[64,8,256]{2,1,0:T(8,128)(2,1)S(1)}, u32[]{:S(2)}, u32[]{:S(2)}) async-start(bf16[64,8,256]{2,1,0:T(8,128)(2,1)} %bitcast.13), calls=%async_computation.3 | async-start | bytes 524288 | tf_op jit(solution)/shard_map/all_to_all | solution.py:250
  98.1 17.0 %copy-start.7 = (s32[64]{0:T(128)S(1)}, s32[64]{0:T(128)}, u32[]{:S(2)}) copy-start(s32[64]{0:T(128)} %constant.42.clone) | copy-start | bytes 772
  107.1 25.8 %all-to-all-start = ((bf16[8,8,7040]{2,1,0:T(8,128)(2,1)}), bf16[8,8,7040]{2,1,0:T(8,128)(2,1)S(1)}, u32[]{:S(2)}, u32[]{:S(2)}) async-start(bf16[8,8,7040]{2,1,0:T(8,128)(2,1)} %maximum_bitcast_fusion), calls=%async_computation | async-start | bytes 1802240 | tf_op jit(solution)/shard_map/all_to_all | solution.py:250
  111.7 27.1 %copy-start.6 = (s32[55]{0:T(128)S(1)}, s32[55]{0:T(128)}, u32[]{:S(2)}) copy-start(s32[55]{0:T(128)} %owner.2) | copy-start | bytes 664
  111.7 7.3 %collective-permute-start.13 = (bf16[512,128]{1,0:T(8,128)(2,1)S(1)}, bf16[512,128]{1,0:T(8,128)(2,1)S(1)}, u32[]{:S(2)}, u32[]{:S(2)}) collective-permute-start(bf16[512,128]{1,0:T(8,128)(2,1)S(1)} %slice.34), channel_id=1, source_target_pairs={{0,3},{1,2},{2,1},{3,0},{4,7},{5,6},{6,5},{7,4},{8,11},{9,10},{10,... | collective-permute-start | bytes 393224 | tf_op jit(solution)/shard_map/ppermute | solution.py:278
  111.8 7.9 %collective-permute-start.12 = (bf16[512,128]{1,0:T(8,128)(2,1)S(1)}, bf16[512,128]{1,0:T(8,128)(2,1)S(1)}, u32[]{:S(2)}, u32[]{:S(2)}) collective-permute-start(bf16[512,128]{1,0:T(8,128)(2,1)S(1)} %slice.34), channel_id=1, source_target_pairs={{0,2},{1,3},{2,0},{3,1},{4,6},{5,7},{6,4},{7,5},{8,10},{9,11},{10,... | collective-permute-start | bytes 393224 | tf_op jit(solution)/shard_map/ppermute | solution.py:278
  113.2 6.5 %collective-permute-start.11 = (bf16[512,128]{1,0:T(8,128)(2,1)S(1)}, bf16[512,128]{1,0:T(8,128)(2,1)S(1)}, u32[]{:S(2)}, u32[]{:S(2)}) collective-permute-start(bf16[512,128]{1,0:T(8,128)(2,1)S(1)} %slice.34), channel_id=1, source_target_pairs={{0,1},{1,0},{2,3},{3,2},{4,5},{5,4},{6,7},{7,6},{8,9},{9,8},{10,11... | collective-permute-start | bytes 393224 | tf_op jit(solution)/shard_map/ppermute | solution.py:278
  133.0 17.4 %all-to-all-start.4 = ((bf16[64,8,256]{2,1,0:T(8,128)(2,1)}), bf16[64,8,256]{2,1,0:T(8,128)(2,1)S(1)}, u32[]{:S(2)}, u32[]{:S(2)}) async-start(bf16[64,8,256]{2,1,0:T(8,128)(2,1)} %bitcast.15), calls=%async_computation.4 | async-start | bytes 524288 | tf_op jit(solution)/shard_map/all_to_all | solution.py:250

commit v4 on v3

--- a/solution.py
+++ b/solution.py
@@ -107,43 +107,50 @@
 SMEM = pl.BlockSpec(memory_space=pltpu.SMEM)
 
 
-def call(kernel, outs, scratch, flops, *operands, scalars=1):
+def call(kernel, outs, scratch, flops, *operands, scalars=1, after=(), vmem=12):
     moved = sum(x.size * x.dtype.itemsize for x in operands)
     moved += sum(x.size * x.dtype.itemsize for x in outs)
+    count = len(operands)
+
+    def body(*refs):
+        kernel(*refs[:count], *refs[count + len(after) :])
+
     return pl.pallas_call(
-        kernel,
+        body,
         out_shape=tuple(outs),
-        in_specs=[SMEM] * scalars + [VMEM] * (len(operands) - scalars),
+        in_specs=[SMEM] * scalars + [VMEM] * (count - scalars) + [pl.BlockSpec(memory_space=pl.ANY)] * len(after),
         out_specs=(VMEM,) * len(outs),
         scratch_shapes=[pltpu.VMEM(shape, dtype) for shape, dtype in scratch],
-        compiler_params=pltpu.CompilerParams(vmem_limit_bytes=40 * 2**20),
+        compiler_params=pltpu.CompilerParams(vmem_limit_bytes=vmem * 2**20),
         cost_estimate=pl.CostEstimate(flops=flops, bytes_accessed=moved, transcendentals=0),
-    )(*operands)
+    )(*operands, *after)
 
 
 def array(shape, dtype):
     return jax.ShapeDtypeStruct(shape, dtype)
 
 
-def products(act, place):
+def sent_products(act, place):
     tokens = act.shape[0]
-    wide, rest = X_TILES * SLAB, Y_TILES * SLAB
-    slab = ((tokens, NT * SLAB), bf16)
-    half = ((256, tokens), bf16)
-    full = ((TILE, tokens), bf16)
-    sent = call(
-        sent_kernel, [array((128, wide), bf16)] * 2, [slab, slab, half], 2 * tokens * 256 * wide, place, act
-    )
-    along = call(
-        along_kernel,
-        [array((128, rest), f32)] * 2 + [array((64, rest), bf16)] * 2 + [array((128, rest), f32)],
-        [slab, full],
-        2 * tokens * TILE * rest,
-        place,
-        act,
-    )
-    kept = call(kept_kernel, [array((64, wide), f32)] * 4, [slab, half], 2 * tokens * 256 * wide, place, act)
-    return sent, along, kept
+    wide = X_TILES * SLAB
+    slab, half = ((tokens, NT * SLAB), bf16), ((256, tokens), bf16)
+    return call(sent_kernel, [array((128, wide), bf16)] * 2, [slab, slab, half], 2 * tokens * 256 * wide, place, act)
+
+
+def kept_products(act, place, after):
+    tokens = act.shape[0]
+    wide = X_TILES * SLAB
+    slab, half = ((tokens, NT * SLAB), bf16), ((256, tokens), bf16)
+    outs = [array((64, wide), f32)] * 4
+    return call(kept_kernel, outs, [slab, half], 2 * tokens * 256 * wide, place, act, after=after)
+
+
+def along_products(act, place, after):
+    tokens = act.shape[0]
+    wide = Y_TILES * SLAB
+    slab, full = ((tokens, NT * SLAB), bf16), ((TILE, tokens), bf16)
+    outs = [array((128, wide), f32)] * 2 + [array((64, wide), bf16)] * 2 + [array((128, wide), f32)]
+    return call(along_kernel, outs, [slab, full], 2 * tokens * TILE * wide, place, act, after=after)
 
 
 def ring(axis, step):
@@ -222,7 +229,7 @@
     out[...] = dot(basis[...], scaled).astype(bf16)
 
 
-def pack_kernel(total, owner, slot, got, out, sums, slots):
+def pack_kernel(total, owner, slot, got, rotated, out, sums, slots):
     full = got[...].astype(f32)
     acc = full[0:8]
     for k in range(8, 64, 8):
@@ -233,13 +240,14 @@
         row = pl.multiple_of(owner[u] * 8, 8)
         lane = pl.multiple_of(slot[u] * SLAB, SLAB)
         slots[pl.ds(row, 8), pl.ds(lane, SLAB)] = sums[:, at * SLAB : (at + 1) * SLAB]
-    out[...] = slots[...].astype(bf16)
-
-
-def unpack_kernel(got, returned, factor, result):
+    out[:, 0:256] = slots[...].astype(bf16)
+    out[:, 256:512] = rotated[...]
+
+
+def unpack_kernel(got, factor, result):
     for s in range(SLOTS):
         factor[s * TILE : (s + 1) * TILE, :] = got[:, s * SLAB : (s + 1) * SLAB].astype(f32)
-    turned = returned[...].astype(f32)
+    turned = got[:, 256:512].astype(f32)
     for b in range(0, NT, 2):
         for q in range(4):
             pair = [turned[PLACES[u] * 8 : PLACES[u] * 8 + 8] for u in (b * 4 + q, b * 4 + 4 + q)]
@@ -263,16 +271,21 @@
     tile_rank = slot_rank(tile_owner).astype(jnp.int32)
     block_rank = slot_rank(block_owner).astype(jnp.int32)
 
-    (near, far), (zero, one, up, down, three), own = products(act, place)
+    near, far = sent_products(act, place)
+    zero, one, up, down, three = along_products(act, place, (near,))
     near = lax.ppermute(near, "xl", [(0, 1), (1, 0)])
     far = lax.ppermute(far, ("xl", "xh"), [(i, 3 - i) for i in range(4)])
 
     [out] = call(
         scatter_kernel, [array((TILE, 640), bf16)], [], 0,
-        place, eigen_basis, eigen_values, gradient.reshape(blocks * rows, cols),
-    )
+        place, eigen_basis, eigen_values, gradient.reshape(blocks * rows, cols), after=(up,),
+    )
+    own = kept_products(act, place, (out,))
     got = exchange(out, DP)
-    [out] = call(forward_kernel, [array((TILE, 256), bf16)], [], 0, block_owner, block_rank, got, scalars=2)
+    [out] = call(
+        forward_kernel, [array((TILE, 256), bf16)], [], 0,
+        block_owner, block_rank, got, scalars=2, after=(near, far),
+    )
     mine = exchange(out, DP)
     quarter = mine[:, :SLAB]
     others = [lax.ppermute(quarter, ("xh", "c"), [(i, i ^ k) for i in range(4)]) for k in (1, 2, 3)]
@@ -281,7 +294,6 @@
         rotate_kernel, [array((TILE, COLS), bf16)], [((TILE, TILE), bf16)], 4 * TILE * TILE * COLS,
         jnp.stack([group, block_rank[my_block]]).astype(jnp.int32), mine, *others, got,
     )
-    returned = exchange(rotated, DP)
 
     along = around_y(lambda: zero, lambda: one, up, down, lambda: three)
     half = along.shape[0] // 2
@@ -301,13 +313,13 @@
 
     [out] = call(
         functools.partial(pack_kernel, micro * tokens * dp_count),
-        [array((TILE, 256), bf16)], [((8, UT * SLAB), f32), ((TILE, 256), f32)], 0,
-        tile_owner, tile_rank, sums, scalars=2,
+        [array((TILE, 512), bf16)], [((8, UT * SLAB), f32), ((TILE, 256), f32)], 0,
+        tile_owner, tile_rank, sums, rotated, scalars=2,
     )
     final = exchange(out, DP)
     factor, result = call(
         unpack_kernel, [array((SLOTS * TILE, SLAB), f32), array((blocks * rows, cols), bf16)], [], 0,
-        final, returned, scalars=0,
+        final, scalars=0,
     )
     return factor.reshape(SLOTS, TILE, SLAB), result.reshape(blocks, rows, cols)
 

time: 169 us -> 141 us (0.83)
  waiting for transfers between devices: 53.7 us -> 39.1 us
  starting transfers between devices: 55.6 us -> 41.7 us
  blocking collectives: 16.5 us -> 20.7 us
  other arithmetic: 12.5 us -> 9.53 us
    all_to_all x4 -> x3, waiting for transfers between devices: 31 us -> 16.1 us  [exchange(): return lax.all_to_all(x, axis, split_axis=0, concat_axis=0, tiled=True)]
    ppermute x1, waiting for transfers between devices: 8.24 us -> 0.01 us  [shards(): near = lax.ppermute(near, 'xl', [(0, 1), (1, 0)])]
    all_to_all x4 -> x3, starting transfers between devices: 32.4 us -> 24.3 us  [exchange(): return lax.all_to_all(x, axis, split_axis=0, concat_axis=0, tiled=True)]
    ppermute x2, waiting for transfers between devices: 0.01 us -> 7.15 us  [around_y(): up = lax.ppermute(up, 'y', ring('y', 1))]
    ppermute x2, waiting for transfers between devices: 10.8 us -> 5.35 us  [around_y(): down = lax.ppermute(down, 'y', ring('y', -1))]
    all_to_all x1, blocking collectives: 16.5 us -> 20.7 us  [exchange(): return lax.all_to_all(x, axis, split_axis=0, concat_axis=0, tiled=True)]
    ppermute x2, starting transfers between devices: 6.09 us -> 2.24 us  [around_y(): down = lax.ppermute(down, 'y', ring('y', -1))]
    ppermute x3, waiting for transfers between devices: 0.73 us -> 4.05 us  [shards(): lax.ppermute(quarter, ('xh', 'c'), [(i, i ^ k) for i in range(4)])]
  transfers between devices with their start and end apart: 18 -> 17, of which waited for: 9 -> 9; matrix products, arithmetic and copies ran while one was open for 8% -> 8% of each run, Pallas kernels for 9% -> 5%
where the time goes in v4:
time: 141 us
  starting transfers between devices  41.7 us (30%)
  waiting for transfers between devices  39.1 us (28%)
  blocking collectives  20.7 us (15%)
  Pallas kernels  18.4 us (13%)
  other arithmetic  9.53 us (7%)
  local copies, waits for them, and re-layouts  8.76 us (6%)
  between operations  2.75 us (2%)
    all_to_all x3, starting transfers between devices, exchange(): return lax.all_to_all(x, axis, split_axis=0, concat_axis=0, tiled=True)  24.3 us
    all_to_all x1, blocking collectives, exchange(): return lax.all_to_all(x, axis, split_axis=0, concat_axis=0, tiled=True)  20.7 us
    pallas_call x8, Pallas kernels, call(): pl.pallas_call(body, out_shape=tuple(outs), in_specs=[SMEM] * scalars + [...  18.4 us
    all_to_all x3, waiting for transfers between devices, exchange(): return lax.all_to_all(x, axis, split_axis=0, concat_axis=0, tiled=True)  16.1 us
    unnamed x22, local copies, waits for them, and re-layouts  7.51 us
    ppermute x2, waiting for transfers between devices, around_y(): up = lax.ppermute(up, 'y', ring('y', 1))  7.15 us
    ppermute x2, waiting for transfers between devices, around_y(): down = lax.ppermute(down, 'y', ring('y', -1))  5.35 us
    ppermute x2, starting transfers between devices, around_y(): down = lax.ppermute(down.astype(bf16), 'y', ring('y', -1))  4.82 us
  transfers between devices with their start and end apart: 17, of which 9 were waited for; matrix products, arithmetic and copies ran while one was open for 8% of the time, Pallas kernels for 5%

profile of v4, /device:TPU:32, one launch (start us, length us, event | category | flops | bytes accessed | tf_op | source)
XLA Modules:
  0.0 141.0 jit_solution(4799757191622484021)
XLA Ops:
  0.7 3.2 %copy-done = bf16[2,384,5120]{2,1,0:T(8,128)(2,1)S(1)} copy-done((bf16[2,384,5120]{2,1,0:T(8,128)(2,1)S(1)}, bf16[2,384,5120]{2,1,0:T(8,128)(2,1)}, u32[]{:S(2)}) %copy-start) | copy-done | bytes 7864344
  4.0 5.8 %shard_map.86 = (bf16[128,4608]{1,0:T(8,128)(2,1)}, bf16[128,4608]{1,0:T(8,128)(2,1)}) custom-call(s32[4]{0:T(128)S(1)} %pad_add_fusion.refs_0_, bf16[768,5120]{1,0:T(8,128)(2,1)S(1)} %bitcast.18), custom_call_target="tpu_custom_call" | custom-call | flops 1811939328 | bytes 10223632 | tf_op jit(solution)/shard_map/pallas_call | solution.py:118
  9.8 3.4 %shard_map.87 = (f32[128,2432]{1,0:T(8,128)S(1)}, f32[128,2432]{1,0:T(8,128)S(1)}, bf16[64,2432]{1,0:T(8,128)(2,1)S(1)}, bf16[64,2432]{1,0:T(8,128)(2,1)S(1)}, f32[128,2432]{1,0:T(8,128)S(1)}) custom-call(s32[4]{0:T(128)S(1)} %pad_add_fusion.refs_0_, bf16[768,5120]{1,0:T(8,128)(2,1)S(1)} %bitcast.19, bf16[128,4608]{1,0:T(8,128)(2,1)} %get-tuple-element.15.refs_2_), custom_call_target="tpu_custom_call" | custom-call | flops 1912602624 | bytes 12222480 | tf_op jit(solution)/shard_map/pallas_call | solution.py:118
  13.2 1.6 %collective-permute-start.6 = (bf16[64,2432]{1,0:T(8,128)(2,1)S(1)}, bf16[64,2432]{1,0:T(8,128)(2,1)S(1)}, u32[]{:S(2)}, u32[]{:S(2)}) collective-permute-start(bf16[64,2432]{1,0:T(8,128)(2,1)S(1)} %get-tuple-element.16.refs_4_), channel_id=1, source_target_pairs={{0,64},{64,128},{128,192},{192,0},{1,65},{65,129},{129,193},{193,1... | collective-permute-start | bytes 933896 | tf_op jit(solution)/shard_map/ppermute | solution.py:162
  14.8 1.7 %collective-permute-start.8 = (bf16[64,2432]{1,0:T(8,128)(2,1)S(1)}, bf16[64,2432]{1,0:T(8,128)(2,1)S(1)}, u32[]{:S(2)}, u32[]{:S(2)}) collective-permute-start(bf16[64,2432]{1,0:T(8,128)(2,1)S(1)} %get-tuple-element.25), channel_id=1, source_target_pairs={{0,192},{64,0},{128,64},{192,128},{1,193},{65,1},{129,65},{193,129... | collective-permute-start | bytes 933896 | tf_op jit(solution)/shard_map/ppermute | solution.py:163
  16.5 7.1 %collective-permute-done.6 = bf16[64,2432]{1,0:T(8,128)(2,1)S(1)} collective-permute-done((bf16[64,2432]{1,0:T(8,128)(2,1)S(1)}, bf16[64,2432]{1,0:T(8,128)(2,1)S(1)}, u32[]{:S(2)}, u32[]{:S(2)}) %collective-permute-start.6) | collective-permute-done | bytes 311328 | tf_op jit(solution)/shard_map/ppermute | solution.py:162
  23.6 0.9 add_convert_fusion.1
  24.5 0.3 collective-permute-start.7
  24.8 0.9 add_convert_fusion
  25.8 2.9 %collective-permute-start.9 = (bf16[128,2432]{1,0:T(8,128)(2,1)}, bf16[128,2432]{1,0:T(8,128)(2,1)}, u32[]{:S(2)}, u32[]{:S(2)}) collective-permute-start(bf16[128,2432]{1,0:T(8,128)(2,1)} %add_convert_fusion), channel_id=1, source_target_pairs={{0,192},{64,0},{128,64},{192,128},{1,193},{65,1},{129,65},{193,129... | collective-permute-start | bytes 1867784 | tf_op jit(solution)/shard_map/ppermute | solution.py:168
  28.7 2.8 %collective-permute-start.1 = (bf16[128,4608]{1,0:T(8,128)(2,1)}, bf16[128,4608]{1,0:T(8,128)(2,1)S(1)}, u32[]{:S(2)}, u32[]{:S(2)}) collective-permute-start(bf16[128,4608]{1,0:T(8,128)(2,1)} %get-tuple-element.20), channel_id=1, source_target_pairs={{0,34},{2,32},{32,2},{34,0},{1,35},{3,33},{33,3},{35,1},{4,38},{6,... | collective-permute-start | bytes 3538952 | tf_op jit(solution)/shard_map/ppermute | solution.py:277
  31.5 0.2 collective-permute-start
  31.7 1.6 %shard_map.88.refs_2_ = bf16[512,640]{1,0:T(8,128)(2,1)} custom-call(s32[4]{0:T(128)S(1)} %pad_add_fusion.refs_0_, bf16[2,512,512]{2,1,0:T(8,128)(2,1)S(1)} %copy-done.5, f32[2,512]{1,0:T(2,128)S(1)} %copy-done.7, bf16[80,1024]{1,0:T(8,128)(2,1)S(1)} %bitcast.28, bf16[64,2432]{1,0:T(8,128)(2,1)S(1)} %get-tuple-element.16.refs_4_), custom_call_target="tpu_custom_call" | custom-call | bytes 1871888 | tf_op jit(solution)/shard_map/pallas_call | solution.py:118
  33.3 10.7 %all-to-all-start.1 = ((bf16[64,8,640]{2,1,0:T(8,128)(2,1)}), bf16[64,8,640]{2,1,0:T(8,128)(2,1)S(1)}, u32[]{:S(2)}, u32[]{:S(2)}) async-start(bf16[64,8,640]{2,1,0:T(8,128)(2,1)} %bitcast.9), calls=%async_computation.1 | async-start | bytes 1310720 | tf_op jit(solution)/shard_map/all_to_all | solution.py:258
  44.0 0.2 convert_reduce_fusion.1.refs_1_
  44.2 3.2 %copy-done.1 = bf16[2,384,5120]{2,1,0:T(8,128)(2,1)S(1)} copy-done((bf16[2,384,5120]{2,1,0:T(8,128)(2,1)S(1)}, bf16[2,384,5120]{2,1,0:T(8,128)(2,1)}, u32[]{:S(2)}) %copy-start.1) | copy-done | bytes 7864344
  47.4 3.3 %shard_map.89 = (f32[64,4608]{1,0:T(8,128)S(1)}, f32[64,4608]{1,0:T(8,128)S(1)}, f32[64,4608]{1,0:T(8,128)S(1)}, f32[64,4608]{1,0:T(8,128)S(1)}) custom-call(s32[4]{0:T(128)S(1)} %pad_add_fusion.refs_0_, bf16[768,5120]{1,0:T(8,128)(2,1)S(1)} %bitcast.20, bf16[512,640]{1,0:T(8,128)(2,1)} %shard_map.88.refs_2_), custom_call_target="tpu_custom_call" | custom-call | flops 1811939328 | bytes 12582928 | tf_op jit(solution)/shard_map/pallas_call | solution.py:118
  50.7 1.0 copy-done.4
  51.7 1.5 %convert_add_fusion = f32[128,2432]{1,0:T(8,128)S(1)} fusion(bf16[128,2432]{1,0:T(8,128)(2,1)} %collective-permute-done.9, f32[128,2432]{1,0:T(8,128)S(1)} %copy-done.3, bf16[128,2432]{1,0:T(8,128)(2,1)} %collective-permute-done.7), kind=kLoop, calls=%fused_computation | loop fusion | flops 1245184 | bytes 3735552 | tf_op jit(solution)/shard_map/add | solution.py:169
  53.2 3.3 %collective-permute-done.1.refs_4_ = bf16[128,4608]{1,0:T(8,128)(2,1)S(1)} collective-permute-done((bf16[128,4608]{1,0:T(8,128)(2,1)}, bf16[128,4608]{1,0:T(8,128)(2,1)S(1)}, u32[]{:S(2)}, u32[]{:S(2)}) %collective-permute-start.1) | collective-permute-done | bytes 1179680 | tf_op jit(solution)/shard_map/ppermute | solution.py:277
  56.7 0.6 collective-permute-start.4
  57.3 0.7 collective-permute-start.10
  58.0 1.2 collective-permute-start.2
  59.2 5.3 %collective-permute-done.4 = bf16[32,4608]{1,0:T(8,128)(2,1)S(1)} collective-permute-done((bf16[32,4608]{1,0:T(8,128)(2,1)S(1)}, bf16[32,4608]{1,0:T(8,128)(2,1)S(1)}, u32[]{:S(2)}, u32[]{:S(2)}) %collective-permute-start.4) | collective-permute-done | bytes 294944 | tf_op jit(solution)/shard_map/ppermute | solution.py:163
  64.5 1.0 add_convert_fusion.3
  65.5 1.9 %collective-permute-start.5 = (bf16[64,4608]{1,0:T(8,128)(2,1)}, bf16[64,4608]{1,0:T(8,128)(2,1)}, u32[]{:S(2)}, u32[]{:S(2)}) collective-permute-start(bf16[64,4608]{1,0:T(8,128)(2,1)} %add_convert_fusion.3), channel_id=1, source_target_pairs={{0,192},{64,0},{128,64},{192,128},{1,193},{65,1},{129,65},{193,129... | collective-permute-start | bytes 1769480 | tf_op jit(solution)/shard_map/ppermute | solution.py:168
  67.4 1.0 add_convert_fusion.4
  68.6 2.9 %collective-permute-done.10 = bf16[64,2432]{1,0:T(8,128)(2,1)S(1)} collective-permute-done((bf16[64,2432]{1,0:T(8,128)(2,1)S(1)}, bf16[64,2432]{1,0:T(8,128)(2,1)S(1)}, u32[]{:S(2)}, u32[]{:S(2)}) %collective-permute-start.10) | collective-permute-done | bytes 311328 | tf_op jit(solution)/shard_map/ppermute | solution.py:302
  71.6 1.3 shard_map.90
  72.9 9.2 %all-to-all-start.2 = ((bf16[64,8,256]{2,1,0:T(8,128)(2,1)}), bf16[64,8,256]{2,1,0:T(8,128)(2,1)S(1)}, u32[]{:S(2)}, u32[]{:S(2)}) async-start(bf16[64,8,256]{2,1,0:T(8,128)(2,1)} %bitcast.11), calls=%async_computation.2 | async-start | bytes 524288 | tf_op jit(solution)/shard_map/all_to_all | solution.py:258
  82.2 0.2 collective-permute-done.3
  82.4 1.9 %add_convert_fusion.2 = bf16[64,4608]{1,0:T(8,128)(2,1)S(1)} fusion(bf16[64,4608]{1,0:T(8,128)(2,1)} %collective-permute-done.5, bf16[64,4608]{1,0:T(8,128)(2,1)} %collective-permute-done.3, f32[64,4608]{1,0:T(8,128)} %copy-done.4, bf16[128,4608]{1,0:T(8,128)(2,1)S(1)} %collective-permute-done.refs_3_), kind=kLoop, calls=%fused_computation.3 | loop fusion | flops 2064384 | bytes 3538944 | tf_op jit(solution)/shard_map/convert_element_type | solution.py:312
  84.3 1.0 maximum_bitcast_fusion
  85.3 8.6 %all-to-all-done.2 = bf16[64,8,256]{2,1,0:T(8,128)(2,1)S(1)} async-done(((bf16[64,8,256]{2,1,0:T(8,128)(2,1)}), bf16[64,8,256]{2,1,0:T(8,128)(2,1)S(1)}, u32[]{:S(2)}, u32[]{:S(2)}) %all-to-all-start.2) | async-done | bytes 262176 | tf_op jit(solution)/shard_map/all_to_all | solution.py:258
  93.9 4.3 %all-to-all-start = ((bf16[8,8,7040]{2,1,0:T(8,128)(2,1)}), bf16[8,8,7040]{2,1,0:T(8,128)(2,1)S(1)}, u32[]{:S(2)}, u32[]{:S(2)}) async-start(bf16[8,8,7040]{2,1,0:T(8,128)(2,1)} %maximum_bitcast_fusion), calls=%async_computation | async-start | bytes 1802240 | tf_op jit(solution)/shard_map/all_to_all | solution.py:258
  98.2 0.6 dynamic_slice.14
  100.8 0.6 dynamic_slice.15
  101.5 2.1 %collective-permute-start.12 = (bf16[512,128]{1,0:T(8,128)(2,1)S(1)}, bf16[512,128]{1,0:T(8,128)(2,1)S(1)}, u32[]{:S(2)}, u32[]{:S(2)}) collective-permute-start(bf16[512,128]{1,0:T(8,128)(2,1)S(1)} %slice.34), channel_id=1, source_target_pairs={{0,2},{1,3},{2,0},{3,1},{4,6},{5,7},{6,4},{7,5},{8,10},{9,11},{10,... | collective-permute-start | bytes 393224 | tf_op jit(solution)/shard_map/ppermute | solution.py:291
  103.6 1.2 collective-permute-start.11
  104.8 0.7 pad_add_fusion.1.refs_0_
  105.5 0.2 convert_reduce_fusion.refs_1_
  105.7 3.0 %collective-permute-done.13.refs_4_ = bf16[512,128]{1,0:T(8,128)(2,1)S(1)} collective-permute-done((bf16[512,128]{1,0:T(8,128)(2,1)S(1)}, bf16[512,128]{1,0:T(8,128)(2,1)S(1)}, u32[]{:S(2)}, u32[]{:S(2)}) %collective-permute-start.13) | collective-permute-done | bytes 131104 | tf_op jit(solution)/shard_map/ppermute | solution.py:291
  108.7 1.0 collective-permute-done.12.refs_3_
  109.8 1.4 shard_map.91.refs_3_
  111.2 7.5 %all-to-all-done = bf16[8,8,7040]{2,1,0:T(8,128)(2,1)S(1)} async-done(((bf16[8,8,7040]{2,1,0:T(8,128)(2,1)}), bf16[8,8,7040]{2,1,0:T(8,128)(2,1)S(1)}, u32[]{:S(2)}, u32[]{:S(2)}) %all-to-all-start) | async-done | bytes 901152 | tf_op jit(solution)/shard_map/all_to_all | solution.py:258
  118.7 0.8 shard_map.92
  119.4 20.7 %all_to_all.44 = bf16[64,8,512]{2,1,0:T(8,128)(2,1)S(1)} all-to-all(bf16[64,8,512]{2,1,0:T(8,128)(2,1)S(1)} %bitcast.24), channel_id=1, replica_groups=mesh['y'=4,'xl'=2,'z'=8,'xh'=2,'c'=2] {'y','xl','z'}, dimensions={0} | all-to-all | bytes 1048576 | tf_op jit(solution)/shard_map/all_to_all | solution.py:258
  140.1 0.9 shard_map.93
  (35 shorter events, 0.7 us)
Async XLA Ops:
  0.7 3.2 %copy-start = (bf16[2,384,5120]{2,1,0:T(8,128)(2,1)S(1)}, bf16[2,384,5120]{2,1,0:T(8,128)(2,1)}, u32[]{:S(2)}) copy-start(bf16[2,384,5120]{2,1,0:T(8,128)(2,1)} %param.7) | copy-start | bytes 23592964
  13.1 12.6 %copy-start.2 = (f32[128,2432]{1,0:T(8,128)}, f32[128,2432]{1,0:T(8,128)S(1)}, u32[]{:S(2)}) copy-start(f32[128,2432]{1,0:T(8,128)S(1)} %get-tuple-element.22) | copy-start | bytes 3735556
  13.2 10.5 %collective-permute-start.6 = (bf16[64,2432]{1,0:T(8,128)(2,1)S(1)}, bf16[64,2432]{1,0:T(8,128)(2,1)S(1)}, u32[]{:S(2)}, u32[]{:S(2)}) collective-permute-start(bf16[64,2432]{1,0:T(8,128)(2,1)S(1)} %get-tuple-element.16.refs_4_), channel_id=1, source_target_pairs={{0,64},{64,128},{128,192},{192,0},{1,65},{65,129},{129,193},{193,1... | collective-permute-start | bytes 933896 | tf_op jit(solution)/shard_map/ppermute | solution.py:162
  14.8 10.0 %collective-permute-start.8 = (bf16[64,2432]{1,0:T(8,128)(2,1)S(1)}, bf16[64,2432]{1,0:T(8,128)(2,1)S(1)}, u32[]{:S(2)}, u32[]{:S(2)}) collective-permute-start(bf16[64,2432]{1,0:T(8,128)(2,1)S(1)} %get-tuple-element.25), channel_id=1, source_target_pairs={{0,192},{64,0},{128,64},{192,128},{1,193},{65,1},{129,65},{193,129... | collective-permute-start | bytes 933896 | tf_op jit(solution)/shard_map/ppermute | solution.py:163
  24.5 7.2 %copy-start.5 = (bf16[2,512,512]{2,1,0:T(8,128)(2,1)S(1)}, bf16[2,512,512]{2,1,0:T(8,128)(2,1)}, u32[]{:S(2)}) copy-start(bf16[2,512,512]{2,1,0:T(8,128)(2,1)} %refs_1_.1) | copy-start | bytes 3145732
  24.5 7.2 %copy-start.6 = (bf16[10,8,1024]{2,1,0:T(8,128)(2,1)S(1)}, bf16[10,8,1024]{2,1,0:T(8,128)(2,1)}, u32[]{:S(2)}) copy-start(bf16[10,8,1024]{2,1,0:T(8,128)(2,1)} %param.9) | copy-start | bytes 491524
  24.5 7.2 %copy-start.7 = (f32[2,512]{1,0:T(2,128)S(1)}, f32[2,512]{1,0:T(2,128)}, u32[]{:S(2)}) copy-start(f32[2,512]{1,0:T(2,128)} %refs_2_.1) | copy-start | bytes 12292
  24.5 27.2 %collective-permute-start.7 = (bf16[128,2432]{1,0:T(8,128)(2,1)}, bf16[128,2432]{1,0:T(8,128)(2,1)}, u32[]{:S(2)}, u32[]{:S(2)}) collective-permute-start(bf16[128,2432]{1,0:T(8,128)(2,1)} %add_convert_fusion.1), channel_id=1, source_target_pairs={{0,64},{64,128},{128,192},{192,0},{1,65},{65,129},{129,193},{193,1... | collective-permute-start | bytes 1867784 | tf_op jit(solution)/shard_map/ppermute | solution.py:167
  25.8 26.0 %collective-permute-start.9 = (bf16[128,2432]{1,0:T(8,128)(2,1)}, bf16[128,2432]{1,0:T(8,128)(2,1)}, u32[]{:S(2)}, u32[]{:S(2)}) collective-permute-start(bf16[128,2432]{1,0:T(8,128)(2,1)} %add_convert_fusion), channel_id=1, source_target_pairs={{0,192},{64,0},{128,64},{192,128},{1,193},{65,1},{129,65},{193,129... | collective-permute-start | bytes 1867784 | tf_op jit(solution)/shard_map/ppermute | solution.py:168
  28.7 27.8 %collective-permute-start.1 = (bf16[128,4608]{1,0:T(8,128)(2,1)}, bf16[128,4608]{1,0:T(8,128)(2,1)S(1)}, u32[]{:S(2)}, u32[]{:S(2)}) collective-permute-start(bf16[128,4608]{1,0:T(8,128)(2,1)} %get-tuple-element.20), channel_id=1, source_target_pairs={{0,34},{2,32},{32,2},{34,0},{1,35},{3,33},{33,3},{35,1},{4,38},{6,... | collective-permute-start | bytes 3538952 | tf_op jit(solution)/shard_map/ppermute | solution.py:277
  31.5 35.9 %collective-permute-start = (bf16[128,4608]{1,0:T(8,128)(2,1)}, bf16[128,4608]{1,0:T(8,128)(2,1)S(1)}, u32[]{:S(2)}, u32[]{:S(2)}) collective-permute-start(bf16[128,4608]{1,0:T(8,128)(2,1)} %get-tuple-element.15.refs_2_), channel_id=1, source_target_pairs={{0,32},{32,0},{1,33},{33,1},{2,34},{34,2},{3,35},{35,3},{4,36},{36... | collective-permute-start | bytes 3538952 | tf_op jit(solution)/shard_map/ppermute | solution.py:276
  33.3 10.7 %copy-start.8 = (s32[10]{0:T(128)S(1)}, s32[10]{0:T(128)}, u32[]{:S(2)}) copy-start(s32[10]{0:T(128)} %refs_0_.2) | copy-start | bytes 124
  33.3 38.2 %all-to-all-start.1 = ((bf16[64,8,640]{2,1,0:T(8,128)(2,1)}), bf16[64,8,640]{2,1,0:T(8,128)(2,1)S(1)}, u32[]{:S(2)}, u32[]{:S(2)}) async-start(bf16[64,8,640]{2,1,0:T(8,128)(2,1)} %bitcast.9), calls=%async_computation.1 | async-start | bytes 1310720 | tf_op jit(solution)/shard_map/all_to_all | solution.py:258
  44.2 3.2 %copy-start.1 = (bf16[2,384,5120]{2,1,0:T(8,128)(2,1)S(1)}, bf16[2,384,5120]{2,1,0:T(8,128)(2,1)}, u32[]{:S(2)}) copy-start(bf16[2,384,5120]{2,1,0:T(8,128)(2,1)} %param.7) | copy-start | bytes 23592964
  47.4 4.3 %copy-start.3 = (f32[128,2432]{1,0:T(8,128)S(1)}, f32[128,2432]{1,0:T(8,128)}, u32[]{:S(2)}) copy-start(f32[128,2432]{1,0:T(8,128)} %copy-done.2) | copy-start | bytes 3735556
  50.7 1.0 copy-start.4
  56.7 7.9 %collective-permute-start.4 = (bf16[32,4608]{1,0:T(8,128)(2,1)S(1)}, bf16[32,4608]{1,0:T(8,128)(2,1)S(1)}, u32[]{:S(2)}, u32[]{:S(2)}) collective-permute-start(bf16[32,4608]{1,0:T(8,128)(2,1)S(1)} %get-tuple-element.29), channel_id=1, source_target_pairs={{0,192},{64,0},{128,64},{192,128},{1,193},{65,1},{129,65},{193,129... | collective-permute-start | bytes 884744 | tf_op jit(solution)/shard_map/ppermute | solution.py:163
  57.3 14.2 %collective-permute-start.10 = (bf16[64,2432]{1,0:T(8,128)(2,1)S(1)}, bf16[64,2432]{1,0:T(8,128)(2,1)S(1)}, u32[]{:S(2)}, u32[]{:S(2)}) collective-permute-start(bf16[64,2432]{1,0:T(8,128)(2,1)S(1)} %dynamic-slice_convert_fusion), channel_id=1, source_target_pairs={{0,32},{32,0},{1,33},{33,1},{2,34},{34,2},{3,35},{35,3},{4,36},{36... | collective-permute-start | bytes 933896 | tf_op jit(solution)/shard_map/ppermute | solution.py:302
  58.0 9.4 %collective-permute-start.2 = (bf16[32,4608]{1,0:T(8,128)(2,1)S(1)}, bf16[32,4608]{1,0:T(8,128)(2,1)S(1)}, u32[]{:S(2)}, u32[]{:S(2)}) collective-permute-start(bf16[32,4608]{1,0:T(8,128)(2,1)S(1)} %get-tuple-element.28), channel_id=1, source_target_pairs={{0,64},{64,128},{128,192},{192,0},{1,65},{65,129},{129,193},{193,1... | collective-permute-start | bytes 884744 | tf_op jit(solution)/shard_map/ppermute | solution.py:162
  65.5 16.6 %collective-permute-start.5 = (bf16[64,4608]{1,0:T(8,128)(2,1)}, bf16[64,4608]{1,0:T(8,128)(2,1)}, u32[]{:S(2)}, u32[]{:S(2)}) collective-permute-start(bf16[64,4608]{1,0:T(8,128)(2,1)} %add_convert_fusion.3), channel_id=1, source_target_pairs={{0,192},{64,0},{128,64},{192,128},{1,193},{65,1},{129,65},{193,129... | collective-permute-start | bytes 1769480 | tf_op jit(solution)/shard_map/ppermute | solution.py:168
  68.4 14.0 %collective-permute-start.3 = (bf16[64,4608]{1,0:T(8,128)(2,1)}, bf16[64,4608]{1,0:T(8,128)(2,1)}, u32[]{:S(2)}, u32[]{:S(2)}) collective-permute-start(bf16[64,4608]{1,0:T(8,128)(2,1)} %add_convert_fusion.4), channel_id=1, source_target_pairs={{0,64},{64,128},{128,192},{192,0},{1,65},{65,129},{129,193},{193,1... | collective-permute-start | bytes 1769480 | tf_op jit(solution)/shard_map/ppermute | solution.py:167
  72.9 21.0 %all-to-all-start.2 = ((bf16[64,8,256]{2,1,0:T(8,128)(2,1)}), bf16[64,8,256]{2,1,0:T(8,128)(2,1)S(1)}, u32[]{:S(2)}, u32[]{:S(2)}) async-start(bf16[64,8,256]{2,1,0:T(8,128)(2,1)} %bitcast.11), calls=%async_computation.2 | async-start | bytes 524288 | tf_op jit(solution)/shard_map/all_to_all | solution.py:258
  85.3 13.0 %copy-start.10 = (s32[64]{0:T(128)S(1)}, s32[64]{0:T(128)}, u32[]{:S(2)}) copy-start(s32[64]{0:T(128)} %constant.42.clone) | copy-start | bytes 772
  85.3 20.3 %copy-start.9 = (s32[55]{0:T(128)S(1)}, s32[55]{0:T(128)}, u32[]{:S(2)}) copy-start(s32[55]{0:T(128)} %refs_0_.3) | copy-start | bytes 664
  93.9 24.8 %all-to-all-start = ((bf16[8,8,7040]{2,1,0:T(8,128)(2,1)}), bf16[8,8,7040]{2,1,0:T(8,128)(2,1)S(1)}, u32[]{:S(2)}, u32[]{:S(2)}) async-start(bf16[8,8,7040]{2,1,0:T(8,128)(2,1)} %maximum_bitcast_fusion), calls=%async_computation | async-start | bytes 1802240 | tf_op jit(solution)/shard_map/all_to_all | solution.py:258
  101.4 7.4 %collective-permute-start.13 = (bf16[512,128]{1,0:T(8,128)(2,1)S(1)}, bf16[512,128]{1,0:T(8,128)(2,1)S(1)}, u32[]{:S(2)}, u32[]{:S(2)}) collective-permute-start(bf16[512,128]{1,0:T(8,128)(2,1)S(1)} %slice.34), channel_id=1, source_target_pairs={{0,3},{1,2},{2,1},{3,0},{4,7},{5,6},{6,5},{7,4},{8,11},{9,10},{10,... | collective-permute-start | bytes 393224 | tf_op jit(solution)/shard_map/ppermute | solution.py:291
  101.5 8.3 %collective-permute-start.12 = (bf16[512,128]{1,0:T(8,128)(2,1)S(1)}, bf16[512,128]{1,0:T(8,128)(2,1)S(1)}, u32[]{:S(2)}, u32[]{:S(2)}) collective-permute-start(bf16[512,128]{1,0:T(8,128)(2,1)S(1)} %slice.34), channel_id=1, source_target_pairs={{0,2},{1,3},{2,0},{3,1},{4,6},{5,7},{6,4},{7,5},{8,10},{9,11},{10,... | collective-permute-start | bytes 393224 | tf_op jit(solution)/shard_map/ppermute | solution.py:291
  103.6 6.2 %collective-permute-start.11 = (bf16[512,128]{1,0:T(8,128)(2,1)S(1)}, bf16[512,128]{1,0:T(8,128)(2,1)S(1)}, u32[]{:S(2)}, u32[]{:S(2)}) collective-permute-start(bf16[512,128]{1,0:T(8,128)(2,1)S(1)} %slice.34), channel_id=1, source_target_pairs={{0,1},{1,0},{2,3},{3,2},{4,5},{5,4},{6,7},{7,6},{8,9},{9,8},{10,11... | collective-permute-start | bytes 393224 | tf_op jit(solution)/shard_map/ppermute | solution.py:291

commit v5 on v4

--- a/solution.py
+++ b/solution.py
@@ -299,7 +299,7 @@
     half = along.shape[0] // 2
     sent = lax.dynamic_slice_in_dim(along, (1 - low) * half, half, 0)
     kept = lax.dynamic_slice_in_dim(along, low * half, half, 0)
-    along = kept + lax.ppermute(sent.astype(bf16), "xl", [(0, 1), (1, 0)]).astype(f32)
+    come = lax.ppermute(sent.astype(bf16), "xl", [(0, 1), (1, 0)])
 
     opposite = (own[2] + far[:64].astype(f32)).astype(bf16)
     across = around_y(
@@ -309,6 +309,8 @@
         opposite[32:],
         lambda: own[3] + far[64:].astype(f32),
     )
+    across, come = lax.optimization_barrier((across, come))
+    along = kept + come.astype(f32)
     sums = exchange(jnp.concatenate([across.astype(bf16), along.astype(bf16)], axis=1), "z")
 
     [out] = call(

time: 141 us -> 151 us (1.071)
  starting transfers between devices: 41.7 us -> 46.6 us
  local copies, waits for them, and re-layouts: 8.76 us -> 12.8 us
    ppermute x2, waiting for transfers between devices: 7.15 us -> 16.4 us  [around_y(): up = lax.ppermute(up, 'y', ring('y', 1))]
    ppermute x2, waiting for transfers between devices: 5.35 us -> 1.76 us  [around_y(): down = lax.ppermute(down, 'y', ring('y', -1))]
    ppermute x1, waiting for transfers between devices: 3.29 us -> 0.01 us  [shards(): far = lax.ppermute(far, ('xl', 'xh'), [(i, 3 - i) for i in range(4)])]
    unnamed x22 -> x36, local copies, waits for them, and re-layouts: 7.51 us -> 10.7 us
    ppermute x1, waiting for transfers between devices: 2.92 us -> 0.01 us  [shards(): come = lax.ppermute(sent.astype(bf16), 'xl', [(0, 1), (1, 0)])]
    ppermute x2, starting transfers between devices: 4.82 us -> 7.57 us  [around_y(): down = lax.ppermute(down.astype(bf16), 'y', ring('y', -1))]
    convert_element_type x1 -> x0, other arithmetic: 1.88 us -> none  [shards(): across.astype(bf16)]
    all_to_all x3, starting transfers between devices: 24.3 us -> 25.8 us  [exchange(): return lax.all_to_all(x, axis, split_axis=0, concat_axis=0, tiled=True)]
  transfers between devices with their start and end apart: 17 -> 17, of which waited for: 9 -> 8; matrix products, arithmetic and copies ran while one was open for 8% -> 7% of each run, Pallas kernels for 5% -> 7%
where the time goes in v5:
time: 151 us
  starting transfers between devices  46.6 us (31%)
  waiting for transfers between devices  39.4 us (26%)
  blocking collectives  21.7 us (14%)
  Pallas kernels  18.5 us (12%)
  local copies, waits for them, and re-layouts  12.8 us (8%)
  other arithmetic  8.75 us (6%)
  between operations  2.83 us (2%)
    all_to_all x3, starting transfers between devices, exchange(): return lax.all_to_all(x, axis, split_axis=0, concat_axis=0, tiled=True)  25.8 us
    all_to_all x1, blocking collectives, exchange(): return lax.all_to_all(x, axis, split_axis=0, concat_axis=0, tiled=True)  21.7 us
    pallas_call x8, Pallas kernels, call(): pl.pallas_call(body, out_shape=tuple(outs), in_specs=[SMEM] * scalars + [...  18.5 us
    ppermute x2, waiting for transfers between devices, around_y(): up = lax.ppermute(up, 'y', ring('y', 1))  16.4 us
    all_to_all x3, waiting for transfers between devices, exchange(): return lax.all_to_all(x, axis, split_axis=0, concat_axis=0, tiled=True)  15.1 us
    unnamed x36, local copies, waits for them, and re-layouts  10.7 us
    ppermute x2, starting transfers between devices, around_y(): down = lax.ppermute(down.astype(bf16), 'y', ring('y', -1))  7.57 us
    ppermute x3, waiting for transfers between devices, shards(): lax.ppermute(quarter, ('xh', 'c'), [(i, i ^ k) for i in range(4)])  5.48 us
  transfers between devices with their start and end apart: 17, of which 8 were waited for; matrix products, arithmetic and copies ran while one was open for 7% of the time, Pallas kernels for 7%

profile of v5, /device:TPU:32, one launch (start us, length us, event | category | flops | bytes accessed | tf_op | source)
XLA Modules:
  0.0 150.5 jit_solution(16377854396651195814)
XLA Ops:
  0.7 3.2 %copy-done = bf16[2,384,5120]{2,1,0:T(8,128)(2,1)S(1)} copy-done((bf16[2,384,5120]{2,1,0:T(8,128)(2,1)S(1)}, bf16[2,384,5120]{2,1,0:T(8,128)(2,1)}, u32[]{:S(2)}) %copy-start) | copy-done | bytes 7864344
  4.0 5.8 %shard_map.86 = (bf16[128,4608]{1,0:T(8,128)(2,1)}, bf16[128,4608]{1,0:T(8,128)(2,1)}) custom-call(s32[4]{0:T(128)S(1)} %pad_add_fusion.refs_0_, bf16[768,5120]{1,0:T(8,128)(2,1)S(1)} %bitcast.18), custom_call_target="tpu_custom_call" | custom-call | flops 1811939328 | bytes 10223632 | tf_op jit(solution)/shard_map/pallas_call | solution.py:118
  9.8 2.8 %collective-permute-start.1 = (bf16[128,4608]{1,0:T(8,128)(2,1)}, bf16[128,4608]{1,0:T(8,128)(2,1)S(1)}, u32[]{:S(2)}, u32[]{:S(2)}) collective-permute-start(bf16[128,4608]{1,0:T(8,128)(2,1)} %get-tuple-element.22), channel_id=1, source_target_pairs={{0,34},{2,32},{32,2},{34,0},{1,35},{3,33},{33,3},{35,1},{4,38},{6,... | collective-permute-start | bytes 3538952 | tf_op jit(solution)/shard_map/ppermute | solution.py:277
  12.6 3.4 %shard_map.87 = (f32[128,2432]{1,0:T(8,128)S(1)}, f32[128,2432]{1,0:T(8,128)S(1)}, bf16[64,2432]{1,0:T(8,128)(2,1)S(1)}, bf16[64,2432]{1,0:T(8,128)(2,1)S(1)}, f32[128,2432]{1,0:T(8,128)S(1)}) custom-call(s32[4]{0:T(128)S(1)} %pad_add_fusion.refs_0_, bf16[768,5120]{1,0:T(8,128)(2,1)S(1)} %bitcast.19, bf16[128,4608]{1,0:T(8,128)(2,1)} %get-tuple-element.17.refs_2_), custom_call_target="tpu_custom_call" | custom-call | flops 1912602624 | bytes 12222480 | tf_op jit(solution)/shard_map/pallas_call | solution.py:118
  15.9 1.0 copy-done.2
  17.0 1.1 copy-done.4
  18.0 1.1 copy-done.6
  19.1 0.7 copy-done.14
  19.8 1.6 %collective-permute-start.6 = (bf16[64,2432]{1,0:T(8,128)(2,1)S(1)}, bf16[64,2432]{1,0:T(8,128)(2,1)}, u32[]{:S(2)}, u32[]{:S(2)}) collective-permute-start(bf16[64,2432]{1,0:T(8,128)(2,1)S(1)} %get-tuple-element.18.refs_4_), channel_id=1, source_target_pairs={{0,64},{64,128},{128,192},{192,0},{1,65},{65,129},{129,193},{193,1... | collective-permute-start | bytes 933896 | tf_op jit(solution)/shard_map/ppermute | solution.py:162
  21.4 0.2 collective-permute-start
  21.6 1.6 %shard_map.88.refs_2_ = bf16[512,640]{1,0:T(8,128)(2,1)} custom-call(s32[4]{0:T(128)S(1)} %pad_add_fusion.refs_0_, bf16[2,512,512]{2,1,0:T(8,128)(2,1)S(1)} %copy-done.9, f32[2,512]{1,0:T(2,128)S(1)} %copy-done.11, bf16[80,1024]{1,0:T(8,128)(2,1)S(1)} %bitcast.28, bf16[64,2432]{1,0:T(8,128)(2,1)S(1)} %get-tuple-element.18.refs_4_), custom_call_target="tpu_custom_call" | custom-call | bytes 1871888 | tf_op jit(solution)/shard_map/pallas_call | solution.py:118
  23.2 12.8 %all-to-all-start.1 = ((bf16[64,8,640]{2,1,0:T(8,128)(2,1)}), bf16[64,8,640]{2,1,0:T(8,128)(2,1)S(1)}, u32[]{:S(2)}, u32[]{:S(2)}) async-start(bf16[64,8,640]{2,1,0:T(8,128)(2,1)} %bitcast.9), calls=%async_computation.1 | async-start | bytes 1310720 | tf_op jit(solution)/shard_map/all_to_all | solution.py:258
  36.0 3.1 %collective-permute-start.8 = (bf16[64,2432]{1,0:T(8,128)(2,1)}, bf16[64,2432]{1,0:T(8,128)(2,1)}, u32[]{:S(2)}, u32[]{:S(2)}) collective-permute-start(bf16[64,2432]{1,0:T(8,128)(2,1)} %copy-done.14), channel_id=1, source_target_pairs={{0,192},{64,0},{128,64},{192,128},{1,193},{65,1},{129,65},{193,129... | collective-permute-start | bytes 933896 | tf_op jit(solution)/shard_map/ppermute | solution.py:163
  39.2 0.2 convert_reduce_fusion.1.refs_1_
  39.4 3.2 %copy-done.1 = bf16[2,384,5120]{2,1,0:T(8,128)(2,1)S(1)} copy-done((bf16[2,384,5120]{2,1,0:T(8,128)(2,1)S(1)}, bf16[2,384,5120]{2,1,0:T(8,128)(2,1)}, u32[]{:S(2)}) %copy-start.1) | copy-done | bytes 7864344
  42.6 3.3 %shard_map.89 = (f32[64,4608]{1,0:T(8,128)S(1)}, f32[64,4608]{1,0:T(8,128)S(1)}, f32[64,4608]{1,0:T(8,128)S(1)}, f32[64,4608]{1,0:T(8,128)S(1)}) custom-call(s32[4]{0:T(128)S(1)} %pad_add_fusion.refs_0_, bf16[768,5120]{1,0:T(8,128)(2,1)S(1)} %bitcast.20, bf16[512,640]{1,0:T(8,128)(2,1)} %shard_map.88.refs_2_), custom_call_target="tpu_custom_call" | custom-call | flops 1811939328 | bytes 12582928 | tf_op jit(solution)/shard_map/pallas_call | solution.py:118
  45.9 1.3 add_convert_fusion.1
  47.5 0.6 collective-permute-start.2
  48.1 1.5 collective-permute-done.8
  49.6 1.1 add_convert_fusion
  50.7 3.9 %collective-permute-start.9 = (bf16[128,2432]{1,0:T(8,128)(2,1)S(1)}, bf16[128,2432]{1,0:T(8,128)(2,1)S(1)}, u32[]{:S(2)}, u32[]{:S(2)}) collective-permute-start(bf16[128,2432]{1,0:T(8,128)(2,1)S(1)} %add_convert_fusion), channel_id=1, source_target_pairs={{0,192},{64,0},{128,64},{192,128},{1,193},{65,1},{129,65},{193,129... | collective-permute-start | bytes 1867784 | tf_op jit(solution)/shard_map/ppermute | solution.py:168
  54.7 0.7 collective-permute-done.refs_3_
  55.4 16.4 %collective-permute-done.2 = bf16[32,4608]{1,0:T(8,128)(2,1)S(1)} collective-permute-done((bf16[32,4608]{1,0:T(8,128)(2,1)S(1)}, bf16[32,4608]{1,0:T(8,128)(2,1)S(1)}, u32[]{:S(2)}, u32[]{:S(2)}) %collective-permute-start.2) | collective-permute-done | bytes 294944 | tf_op jit(solution)/shard_map/ppermute | solution.py:162
  71.7 1.0 add_convert_fusion.3
  72.7 0.3 collective-permute-done.4
  73.0 1.0 add_convert_fusion.2
  73.9 3.7 %collective-permute-start.5 = (bf16[64,4608]{1,0:T(8,128)(2,1)}, bf16[64,4608]{1,0:T(8,128)(2,1)}, u32[]{:S(2)}, u32[]{:S(2)}) collective-permute-start(bf16[64,4608]{1,0:T(8,128)(2,1)} %add_convert_fusion.2), channel_id=1, source_target_pairs={{0,192},{64,0},{128,64},{192,128},{1,193},{65,1},{129,65},{193,129... | collective-permute-start | bytes 1769480 | tf_op jit(solution)/shard_map/ppermute | solution.py:168
  77.8 0.8 dynamic-slice_convert_fusion
  78.7 0.3 copy-done.15
  79.0 1.2 collective-permute-start.10
  80.2 1.3 shard_map.90
  81.6 8.7 %all-to-all-start.2 = ((bf16[64,8,256]{2,1,0:T(8,128)(2,1)}), bf16[64,8,256]{2,1,0:T(8,128)(2,1)S(1)}, u32[]{:S(2)}, u32[]{:S(2)}) async-start(bf16[64,8,256]{2,1,0:T(8,128)(2,1)} %bitcast.11), calls=%async_computation.2 | async-start | bytes 524288 | tf_op jit(solution)/shard_map/all_to_all | solution.py:258
  90.3 2.0 %convert_add_fusion.1 = bf16[64,4608]{1,0:T(8,128)(2,1)S(1)} fusion(bf16[64,4608]{1,0:T(8,128)(2,1)} %collective-permute-done.5, bf16[64,4608]{1,0:T(8,128)(2,1)} %collective-permute-done.3, f32[64,4608]{1,0:T(8,128)} %copy-done.8, bf16[128,4608]{1,0:T(8,128)(2,1)S(1)} %collective-permute-done.refs_3_), kind=kLoop, calls=%fused_computation.3 | loop fusion | flops 2064384 | bytes 3538944 | tf_op jit(solution)/shard_map/add | solution.py:169
  92.4 1.0 maximum_bitcast_fusion
  93.4 8.6 %all-to-all-done.2 = bf16[64,8,256]{2,1,0:T(8,128)(2,1)S(1)} async-done(((bf16[64,8,256]{2,1,0:T(8,128)(2,1)}), bf16[64,8,256]{2,1,0:T(8,128)(2,1)S(1)}, u32[]{:S(2)}, u32[]{:S(2)}) %all-to-all-start.2) | async-done | bytes 262176 | tf_op jit(solution)/shard_map/all_to_all | solution.py:258
  102.0 4.3 %all-to-all-start = ((bf16[8,8,7040]{2,1,0:T(8,128)(2,1)}), bf16[8,8,7040]{2,1,0:T(8,128)(2,1)S(1)}, u32[]{:S(2)}, u32[]{:S(2)}) async-start(bf16[8,8,7040]{2,1,0:T(8,128)(2,1)} %maximum_bitcast_fusion), calls=%async_computation | async-start | bytes 1802240 | tf_op jit(solution)/shard_map/all_to_all | solution.py:258
  106.3 0.6 dynamic_slice.14
  108.8 0.6 dynamic_slice.15
  109.5 0.9 collective-permute-start.12
  110.4 2.5 %collective-permute-start.13 = (bf16[512,128]{1,0:T(8,128)(2,1)S(1)}, bf16[512,128]{1,0:T(8,128)(2,1)S(1)}, u32[]{:S(2)}, u32[]{:S(2)}) collective-permute-start(bf16[512,128]{1,0:T(8,128)(2,1)S(1)} %slice.34), channel_id=1, source_target_pairs={{0,3},{1,2},{2,1},{3,0},{4,7},{5,6},{6,5},{7,4},{8,11},{9,10},{10,... | collective-permute-start | bytes 393224 | tf_op jit(solution)/shard_map/ppermute | solution.py:291
  112.9 0.7 pad_add_fusion.1.refs_0_
  113.8 3.6 %collective-permute-done.12.refs_3_ = bf16[512,128]{1,0:T(8,128)(2,1)S(1)} collective-permute-done((bf16[512,128]{1,0:T(8,128)(2,1)S(1)}, bf16[512,128]{1,0:T(8,128)(2,1)S(1)}, u32[]{:S(2)}, u32[]{:S(2)}) %collective-permute-start.12) | collective-permute-done | bytes 131104 | tf_op jit(solution)/shard_map/ppermute | solution.py:291
  117.4 1.9 %collective-permute-done.13.refs_4_ = bf16[512,128]{1,0:T(8,128)(2,1)S(1)} collective-permute-done((bf16[512,128]{1,0:T(8,128)(2,1)S(1)}, bf16[512,128]{1,0:T(8,128)(2,1)S(1)}, u32[]{:S(2)}, u32[]{:S(2)}) %collective-permute-start.13) | collective-permute-done | bytes 131104 | tf_op jit(solution)/shard_map/ppermute | solution.py:291
  119.3 1.4 shard_map.91.refs_3_
  120.7 6.5 %all-to-all-done = bf16[8,8,7040]{2,1,0:T(8,128)(2,1)S(1)} async-done(((bf16[8,8,7040]{2,1,0:T(8,128)(2,1)}), bf16[8,8,7040]{2,1,0:T(8,128)(2,1)S(1)}, u32[]{:S(2)}, u32[]{:S(2)}) %all-to-all-start) | async-done | bytes 901152 | tf_op jit(solution)/shard_map/all_to_all | solution.py:258
  127.2 0.8 shard_map.92
  127.9 21.7 %all_to_all.44 = bf16[64,8,512]{2,1,0:T(8,128)(2,1)S(1)} all-to-all(bf16[64,8,512]{2,1,0:T(8,128)(2,1)S(1)} %bitcast.24), channel_id=1, replica_groups=mesh['y'=4,'xl'=2,'z'=8,'xh'=2,'c'=2] {'y','xl','z'}, dimensions={0} | all-to-all | bytes 1048576 | tf_op jit(solution)/shard_map/all_to_all | solution.py:258
  149.7 0.9 shard_map.93
  (49 shorter events, 1.0 us)
Async XLA Ops:
  0.7 3.2 %copy-start = (bf16[2,384,5120]{2,1,0:T(8,128)(2,1)S(1)}, bf16[2,384,5120]{2,1,0:T(8,128)(2,1)}, u32[]{:S(2)}) copy-start(bf16[2,384,5120]{2,1,0:T(8,128)(2,1)} %param.7) | copy-start | bytes 23592964
  9.8 37.5 %collective-permute-start.1 = (bf16[128,4608]{1,0:T(8,128)(2,1)}, bf16[128,4608]{1,0:T(8,128)(2,1)S(1)}, u32[]{:S(2)}, u32[]{:S(2)}) collective-permute-start(bf16[128,4608]{1,0:T(8,128)(2,1)} %get-tuple-element.22), channel_id=1, source_target_pairs={{0,34},{2,32},{32,2},{34,0},{1,35},{3,33},{33,3},{35,1},{4,38},{6,... | collective-permute-start | bytes 3538952 | tf_op jit(solution)/shard_map/ppermute | solution.py:277
  12.6 9.0 %copy-start.9 = (bf16[2,512,512]{2,1,0:T(8,128)(2,1)S(1)}, bf16[2,512,512]{2,1,0:T(8,128)(2,1)}, u32[]{:S(2)}) copy-start(bf16[2,512,512]{2,1,0:T(8,128)(2,1)} %refs_1_.1) | copy-start | bytes 3145732
  12.6 9.0 %copy-start.10 = (bf16[10,8,1024]{2,1,0:T(8,128)(2,1)S(1)}, bf16[10,8,1024]{2,1,0:T(8,128)(2,1)}, u32[]{:S(2)}) copy-start(bf16[10,8,1024]{2,1,0:T(8,128)(2,1)} %param.9) | copy-start | bytes 491524
  12.6 9.0 %copy-start.11 = (f32[2,512]{1,0:T(2,128)S(1)}, f32[2,512]{1,0:T(2,128)}, u32[]{:S(2)}) copy-start(f32[2,512]{1,0:T(2,128)} %refs_2_.1) | copy-start | bytes 12292
  15.9 1.1 copy-start.2
  17.0 1.1 copy-start.4
  18.0 1.1 copy-start.6
  19.1 0.7 copy-start.14
  19.8 26.1 %collective-permute-start.6 = (bf16[64,2432]{1,0:T(8,128)(2,1)S(1)}, bf16[64,2432]{1,0:T(8,128)(2,1)}, u32[]{:S(2)}, u32[]{:S(2)}) collective-permute-start(bf16[64,2432]{1,0:T(8,128)(2,1)S(1)} %get-tuple-element.18.refs_4_), channel_id=1, source_target_pairs={{0,64},{64,128},{128,192},{192,0},{1,65},{65,129},{129,193},{193,1... | collective-permute-start | bytes 933896 | tf_op jit(solution)/shard_map/ppermute | solution.py:162
  21.4 34.0 %collective-permute-start = (bf16[128,4608]{1,0:T(8,128)(2,1)}, bf16[128,4608]{1,0:T(8,128)(2,1)S(1)}, u32[]{:S(2)}, u32[]{:S(2)}) collective-permute-start(bf16[128,4608]{1,0:T(8,128)(2,1)} %get-tuple-element.17.refs_2_), channel_id=1, source_target_pairs={{0,32},{32,0},{1,33},{33,1},{2,34},{34,2},{3,35},{35,3},{4,36},{36... | collective-permute-start | bytes 3538952 | tf_op jit(solution)/shard_map/ppermute | solution.py:276
  23.2 16.0 %copy-start.12 = (s32[10]{0:T(128)S(1)}, s32[10]{0:T(128)}, u32[]{:S(2)}) copy-start(s32[10]{0:T(128)} %refs_0_.2) | copy-start | bytes 124
  23.2 57.0 %all-to-all-start.1 = ((bf16[64,8,640]{2,1,0:T(8,128)(2,1)}), bf16[64,8,640]{2,1,0:T(8,128)(2,1)S(1)}, u32[]{:S(2)}, u32[]{:S(2)}) async-start(bf16[64,8,640]{2,1,0:T(8,128)(2,1)} %bitcast.9), calls=%async_computation.1 | async-start | bytes 1310720 | tf_op jit(solution)/shard_map/all_to_all | solution.py:258
  36.0 13.6 %collective-permute-start.8 = (bf16[64,2432]{1,0:T(8,128)(2,1)}, bf16[64,2432]{1,0:T(8,128)(2,1)}, u32[]{:S(2)}, u32[]{:S(2)}) collective-permute-start(bf16[64,2432]{1,0:T(8,128)(2,1)} %copy-done.14), channel_id=1, source_target_pairs={{0,192},{64,0},{128,64},{192,128},{1,193},{65,1},{129,65},{193,129... | collective-permute-start | bytes 933896 | tf_op jit(solution)/shard_map/ppermute | solution.py:163
  39.4 3.2 %copy-start.1 = (bf16[2,384,5120]{2,1,0:T(8,128)(2,1)S(1)}, bf16[2,384,5120]{2,1,0:T(8,128)(2,1)}, u32[]{:S(2)}) copy-start(bf16[2,384,5120]{2,1,0:T(8,128)(2,1)} %param.7) | copy-start | bytes 23592964
  42.6 3.3 %copy-start.7 = (f32[128,2432]{1,0:T(8,128)S(1)}, f32[128,2432]{1,0:T(8,128)}, u32[]{:S(2)}) copy-start(f32[128,2432]{1,0:T(8,128)} %copy-done.6) | copy-start | bytes 3735556
  45.9 1.5 %copy-start.8 = (f32[64,4608]{1,0:T(8,128)}, f32[64,4608]{1,0:T(8,128)S(1)}, u32[]{:S(2)}) copy-start(f32[64,4608]{1,0:T(8,128)S(1)} %get-tuple-element.19) | copy-start | bytes 3538948
  47.2 30.4 %collective-permute-start.7 = (bf16[128,2432]{1,0:T(8,128)(2,1)S(1)}, bf16[128,2432]{1,0:T(8,128)(2,1)S(1)}, u32[]{:S(2)}, u32[]{:S(2)}) collective-permute-start(bf16[128,2432]{1,0:T(8,128)(2,1)S(1)} %add_convert_fusion.1), channel_id=1, source_target_pairs={{0,64},{64,128},{128,192},{192,0},{1,65},{65,129},{129,193},{193,1... | collective-permute-start | bytes 1867784 | tf_op jit(solution)/shard_map/ppermute | solution.py:167
  47.3 2.3 %copy-start.5 = (f32[128,2432]{1,0:T(8,128)S(1)}, f32[128,2432]{1,0:T(8,128)}, u32[]{:S(2)}) copy-start(f32[128,2432]{1,0:T(8,128)} %copy-done.4) | copy-start | bytes 3735556
  47.5 24.2 %collective-permute-start.2 = (bf16[32,4608]{1,0:T(8,128)(2,1)S(1)}, bf16[32,4608]{1,0:T(8,128)(2,1)S(1)}, u32[]{:S(2)}, u32[]{:S(2)}) collective-permute-start(bf16[32,4608]{1,0:T(8,128)(2,1)S(1)} %get-tuple-element.32), channel_id=1, source_target_pairs={{0,64},{64,128},{128,192},{192,0},{1,65},{65,129},{129,193},{193,1... | collective-permute-start | bytes 884744 | tf_op jit(solution)/shard_map/ppermute | solution.py:162
  50.7 27.0 %collective-permute-start.9 = (bf16[128,2432]{1,0:T(8,128)(2,1)S(1)}, bf16[128,2432]{1,0:T(8,128)(2,1)S(1)}, u32[]{:S(2)}, u32[]{:S(2)}) collective-permute-start(bf16[128,2432]{1,0:T(8,128)(2,1)S(1)} %add_convert_fusion), channel_id=1, source_target_pairs={{0,192},{64,0},{128,64},{192,128},{1,193},{65,1},{129,65},{193,129... | collective-permute-start | bytes 1867784 | tf_op jit(solution)/shard_map/ppermute | solution.py:168
  54.6 18.4 %collective-permute-start.4 = (bf16[32,4608]{1,0:T(8,128)(2,1)S(1)}, bf16[32,4608]{1,0:T(8,128)(2,1)S(1)}, u32[]{:S(2)}, u32[]{:S(2)}) collective-permute-start(bf16[32,4608]{1,0:T(8,128)(2,1)S(1)} %get-tuple-element.33), channel_id=1, source_target_pairs={{0,192},{64,0},{128,64},{192,128},{1,193},{65,1},{129,65},{193,129... | collective-permute-start | bytes 884744 | tf_op jit(solution)/shard_map/ppermute | solution.py:163
  72.7 17.6 %collective-permute-start.3 = (bf16[64,4608]{1,0:T(8,128)(2,1)}, bf16[64,4608]{1,0:T(8,128)(2,1)}, u32[]{:S(2)}, u32[]{:S(2)}) collective-permute-start(bf16[64,4608]{1,0:T(8,128)(2,1)} %add_convert_fusion.3), channel_id=1, source_target_pairs={{0,64},{64,128},{128,192},{192,0},{1,65},{65,129},{129,193},{193,1... | collective-permute-start | bytes 1769480 | tf_op jit(solution)/shard_map/ppermute | solution.py:167
  73.0 4.7 %copy-start.3 = (f32[128,2432]{1,0:T(8,128)S(1)}, f32[128,2432]{1,0:T(8,128)}, u32[]{:S(2)}) copy-start(f32[128,2432]{1,0:T(8,128)} %copy-done.2) | copy-start | bytes 3735556
  73.9 16.3 %collective-permute-start.5 = (bf16[64,4608]{1,0:T(8,128)(2,1)}, bf16[64,4608]{1,0:T(8,128)(2,1)}, u32[]{:S(2)}, u32[]{:S(2)}) collective-permute-start(bf16[64,4608]{1,0:T(8,128)(2,1)} %add_convert_fusion.2), channel_id=1, source_target_pairs={{0,192},{64,0},{128,64},{192,128},{1,193},{65,1},{129,65},{193,129... | collective-permute-start | bytes 1769480 | tf_op jit(solution)/shard_map/ppermute | solution.py:168
  77.8 1.2 copy-start.15
  79.0 13.3 %collective-permute-start.10 = (bf16[64,2432]{1,0:T(8,128)(2,1)}, bf16[64,2432]{1,0:T(8,128)(2,1)S(1)}, u32[]{:S(2)}, u32[]{:S(2)}) collective-permute-start(bf16[64,2432]{1,0:T(8,128)(2,1)} %dynamic-slice_convert_fusion), channel_id=1, source_target_pairs={{0,32},{32,0},{1,33},{33,1},{2,34},{34,2},{3,35},{35,3},{4,36},{36... | collective-permute-start | bytes 933896 | tf_op jit(solution)/shard_map/ppermute | solution.py:302
  81.6 20.4 %all-to-all-start.2 = ((bf16[64,8,256]{2,1,0:T(8,128)(2,1)}), bf16[64,8,256]{2,1,0:T(8,128)(2,1)S(1)}, u32[]{:S(2)}, u32[]{:S(2)}) async-start(bf16[64,8,256]{2,1,0:T(8,128)(2,1)} %bitcast.11), calls=%async_computation.2 | async-start | bytes 524288 | tf_op jit(solution)/shard_map/all_to_all | solution.py:258
  90.3 2.0 %copy-start.16 = (f32[128,2432]{1,0:T(8,128)S(1)}, f32[128,2432]{1,0:T(8,128)}, u32[]{:S(2)}) copy-start(f32[128,2432]{1,0:T(8,128)} %copy-done.15) | copy-start | bytes 3735556
  93.4 12.9 %copy-start.17 = (s32[64]{0:T(128)S(1)}, s32[64]{0:T(128)}, u32[]{:S(2)}) copy-start(s32[64]{0:T(128)} %constant.42.clone) | copy-start | bytes 772
  93.4 20.3 %copy-start.13 = (s32[55]{0:T(128)S(1)}, s32[55]{0:T(128)}, u32[]{:S(2)}) copy-start(s32[55]{0:T(128)} %refs_0_.3) | copy-start | bytes 664
  102.0 25.2 %all-to-all-start = ((bf16[8,8,7040]{2,1,0:T(8,128)(2,1)}), bf16[8,8,7040]{2,1,0:T(8,128)(2,1)S(1)}, u32[]{:S(2)}, u32[]{:S(2)}) async-start(bf16[8,8,7040]{2,1,0:T(8,128)(2,1)} %maximum_bitcast_fusion), calls=%async_computation | async-start | bytes 1802240 | tf_op jit(solution)/shard_map/all_to_all | solution.py:258
  109.4 4.4 %collective-permute-start.11 = (bf16[512,128]{1,0:T(8,128)(2,1)S(1)}, bf16[512,128]{1,0:T(8,128)(2,1)S(1)}, u32[]{:S(2)}, u32[]{:S(2)}) collective-permute-start(bf16[512,128]{1,0:T(8,128)(2,1)S(1)} %slice.34), channel_id=1, source_target_pairs={{0,1},{1,0},{2,3},{3,2},{4,5},{5,4},{6,7},{7,6},{8,9},{9,8},{10,11... | collective-permute-start | bytes 393224 | tf_op jit(solution)/shard_map/ppermute | solution.py:291
  109.5 7.9 %collective-permute-start.12 = (bf16[512,128]{1,0:T(8,128)(2,1)S(1)}, bf16[512,128]{1,0:T(8,128)(2,1)S(1)}, u32[]{:S(2)}, u32[]{:S(2)}) collective-permute-start(bf16[512,128]{1,0:T(8,128)(2,1)S(1)} %slice.34), channel_id=1, source_target_pairs={{0,2},{1,3},{2,0},{3,1},{4,6},{5,7},{6,4},{7,5},{8,10},{9,11},{10,... | collective-permute-start | bytes 393224 | tf_op jit(solution)/shard_map/ppermute | solution.py:291
  110.4 8.9 %collective-permute-start.13 = (bf16[512,128]{1,0:T(8,128)(2,1)S(1)}, bf16[512,128]{1,0:T(8,128)(2,1)S(1)}, u32[]{:S(2)}, u32[]{:S(2)}) collective-permute-start(bf16[512,128]{1,0:T(8,128)(2,1)S(1)} %slice.34), channel_id=1, source_target_pairs={{0,3},{1,2},{2,1},{3,0},{4,7},{5,6},{6,5},{7,4},{8,11},{9,10},{10,... | collective-permute-start | bytes 393224 | tf_op jit(solution)/shard_map/ppermute | solution.py:291
